TPU v7x, 32 devices: a whole 2x2x4 slice. The times are simulated.
32 devices in a mesh: img: 16 (over z, y, x), row: 2 (over core).
Axes of the slice: x: 2, y: 2, z: 4, core: 2. Of those that a mesh axis runs over, the one named last changes fastest.
Arguments:
- images: bfloat16 [48, 16, 16, 1024], P('img', 'row'), may hold values from -6 to 6
- extents: int32 [48, 2], P('img'), may hold values from 9 to 16, as said below
- entry_weight: bfloat16 [1024, 256], replicated, may hold values from -0.1875 to 0.1875
- middle_weight: bfloat16 [3, 3, 256, 256], replicated, may hold values from -0.125 to 0.125
- closing_weight: bfloat16 [256, 1024], replicated, may hold values from -0.375 to 0.375
- widen_weight: bfloat16 [1024, 512], replicated, may hold values from -0.1875 to 0.1875
- strided_weight: bfloat16 [3, 3, 512, 512], replicated, may hold values from -0.09375 to 0.09375
- expand_weight: bfloat16 [512, 2048], replicated, may hold values from -0.25 to 0.25
- shortcut_weight: bfloat16 [1024, 2048], replicated, may hold values from -0.1875 to 0.1875
- entry_affine: float32 [2, 256], replicated, may hold values from 0.5 to 1.5
- middle_affine: float32 [2, 256], replicated, may hold values from 0.5 to 1.5
- closing_affine: float32 [2, 1024], replicated, may hold values from 0.5 to 1.5
- widen_affine: float32 [2, 512], replicated, may hold values from 0.5 to 1.5
- strided_affine: float32 [2, 512], replicated, may hold values from 0.5 to 1.5
- expand_affine: float32 [2, 2048], replicated, may hold values from 0.5 to 1.5
- shortcut_affine: float32 [2, 2048], replicated, may hold values from 0.5 to 1.5
- cotangent: bfloat16 [48, 8, 8, 2048], P('img', 'row'), may hold values from -6 to 6
Outputs:
- features: bfloat16 [48, 8, 8, 2048], P('img', 'row')
- image_grads: bfloat16 [48, 16, 16, 1024], P('img', 'row')
- entry_gradient: float32 [1024, 256], P('row')
- middle_gradient: float32 [3, 3, 256, 256], P(None, None, 'row')
- closing_gradient: float32 [256, 1024], P('row')
- widen_gradient: float32 [1024, 512], P('row')
- strided_gradient: float32 [3, 3, 512, 512], P(None, None, 'row')
- expand_gradient: float32 [512, 2048], P('row')
- shortcut_gradient: float32 [1024, 2048], P('row')
- affine_entry: float32 [2, 256], replicated
- affine_middle: float32 [2, 256], replicated
- affine_closing: float32 [2, 1024], replicated
- affine_widen: float32 [2, 512], replicated
- affine_strided: float32 [2, 512], replicated
- affine_expand: float32 [2, 2048], replicated
- affine_shortcut: float32 [2, 2048], replicated
Inputs may be any that keep to these rules, and one draw needn't show every extreme that they name: Row and column extents of each image's valid region, which starts at its top-left cell; in every draw some image is valid on all 16 x 16 cells.
All inputs are finite; a program needn't handle non-finite values.
Results may differ from a plain program's by a relative error of at most 0.019.
Values may be sent and summed in bfloat16 or wider, within the bound.
No kernel may reach another device: no remote copies, remote signals or barrier semaphores. Data moves between devices by JAX's collectives and lax.ppermute only.
A program may use at most 192 MiB of HBM per device.

v0:
```python
import math

import jax
import jax.numpy as jnp
from jax import lax
from jax.sharding import PartitionSpec as P

EPS = 1e-05
DIMS = ("NHWC", "HWIO", "NHWC")


def extended(block, sides, width):
    for axis, dim in sides:
        count = lax.axis_size(axis)
        forward = [(i, i + 1) for i in range(count - 1)]
        backward = [(target, source) for source, target in forward]
        low = lax.ppermute(
            lax.slice_in_dim(block, block.shape[dim] - width, None, axis=dim), axis, forward
        )
        high = lax.ppermute(lax.slice_in_dim(block, 0, width, axis=dim), axis, backward)
        block = jnp.concatenate([low, block, high], axis=dim)
    return block


def from_behind(value, axis, steps):
    count = lax.axis_size(axis)
    initial, last = (max(0, -steps), min(count, count - steps))
    return lax.ppermute(value, axis, [(source, source + steps) for source in range(initial, last)])


def activate(value):
    gate = jax.nn.sigmoid(value)
    return (value * gate, gate * (1.0 + value * (1.0 - gate)))


def pointwise(left, weight):
    return jnp.einsum("brgc,cm->brgm", left, weight, preferred_element_type=jnp.float32)


def pointwise_back(grad, weight):
    return jnp.einsum("brgm,cm->brgc", grad, weight, preferred_element_type=jnp.float32)


def weight_grad(left, grad):
    return jnp.einsum("brgc,brgm->cm", left, grad, preferred_element_type=jnp.float32)


def conv_valid(left, kernel, stride):
    return lax.conv_general_dilated(
        left,
        kernel,
        (stride, stride),
        "VALID",
        dimension_numbers=DIMS,
        preferred_element_type=jnp.float32,
    )


def flip_kernel(kernel):
    return jnp.transpose(kernel[::-1, ::-1], (0, 1, 3, 2))


def tap_grads(padded, grad, stride):
    height, width = (grad.shape[1], grad.shape[2])
    layers = []
    for row_tap in range(3):
        line = []
        for col_tap in range(3):
            piece = lax.slice(
                padded,
                (0, row_tap, col_tap, 0),
                (
                    padded.shape[0],
                    row_tap + stride * (height - 1) + 1,
                    col_tap + stride * (width - 1) + 1,
                    padded.shape[3],
                ),
                (1, stride, stride, 1),
            )
            line.append(weight_grad(piece, grad))
        layers.append(jnp.stack(line))
    return jnp.stack(layers)


def normalize(value, mask, count, params):
    weighted = value * mask
    total = lax.psum(jnp.sum(weighted, axis=(0, 1, 2)), ("img", "row"))
    mean = total / count
    centred = (value - mean) * mask
    spread = lax.psum(jnp.sum(centred * centred, axis=(0, 1, 2)), ("img", "row")) / count
    scale = lax.rsqrt(spread + EPS)
    unit = (value - mean) * scale
    return (unit * params[0] + params[1], unit, scale)


def normalize_back(grad, unit, scale, mask, count, params):
    gain_grad, bias_grad = lax.psum(
        (jnp.sum(grad * unit, axis=(0, 1, 2)), jnp.sum(grad, axis=(0, 1, 2))), ("img", "row")
    )
    value_grad = params[0] * scale / count * (count * grad - bias_grad - unit * gain_grad) * mask
    return (value_grad.astype(jnp.bfloat16), jnp.stack([gain_grad, bias_grad]))


def reduce_grads(grads):
    groups = lax.axis_size("row")
    members = lax.axis_size("img")
    pieces = []
    shapes = []
    for gradient in grads:
        if gradient.ndim == 4:
            gradient = jnp.transpose(gradient, (2, 0, 1, 3))
        shapes.append(gradient.shape)
        pieces.append(gradient.reshape(groups, -1))
    packed = jnp.concatenate(pieces, axis=1)
    shares = lax.psum_scatter(
        packed.astype(jnp.bfloat16), "row", scatter_dimension=0, tiled=True
    ).astype(jnp.float32)
    length = shares.shape[1]
    padded_length = -(-length // members) * members
    shares = jnp.pad(shares, ((0, 0), (0, padded_length - length)))
    slice_sum = lax.psum_scatter(shares, "img", scatter_dimension=1, tiled=True)
    totals = lax.all_gather(slice_sum.astype(jnp.bfloat16), "img", axis=1, tiled=True).astype(
        slice_sum.dtype
    )
    results = []
    start = 0
    for shape in shapes:
        local_shape = (shape[0] // groups,) + tuple(shape[1:])
        amount = math.prod(local_shape)
        result = totals[0, start : start + amount].reshape(local_shape)
        start = start + amount
        if len(shape) == 4:
            result = jnp.transpose(result, (1, 2, 0, 3))
        results.append(result)
    return tuple(results)


def per_device(
    images,
    extents,
    entry_weight,
    middle_weight,
    closing_weight,
    widen_weight,
    strided_weight,
    expand_weight,
    shortcut_weight,
    entry_affine,
    middle_affine,
    closing_affine,
    widen_affine,
    strided_affine,
    expand_affine,
    shortcut_affine,
    cotangent,
):
    height = images.shape[1]
    width = images.shape[2]
    offset = lax.axis_index("row") * height
    line = offset + jnp.arange(height)
    column = jnp.arange(width)
    valid_rows = extents[:, 0]
    valid_cols = extents[:, 1]
    inside = (line[None, :, None] < valid_rows[:, None, None]) & (
        column[None, None, :] < valid_cols[:, None, None]
    )
    mask = inside.astype(jnp.float32)[..., None]
    small_mask = mask[:, ::2, ::2]
    count, small_count = lax.psum(
        (
            jnp.sum(valid_rows * valid_cols).astype(jnp.float32),
            jnp.sum((valid_rows + 1) // 2 * ((valid_cols + 1) // 2)).astype(jnp.float32),
        ),
        "img",
    )
    column_pad = ((0, 0), (0, 0), (1, 1), (0, 0))
    entry_in = images * mask.astype(jnp.bfloat16)
    entry_raw = pointwise(entry_in, entry_weight)
    entry_norm, entry_unit, entry_scale = normalize(entry_raw, mask, count, entry_affine)
    entry_value, entry_slope = activate(entry_norm)
    entry_act = (entry_value * mask).astype(jnp.bfloat16)
    entry_rim = extended(entry_act, (("row", 1),), 1)
    entry_padded = jnp.pad(entry_rim, column_pad)
    middle_raw = conv_valid(entry_padded, middle_weight, 1)
    middle_norm, middle_unit, middle_scale = normalize(middle_raw, mask, count, middle_affine)
    middle_value, middle_slope = activate(middle_norm)
    middle_act = (middle_value * mask).astype(jnp.bfloat16)
    closing_raw = pointwise(middle_act, closing_weight)
    closing_norm, closing_unit, closing_scale = normalize(closing_raw, mask, count, closing_affine)
    block_value, block_slope = activate(closing_norm + entry_in.astype(jnp.float32))
    block_out = (block_value * mask).astype(jnp.bfloat16)
    widen_raw = pointwise(block_out, widen_weight)
    widen_norm, widen_unit, widen_scale = normalize(widen_raw, mask, count, widen_affine)
    widen_value, widen_slope = activate(widen_norm)
    widen_act = (widen_value * mask).astype(jnp.bfloat16)
    above = from_behind(widen_act[:, height - 1 :], "row", 1)
    strided_padded = jnp.pad(
        jnp.concatenate([above, widen_act], axis=1), ((0, 0), (0, 0), (1, 0), (0, 0))
    )
    strided_raw = conv_valid(strided_padded, strided_weight, 2)
    strided_norm, strided_unit, strided_scale = normalize(
        strided_raw, small_mask, small_count, strided_affine
    )
    strided_value, strided_slope = activate(strided_norm)
    strided_act = (strided_value * small_mask).astype(jnp.bfloat16)
    expand_raw = pointwise(strided_act, expand_weight)
    shortcut_in = block_out[:, ::2, ::2]
    shortcut_raw = pointwise(shortcut_in, shortcut_weight)
    expand_norm, expand_unit, expand_scale = normalize(
        expand_raw, small_mask, small_count, expand_affine
    )
    shortcut_norm, shortcut_unit, shortcut_scale = normalize(
        shortcut_raw, small_mask, small_count, shortcut_affine
    )
    final_value, final_slope = activate(expand_norm + shortcut_norm)
    features = (final_value * small_mask).astype(jnp.bfloat16)
    final_grad = cotangent.astype(jnp.float32) * small_mask * final_slope
    expand_grad, affine_expand = normalize_back(
        final_grad, expand_unit, expand_scale, small_mask, small_count, expand_affine
    )
    shortcut_grad, affine_shortcut = normalize_back(
        final_grad, shortcut_unit, shortcut_scale, small_mask, small_count, shortcut_affine
    )
    expand_gradient = weight_grad(strided_act, expand_grad)
    shortcut_gradient = weight_grad(shortcut_in, shortcut_grad)
    strided_back = pointwise_back(expand_grad, expand_weight) * small_mask * strided_slope
    strided_grad, affine_strided = normalize_back(
        strided_back, strided_unit, strided_scale, small_mask, small_count, strided_affine
    )
    strided_gradient = tap_grads(strided_padded, strided_grad, 2)
    spread_grad = lax.conv_general_dilated(
        strided_grad,
        flip_kernel(strided_weight),
        (1, 1),
        ((2, 2), (2, 2)),
        lhs_dilation=(2, 2),
        dimension_numbers=DIMS,
        preferred_element_type=jnp.float32,
    )
    spill = from_behind(spread_grad[:, :1, 1:].astype(jnp.bfloat16), "row", -1).astype(jnp.float32)
    widen_back = spread_grad[:, 1:, 1:] + jnp.pad(spill, ((0, 0), (height - 1, 0), (0, 0), (0, 0)))
    widen_back = widen_back * mask * widen_slope
    widen_grad, affine_widen = normalize_back(
        widen_back, widen_unit, widen_scale, mask, count, widen_affine
    )
    widen_gradient = weight_grad(block_out, widen_grad)
    late = reduce_grads((widen_gradient, strided_gradient, expand_gradient, shortcut_gradient))
    short_spread = lax.pad(
        pointwise_back(shortcut_grad, shortcut_weight),
        jnp.float32(0),
        ((0, 0, 0), (0, 1, 1), (0, 1, 1), (0, 0, 0)),
    )
    block_back = (pointwise_back(widen_grad, widen_weight) + short_spread) * mask * block_slope
    closing_grad, affine_closing = normalize_back(
        block_back, closing_unit, closing_scale, mask, count, closing_affine
    )
    closing_gradient = weight_grad(middle_act, closing_grad)
    middle_back = pointwise_back(closing_grad, closing_weight) * mask * middle_slope
    middle_grad, affine_middle = normalize_back(
        middle_back, middle_unit, middle_scale, mask, count, middle_affine
    )
    middle_gradient = tap_grads(entry_padded, middle_grad, 1)
    grad_rim = extended(middle_grad, (("row", 1),), 1)
    entry_back = (
        conv_valid(jnp.pad(grad_rim, column_pad), flip_kernel(middle_weight), 1)
        * mask
        * entry_slope
    )
    entry_grad, affine_entry = normalize_back(
        entry_back, entry_unit, entry_scale, mask, count, entry_affine
    )
    entry_gradient = weight_grad(entry_in, entry_grad)
    image_grads = ((block_back + pointwise_back(entry_grad, entry_weight)) * mask).astype(
        jnp.bfloat16
    )
    early = reduce_grads((entry_gradient, middle_gradient, closing_gradient))
    widen_total, strided_total, expand_total, shortcut_total = late
    entry_total, middle_total, closing_total = early
    return (
        features,
        image_grads,
        entry_total,
        middle_total,
        closing_total,
        widen_total,
        strided_total,
        expand_total,
        shortcut_total,
        affine_entry,
        affine_middle,
        affine_closing,
        affine_widen,
        affine_strided,
        affine_expand,
        affine_shortcut,
    )


def solution(mesh):
    return jax.shard_map(
        per_device,
        mesh=mesh,
        in_specs=(
            P("img", "row", None, None),
            P("img", None),
            P(),
            P(),
            P(),
            P(),
            P(),
            P(),
            P(),
            P(),
            P(),
            P(),
            P(),
            P(),
            P(),
            P(),
            P("img", "row", None, None),
        ),
        out_specs=(
            P("img", "row", None, None),
            P("img", "row", None, None),
            P("row", None),
            P(None, None, "row", None),
            P("row", None),
            P("row", None),
            P(None, None, "row", None),
            P("row", None),
            P("row", None),
            P(),
            P(),
            P(),
            P(),
            P(),
            P(),
            P(),
        ),
        check_vma=False,
    )
```

profile of v0, /device:TPU:0, one launch (start us, length us, event | category | flops | bytes accessed | tf_op | source)
XLA Modules:
  0.0 6425.4 jit_solution(10610799523533423410)
XLA Ops:
  14.0 42.0 psum.206
  56.0 41.0 all-reduce.16
  149.0 41.0 psum.209
  236.9 40.3 psum.211
  280.8 40.4 psum.212
  328.0 40.8 psum.213
  371.9 40.1 psum.214
  438.0 40.9 psum.215
  482.9 40.5 psum.217
  532.2 40.9 psum.218
  579.4 40.1 psum.220
  625.3 41.1 all-reduce.14
  672.5 40.4 all-reduce.13
  719.5 41.4 all-reduce.12
  802.7 40.3 all-reduce.11
  860.7 41.8 all-reduce.10
  976.4 187.9 %pad_maximum_fusion = bf16[2,3014656]{1,0:T(2,128)(2,1)} fusion(bf16[2,1048576]{1,0:T(2,128)(2,1)S(1)} %copy-done.3, bf16[2,524288]{1,0:T(2,128)(2,1)S(1)} %copy-done.7, bf16[2,1179648]{1,0:T(2,128)(2,1)} %reshape.182, bf16[2,262144]{1,0:T(2,128)(2,1)S(1)} %reshape.181), kind=kLoop, calls=%fused_computation | loop fusion | flops 48234496 | bytes 24117248 | tf_op jit(solution)/shard_map/concatenate | solution.py:114
  1172.4 41.5 all-reduce.8
  1253.8 49.2 all-reduce.21.cloned.1.call-done
  1323.0 4713.9 %all-reduce.22 = (bf16[1,557056]{1,0:T(2,128)(2,1)}, bf16[1,3014656]{1,0:T(2,128)(2,1)}) all-reduce(f32[1,557056]{1,0:T(1,128)} %dynamic-slice_convert_fusion.1, f32[1,3014656]{1,0:T(1,128)} %dynamic-slice_convert_fusion), channel_id=3, replica_groups=mesh['img'=16,'row'=2] {'img'}, use_global_device_ids=true, to_apply=%region_59.60.clone | all-reduce | flops 3571712 | bytes 21430272
  6046.8 57.8 all-gather.3.cloned.1.call-done
  6130.1 123.6 %all-gather.5.cloned.1.call-done = bf16[1,3014656]{1,0:T(2,128)(2,1)} async-done(((bf16[1,188416]{1,0:T(2,128)(2,1)}), bf16[1,3014656]{1,0:T(2,128)(2,1)}) %all-gather.5.cloned.1.call-update) | async-done | bytes 6029328 | tf_op jit(solution)/shard_map/all_gather | solution.py:122
  6278.6 50.9 slice_reduce_fusion
  6351.3 45.3 slice_reduce_fusion.1
  (461 shorter events, 484.0 us)
Async XLA Ops:
  7.2 523.0 %copy-start = (bf16[512,2048]{1,0:T(8,128)(2,1)S(1)}, bf16[512,2048]{1,0:T(8,128)(2,1)}, u32[]{:S(2)}) copy-start(bf16[512,2048]{1,0:T(8,128)(2,1)} %param.24) | copy-start | bytes 6291460
  7.2 1295.8 %all-reduce.21.cloned.1.call-start = ((), (), s32[]{:S(2)}) async-start(), calls=%async_computation.2 | async-start | bytes 28573696
  11.4 124.5 %copy-start.85 = (bf16[3,8,16]{2,1,0:T(8,128)(2,1)}, bf16[3,8,16]{2,1,0:T(8,128)(2,1)S(1)}, u32[]{:S(2)}) copy-start(bf16[3,8,16]{2,1,0:T(8,128)(2,1)S(1)} %copy.117) | copy-start | bytes 2308
  12.2 123.7 %copy-start.91 = (f32[1,256]{1,0:T(1,128)}, f32[1,256]{1,0:T(1,128)S(1)}, u32[]{:S(2)}) copy-start(f32[1,256]{1,0:T(1,128)S(1)} %get-tuple-element.157) | copy-start | bytes 3076
  12.2 123.7 %copy-start.99 = (f32[1,256]{1,0:T(1,128)}, f32[1,256]{1,0:T(1,128)S(1)}, u32[]{:S(2)}) copy-start(f32[1,256]{1,0:T(1,128)S(1)} %get-tuple-element.158) | copy-start | bytes 3076
  12.2 128.9 %copy-start.110 = (f32[2,512]{1,0:T(2,128)S(1)}, f32[2,512]{1,0:T(2,128)}, u32[]{:S(2)}) copy-start(f32[2,512]{1,0:T(2,128)} %param.30) | copy-start | bytes 12292
  12.2 129.5 %copy-start.111 = (f32[2,512]{1,0:T(2,128)S(1)}, f32[2,512]{1,0:T(2,128)}, u32[]{:S(2)}) copy-start(f32[2,512]{1,0:T(2,128)} %param.29) | copy-start | bytes 12292
  12.2 130.1 %copy-start.108 = (f32[2,1024]{1,0:T(2,128)S(1)}, f32[2,1024]{1,0:T(2,128)}, u32[]{:S(2)}) copy-start(f32[2,1024]{1,0:T(2,128)} %param.28) | copy-start | bytes 24580
  12.2 130.7 %copy-start.93 = (f32[2,2048]{1,0:T(2,128)S(1)}, f32[2,2048]{1,0:T(2,128)}, u32[]{:S(2)}) copy-start(f32[2,2048]{1,0:T(2,128)} %param.32) | copy-start | bytes 49156
  12.2 131.3 %copy-start.94 = (f32[2,2048]{1,0:T(2,128)S(1)}, f32[2,2048]{1,0:T(2,128)}, u32[]{:S(2)}) copy-start(f32[2,2048]{1,0:T(2,128)} %param.31) | copy-start | bytes 49156
  12.2 131.9 %copy-start.115 = (f32[2,256]{1,0:T(2,128)S(1)}, f32[2,256]{1,0:T(2,128)}, u32[]{:S(2)}) copy-start(f32[2,256]{1,0:T(2,128)} %param.27) | copy-start | bytes 6148
  14.0 132.5 %copy-start.10 = (f32[3,8,16,256]{3,2,1,0:T(8,128)}, f32[3,8,16,256]{3,2,1,0:T(8,128)S(1)}, u32[]{:S(2)}) copy-start(f32[3,8,16,256]{3,2,1,0:T(8,128)S(1)} %get-tuple-element.164) | copy-start | bytes 1179652
  97.7 47.7 copy-start.79
  136.7 8.7 collective-permute-start.1
  138.0 7.4 collective-permute-start
  235.3 87.7 %copy-start.32 = (bf16[3,8,16,1024]{3,2,1,0:T(8,128)(2,1)S(1)}, bf16[3,8,16,1024]{3,2,1,0:T(8,128)(2,1)}, u32[]{:S(2)}) copy-start(bf16[3,8,16,1024]{3,2,1,0:T(8,128)(2,1)} %param.17) | copy-start | bytes 2359300
  417.0 12.0 collective-permute-start.2
  768.4 30.7 collective-permute-start.3
  856.2 46.3 copy-start.70
  856.2 46.3 copy-start.97
  957.9 209.9 %collective-permute-start.5 = (bf16[3,1,16,256]{3,2,1,0:T(8,128)(2,1)}, bf16[3,1,16,256]{3,2,1,0:T(8,128)(2,1)}, u32[]{:S(2)}, u32[]{:S(2)}) collective-permute-start(bf16[3,1,16,256]{3,2,1,0:T(8,128)(2,1)} %get-tuple-element.130), channel_id=1, source_target_pairs={{1,0},{3,2},{5,4},{7,6},{9,8},{11,10},{13,12},{15,14},{17,16},{19,... | collective-permute-start | bytes 73736 | tf_op jit(solution)/shard_map/ppermute | solution.py:20
  959.2 208.6 %collective-permute-start.4 = (bf16[3,1,16,256]{3,2,1,0:T(8,128)(2,1)S(1)}, bf16[3,1,16,256]{3,2,1,0:T(8,128)(2,1)}, u32[]{:S(2)}, u32[]{:S(2)}) collective-permute-start(bf16[3,1,16,256]{3,2,1,0:T(8,128)(2,1)S(1)} %get-tuple-element.129), channel_id=1, source_target_pairs={{0,1},{2,3},{4,5},{6,7},{8,9},{10,11},{12,13},{14,15},{16,17},{18,... | collective-permute-start | bytes 73736 | tf_op jit(solution)/shard_map/ppermute | solution.py:17
  1250.7 4854.0 %all-gather.3.cloned.1.call-start = ((), (), s32[]{:S(2)}) async-start(), calls=%async_computation | async-start | bytes 2367488 | tf_op jit(solution)/shard_map/all_gather | solution.py:122
  6038.8 214.9 %all-gather.5.cloned.1.call-start = ((), (), s32[]{:S(2)}) async-start(), calls=%async_computation.1 | async-start | bytes 12812288 | tf_op jit(solution)/shard_map/all_gather | solution.py:122
  (108 other events, 775.7 us)
Sparse Core Ops, SparseCore 0:
  1250.8 52.1 all-reduce.20
  6038.9 65.6 all-gather.2
  6108.3 145.3 all-gather.4
where the time goes:
time: 6440 us; the launch traced here: 6430 us
  blocking collectives  5520 us (86%)
  other arithmetic  333 us (5%)
  local copies, waits for them, and re-layouts  254 us (4%)
  waiting for transfers between devices  231 us (4%)
    unnamed x1, blocking collectives  4710 us
    psum x7, blocking collectives, normalize(): total = lax.psum(jnp.sum(weighted, axis=(0, 1, 2)), ('img', 'row'))  286 us
    psum x6, blocking collectives, normalize_back(): lax.psum((jnp.sum(grad * unit, axis=(0, 1, 2)), jnp.sum(grad, axis=(0, 1,...  244 us
    psum x6, blocking collectives, normalize(): lax.psum(jnp.sum(centred * centred, axis=(0, 1, 2)), ('img', 'row')) / count  239 us
    concatenate x2, other arithmetic, reduce_grads(): packed = jnp.concatenate(pieces, axis=1)  222 us
    all_gather x2, waiting for transfers between devices, reduce_grads(): lax.all_gather(slice_sum.astype(jnp.bfloat16), 'img', axis=1, tiled=True)  181 us
    slice x6, local copies, waits for them, and re-layouts, reduce_grads(): result = totals[0, start:start + amount].reshape(local_shape)  145 us
  transfers between devices with their start and end apart: 9, of which 3 were waited for; matrix products, arithmetic and copies ran while one was open for 4% of the time, Pallas kernels for 0%

commit v1 on v0

v1 whole, which is shorter than its diff:
```python
import functools
import math

import jax
import jax.numpy as jnp
from jax import lax
from jax.experimental import pallas as pl
from jax.experimental.pallas import tpu as pltpu
from jax.sharding import PartitionSpec as P

EPS = 1e-05
BOTH = ("img", "row")
F32 = jnp.float32
BF16 = jnp.bfloat16
LANES = 128
MIB = 1 << 20


def swap_rows(value):
    count = lax.axis_size("row")
    return lax.ppermute(value, "row", [(i, (i + 1) % count) for i in range(count)])


def gather_all(message):
    return lax.all_to_all(message, BOTH, 0, 0, tiled=True)


def gather_img(message):
    return lax.all_to_all(message, "img", 0, 0, tiled=True)


def orders():
    bits = lax.axis_size("img").bit_length() - 1
    ascending = list(range(bits))
    swapped = ascending[:]
    if bits > 1:
        swapped[0], swapped[1] = 1, 0
    return ascending, swapped


def permute_bit(value, bit):
    count = lax.axis_size("img")
    return lax.ppermute(value, "img", [(i, i ^ (1 << bit)) for i in range(count)])


class Late:
    def __init__(self, source, buffer, semaphores):
        self.buffer = buffer
        self.shape, self.ndim, self.dtype = buffer.shape, len(buffer.shape), buffer.dtype
        parts = parts_of(self.shape)
        if parts == 1:
            self.copies = [pltpu.make_async_copy(source, buffer, semaphores.at[0])]
        else:
            self.copies = [
                pltpu.make_async_copy(source.at[i], buffer.at[i], semaphores.at[i]) for i in range(parts)
            ]
        for copy in self.copies:
            copy.start()
        self.waiting = set(range(parts))

    def ready(self, part=None):
        for i in sorted(self.waiting):
            if part is None or i == part:
                self.copies[i].wait()
                self.waiting.remove(i)
        return self.buffer

    def __getitem__(self, index):
        first = index[0] if isinstance(index, tuple) else index
        part = first if isinstance(first, int) and len(self.copies) > 1 else None
        return self.ready(part)[index]


def parts_of(shape):
    return shape[0] if len(shape) >= 3 and shape[0] == 3 else 1


class Saved:
    def __init__(self, target, buffer, semaphore):
        self.target, self.buffer, self.semaphore, self.copy = target, buffer, semaphore, None
        self.shape, self.ndim, self.dtype = buffer.shape, len(buffer.shape), buffer.dtype

    def send(self):
        if self.copy is None:
            self.copy = pltpu.make_async_copy(self.buffer, self.target, self.semaphore)
            self.copy.start()

    def __getitem__(self, index):
        return self.buffer[index]

    def __setitem__(self, index, value):
        self.buffer[index] = value


def send(*results):
    for result in results:
        if isinstance(result, Saved):
            result.send()


def call(kernel, outs, *operands, scratch=(), smem=(), late=(), flops=0, keep=(), limit=24):
    late = [place for place in (range(len(operands)) if late is None else late) if place not in smem]
    saved = [place for place in range(len(outs)) if place not in keep]
    moved = sum(x.size * x.dtype.itemsize for x in operands) + sum(
        math.prod(shape) * jnp.dtype(dtype).itemsize for shape, dtype in outs
    )

    def place_of_operand(place):
        if place in smem:
            return pltpu.SMEM
        return pl.ANY if place in late else pltpu.VMEM

    operands = [
        pltpu.with_memory_space_constraint(x, pltpu.HBM) if place in late else x for place, x in enumerate(operands)
    ]
    buffers = [pltpu.VMEM(operands[place].shape, operands[place].dtype) for place in late]
    buffers += [pltpu.VMEM(*outs[place]) for place in saved]
    semaphores = [pltpu.SemaphoreType.DMA((parts_of(operands[place].shape),)) for place in late]
    semaphores += [pltpu.SemaphoreType.DMA] * len(saved)

    def body(*refs):
        refs = list(refs)
        inputs, refs = refs[: len(operands)], refs[len(operands) :]
        results, refs = refs[: len(outs)], refs[len(outs) :]
        own, refs = refs[: len(scratch)], refs[len(scratch) :]
        space, marks = refs[: len(buffers)], refs[len(buffers) :]
        for number, place in enumerate(late):
            inputs[place] = Late(inputs[place], space[number], marks[number])
        for number, place in enumerate(saved):
            number += len(late)
            results[place] = Saved(results[place], space[number], marks[number])
        kernel(*inputs, *results, *own)
        for place in late:
            inputs[place].ready()
        for place in saved:
            results[place].send()
        for place in saved:
            results[place].copy.wait()

    return pl.pallas_call(
        body,
        out_shape=[
            (pltpu.VMEM if place in keep else pltpu.HBM)(shape, dtype) for place, (shape, dtype) in enumerate(outs)
        ],
        in_specs=[pl.BlockSpec(memory_space=place_of_operand(place)) for place in range(len(operands))],
        out_specs=[
            pl.BlockSpec(memory_space=pltpu.VMEM if place in keep else pl.ANY) for place in range(len(outs))
        ],
        scratch_shapes=[pltpu.VMEM(shape, dtype) for shape, dtype in scratch] + buffers + semaphores,
        compiler_params=pltpu.CompilerParams(vmem_limit_bytes=limit * MIB),
        cost_estimate=pl.CostEstimate(flops=flops, bytes_accessed=moved, transcendentals=0),
    )(*operands)


def dot(left, right):
    return jnp.dot(left, right, preferred_element_type=F32)


def dot_back(grad, weight):
    return lax.dot_general(grad, weight, (((1,), (1,)), ((), ())), preferred_element_type=F32)


def wide(mask, width):
    return mask if width == LANES else jnp.concatenate([mask] * (width // LANES), axis=1)


def column_sum(value):
    return jnp.sum(value, axis=0, keepdims=True)


def spread_message(message, rows):
    tile = rows[...]
    for device in range(message.shape[0]):
        message[device] = tile


def put_row(rows, place, vector):
    for block in range(vector.shape[1] // LANES):
        rows[place + block : place + block + 1, :] = vector[:, block * LANES : (block + 1) * LANES]


def local_stats(raw, mask, rows, place=0):
    blocks = raw.shape[1] // LANES
    number = jnp.maximum(column_sum(mask[...]), 1.0)
    for block in range(blocks):
        columns = slice(block * LANES, (block + 1) * LANES)
        total = column_sum(raw[:, columns] * mask[...])
        centred = (raw[:, columns] - total / number) * mask[...]
        rows[place + block : place + block + 1, :] = total
        rows[place + blocks + block : place + blocks + block + 1, :] = column_sum(centred * centred)


def total_count(counts, place):
    return functools.reduce(
        jnp.add, [counts[i, place : place + 1, :] for i in range(counts.shape[0])]
    )


def join_stats(gathered, counts, place, stats, blocks):
    devices = gathered.shape[0]
    count = total_count(counts, place)
    mean = functools.reduce(jnp.add, [gathered[i, :blocks, :] for i in range(devices)]) / count
    spread = functools.reduce(jnp.add, [gathered[i, blocks : 2 * blocks, :] for i in range(devices)])
    for i in range(devices):
        number = counts[i, place : place + 1, :]
        shift = gathered[i, :blocks, :] / jnp.maximum(number, 1.0) - mean
        spread = spread + number * (shift * shift)
    scale = lax.rsqrt(spread / count + EPS)
    for block in range(blocks):
        columns = slice(block * LANES, (block + 1) * LANES)
        stats[0:1, columns] = mean[block : block + 1, :]
        stats[1:2, columns] = scale[block : block + 1, :]


def join_sums(gathered, affine):
    total = functools.reduce(jnp.add, [gathered[i] for i in range(gathered.shape[0])])
    blocks = affine.shape[1] // LANES
    for block in range(blocks):
        columns = slice(block * LANES, (block + 1) * LANES)
        affine[0:1, columns] = total[block : block + 1, :]
        affine[1:2, columns] = total[blocks + block : blocks + block + 1, :]


def chunks(rows, width, chunk=32, block=256):
    for start in range(0, width, block):
        for row in range(0, rows, chunk):
            yield slice(row, row + min(chunk, rows - row)), slice(start, start + min(block, width - start))


def silu_parts(value):
    gate = jax.nn.sigmoid(value)
    return value * gate, gate * (1.0 + value * (1.0 - gate))


def normed(raw, stats, params, columns):
    unit = (raw - stats[0:1, columns]) * stats[1:2, columns]
    return unit, unit * params[0:1, columns] + params[1:2, columns]


def act_pass(raw, mask, stats, params, unit, slope, act, skip=None, keep=None):
    rows, width = raw.shape
    for here, columns in chunks(rows, width):
        u, value = normed(raw[here, columns], stats, params, columns)
        if skip is not None:
            value = value + skip[here, columns].astype(F32)
        m = wide(mask[here, :], columns.stop - columns.start)
        out, rise = silu_parts(value)
        out = out * m
        unit[here, columns] = u
        slope[here, columns] = rise * m
        if act is not None:
            act[here, columns] = out.astype(BF16)
        if keep is not None:
            keep(here, columns, out)


def back_pass(back, unit, slope, rows):
    blocks = back.shape[1] // LANES
    for block in range(blocks):
        columns = slice(block * LANES, (block + 1) * LANES)
        value = back[:, columns] * slope[:, columns]
        back[:, columns] = value
        rows[block : block + 1, :] = column_sum(value * unit[:, columns])
        rows[blocks + block : blocks + block + 1, :] = column_sum(value)


def raw_grad(back, unit, mask, sums, stats, params, count, columns):
    width = columns.stop - columns.start
    n = wide(count, width)
    factor = params[0:1, columns] * stats[1:2, columns]
    centred = back - sums[1:2, columns] / n - unit * (sums[0:1, columns] / n)
    return factor * centred * wide(mask, width)


def grad_pass(back, unit, mask, sums, stats, params, count, grad, keep=None):
    for here, columns in chunks(*back.shape):
        value = raw_grad(
            back[here, columns], unit[here, columns], mask[here, :], sums, stats, params, count, columns
        )
        grad[here, columns] = value.astype(BF16)
        if keep is not None:
            keep(here, columns, value)


def valid(extents, image, first_row, columns, shape, step):
    place = lax.broadcasted_iota(jnp.int32, shape, 0)
    row = first_row + step * (place // columns)
    column = step * (place % columns)
    return jnp.where((row < extents[image, 0]) & (column < extents[image, 1]), 1.0, 0.0).astype(F32)


def own_half(core, size):
    return pl.ds(pl.multiple_of(core[0] * size, LANES), size)


def other_half(core, size):
    return pl.ds(pl.multiple_of((1 - core[0]) * size, LANES), size)


def give_half(core, value, give):
    give[...] = value[:, other_half(core, give.shape[1])]
    send(give)


def entry_kernel(
    dims, extents, flag, core, images, weight,
    entry_in, mask, small, above, below, small_below, raw, edge, message, give, rows,
):
    batch, height, width = dims
    pixels = height * width
    upper = flag[0]
    for b in range(batch):
        mask[b * pixels : (b + 1) * pixels, :] = valid(extents, b, 0, width, (pixels, LANES), 1)
        small[b * pixels // 4 : (b + 1) * pixels // 4, :] = valid(
            extents, b, 0, width // 2, (pixels // 4, LANES), 2
        )
        line = slice(b * width, (b + 1) * width)
        above[line, :] = valid(extents, b, -1, width, (width, LANES), 1) * (1.0 - upper)
        below[line, :] = valid(extents, b, height, width, (width, LANES), 1) * upper
        small_below[b * width // 2 : (b + 1) * width // 2, :] = (
            valid(extents, b, height, width // 2, (width // 2, LANES), 2) * upper
        )
    for here, columns in chunks(*images.shape):
        m = wide(mask[here, :], columns.stop - columns.start)
        entry_in[here, columns] = (images[here, columns].astype(F32) * m).astype(BF16)
    send(entry_in, mask, small, above, below, small_below)
    give_half(core, entry_in, give)
    raw[...] = dot(entry_in[...], weight[...])
    for b in range(batch):
        first = raw[b * pixels : b * pixels + width, :]
        last = raw[(b + 1) * pixels - width : (b + 1) * pixels, :]
        edge[b * width : (b + 1) * width, :] = last * upper + first * (1.0 - upper)
    rows[...] = jnp.zeros_like(rows)
    local_stats(raw, mask, rows)
    blocks = raw.shape[1] // LANES
    rows[2 * blocks : 2 * blocks + 1, :] = column_sum(mask[...])
    rows[2 * blocks + 1 : 2 * blocks + 2, :] = column_sum(small[...])
    spread_message(message, rows)


def put_blocks(target, here, columns, value):
    for start in range(columns.start, columns.stop, LANES):
        offset = start - columns.start
        target[start // LANES, here, :] = value[:, offset : offset + LANES]


def column_masks(rows, width):
    place = lax.broadcasted_iota(jnp.int32, (rows, LANES), 0) % width
    return (
        jnp.where(place == 0, 0.0, 1.0).astype(F32),
        jnp.where(place == width - 1, 0.0, 1.0).astype(F32),
    )


def fill_triple(padded, triple, batch, lines, width):
    size = lines * width
    channels = padded.shape[1]
    left_ok, right_ok = column_masks(size, width)
    for b in range(batch):
        start = 8 + b * size
        for c in range(0, channels, LANES):
            columns = slice(c, c + LANES)
            triple[b, :, c : c + LANES] = (padded[start - 1 : start - 1 + size, columns] * left_ok).astype(BF16)
            triple[b, :, channels + c : channels + c + LANES] = padded[start : start + size, columns].astype(BF16)
            triple[b, :, 2 * channels + c : 2 * channels + c + LANES] = (
                padded[start + 1 : start + 1 + size, columns] * right_ok
            ).astype(BF16)


def middle_kernel(
    dims, core, gathered, raw, halo, mask, above, below, params, weight,
    unit, slope, stats, out, message, triple, give, rows, padded,
):
    batch, height, width = dims
    pixels = height * width
    size = pixels + 2 * width
    blocks = raw.shape[1] // LANES
    join_stats(gathered, gathered, 2 * blocks, stats, blocks)
    everything = slice(0, raw.shape[1])
    _, value = normed(halo[...], stats, params, everything)
    rim, _ = silu_parts(value)
    padded[0:8, :] = jnp.zeros((8, raw.shape[1]), F32)
    padded[8 + batch * size :, :] = jnp.zeros((8, raw.shape[1]), F32)
    for b in range(batch):
        line = slice(b * width, (b + 1) * width)
        top = 8 + b * size
        padded[top : top + width, :] = rim[line] * wide(above[line, :], raw.shape[1])
        padded[top + size - width : top + size, :] = rim[line] * wide(below[line, :], raw.shape[1])

    def keep(here, columns, value):
        b = here.start // pixels
        start = 8 + b * size + width + here.start - b * pixels
        padded[start : start + here.stop - here.start, columns] = value

    act_pass(raw, mask, stats, params, unit, slope, None, keep=keep)
    send(unit, slope, stats)
    fill_triple(padded, triple, batch, height + 2, width)
    send(triple)
    give_taps(core, triple, give)
    total = None
    for tap in range(3):
        left = triple[:, tap * width : tap * width + pixels, :].reshape(batch * pixels, -1)
        part = dot(left, weight[tap])
        total = part if total is None else total + part
    out[...] = total
    local_stats(out, mask, rows)
    spread_message(message, rows)


def give_taps(core, taps, give):
    full, half = taps.shape[2] // 3, give.shape[2] // 3
    for tap in range(3):
        start = pl.multiple_of(tap * full + (1 - core[0]) * half, LANES)
        give[:, :, tap * half : (tap + 1) * half] = taps[:, :, pl.ds(start, half)]
    send(give)


def closing_kernel(
    core, gathered, counts, raw, mask, params, weight, act, unit, slope, stats, out, message, give, rows
):
    blocks = raw.shape[1] // LANES
    join_stats(gathered, counts, 4, stats, blocks)
    act_pass(raw, mask, stats, params, unit, slope, act)
    send(unit, slope, act, stats)
    give_half(core, act, give)
    out[...] = dot(act[...], weight[...])
    local_stats(out, mask, rows)
    spread_message(message, rows)


def widen_kernel(
    dims, core, gathered, counts, raw, entry_in, mask, params, weight,
    act, unit, slope, stats, short, out, edge, message, give, give_short, rows, even,
):
    batch, height, width = dims
    pixels = height * width
    blocks = raw.shape[1] // LANES
    join_stats(gathered, counts, 4, stats, blocks)

    def keep(here, columns, value):
        put_blocks(even, here, columns, value)

    act_pass(raw, mask, stats, params, unit, slope, act, skip=entry_in, keep=keep)
    send(unit, slope, act, stats)
    give_half(core, act, give)
    out[...] = dot(act[...], weight[...])
    for b in range(batch):
        edge[b * width : (b + 1) * width, :] = out[(b + 1) * pixels - width : (b + 1) * pixels, :]
    local_stats(out, mask, rows)
    spread_message(message, rows)
    for c in range(0, raw.shape[1], LANES):
        columns = slice(c, c + LANES)
        lines = []
        for b in range(batch):
            for i in range(height // 2):
                lines.append(even[c // LANES, pl.ds(b * pixels + 2 * i * width, width // 2, stride=2), :])
        short[:, columns] = jnp.concatenate(lines, axis=0).astype(BF16)
    send(short)
    give_half(core, short, give_short)


def shortcut_kernel(short, small, weight, out, rows):
    out[...] = dot(short[...], weight[...])
    send(out)
    local_stats(out, small, rows)


def strided_kernel(
    dims, core, gathered, counts, raw, halo, mask, small, above, params, weight,
    unit, slope, stats, out, message, taps, give, rows, padded,
):
    batch, height, width = dims
    pixels = height * width
    size = pixels + width
    half, half_width = height // 2, width // 2
    blocks = raw.shape[1] // LANES
    join_stats(gathered, counts, 4, stats, blocks)
    everything = slice(0, raw.shape[1])
    _, value = normed(halo[...], stats, params, everything)
    rim, _ = silu_parts(value)
    for block in range(padded.shape[0]):
        padded[block, 0:8, :] = jnp.zeros((8, LANES), F32)
    for b in range(batch):
        line = slice(b * width, (b + 1) * width)
        start = 8 + b * size
        put_blocks(padded, slice(start, start + width), everything, rim[line] * wide(above[line, :], raw.shape[1]))

    def keep(here, columns, value):
        b = here.start // pixels
        start = 8 + b * size + width + here.start - b * pixels
        put_blocks(padded, slice(start, start + here.stop - here.start), columns, value)

    act_pass(raw, mask, stats, params, unit, slope, None, keep=keep)
    send(unit, slope, stats)
    lines = height + 1
    not_first, _ = column_masks(lines * half_width, half_width)
    channels = raw.shape[1]
    for block in range(channels // LANES):
        for b in range(batch):
            start = 8 + b * size
            before = padded[block, pl.ds(start - 1, lines * half_width, stride=2), :] * not_first
            at = padded[block, pl.ds(start, lines * half_width, stride=2), :]
            after = padded[block, pl.ds(start + 1, lines * half_width, stride=2), :]
            for k, value in enumerate((before, at, after)):
                value = value.reshape(lines, half_width, LANES)
                place = k * channels + block * LANES
                for tap in range(3):
                    pieces = [value[tap + 2 * i] for i in range(half)]
                    taps[tap, b * half * half_width : (b + 1) * half * half_width, place : place + LANES] = (
                        jnp.concatenate(pieces, axis=0).astype(BF16)
                    )
    send(taps)
    give_taps(core, taps, give)
    total = None
    for tap in range(3):
        part = dot(taps[tap], weight[tap])
        total = part if total is None else total + part
    out[...] = total
    local_stats(out, small, rows)
    spread_message(message, rows)


def expand_kernel(
    gathered, counts, raw, small, params, weight, short_rows, flag, core,
    act, unit, slope, stats, out, mine, theirs, give, rows,
):
    blocks = raw.shape[1] // LANES
    join_stats(gathered, counts, 5, stats, blocks)
    act_pass(raw, small, stats, params, unit, slope, act)
    send(unit, slope, act, stats)
    give_half(core, act, give)
    out[...] = dot(act[...], weight[...])
    local_stats(out, small, rows)
    upper = flag[0]
    size = rows.shape[0]
    number = jnp.broadcast_to(column_sum(small[...]), (8, LANES))
    mine[:size, :] = rows[...] * upper + short_rows[...] * (1.0 - upper)
    theirs[:size, :] = rows[...] * (1.0 - upper) + short_rows[...] * upper
    mine[size:, :] = number
    theirs[size:, :] = number


def pair_kernel(mine, other, message):
    size = mine.shape[0] - 8
    blocks = size // 2
    first, second = mine[size : size + 1, :], other[size : size + 1, :]
    both = first + second
    gap = mine[:blocks, :] / jnp.maximum(first, 1.0) - other[:blocks, :] / jnp.maximum(second, 1.0)
    weight = first * second / jnp.maximum(both, 1.0)
    total = mine[:blocks, :] + other[:blocks, :]
    square = mine[blocks:size, :] + other[blocks:size, :] + gap * gap * weight
    number = jnp.broadcast_to(both, (8, LANES))
    for i in range(message.shape[0]):
        message[i, :blocks, :] = total
        message[i, blocks:size, :] = square
        message[i, size:, :] = number


def join_kernel(gathered, stats):
    size = gathered.shape[1] - 8
    stats[...] = jnp.zeros_like(stats)
    join_stats(gathered, gathered, size, stats, size // 2)


def final_kernel(
    own, other, flag, expand_raw, short_raw, small, expand_params, short_params, cotangent,
    features, grad, expand_unit, short_unit, expand_stats, short_stats, mine, theirs, rows,
):
    upper = flag[0]
    expand_stats[...] = own[...] * upper + other[...] * (1.0 - upper)
    short_stats[...] = own[...] * (1.0 - upper) + other[...] * upper
    height, width = expand_raw.shape
    blocks = width // LANES
    for block in range(blocks):
        columns = slice(block * LANES, (block + 1) * LANES)
        first, first_value = normed(expand_raw[:, columns], expand_stats, expand_params, columns)
        second, second_value = normed(short_raw[:, columns], short_stats, short_params, columns)
        out, rise = silu_parts(first_value + second_value)
        features[:, columns] = (out * small[...]).astype(BF16)
        value = cotangent[:, columns].astype(F32) * (rise * small[...])
        grad[:, columns] = value
        expand_unit[:, columns] = first
        short_unit[:, columns] = second
        rows[block : block + 1, :] = column_sum(value * first)
        rows[blocks + block : blocks + block + 1, :] = column_sum(value * second)
        rows[2 * blocks + block : 2 * blocks + block + 1, :] = column_sum(value)
    half = blocks // 2
    for stat in range(3):
        low = rows[stat * blocks : stat * blocks + half, :]
        high = rows[stat * blocks + half : (stat + 1) * blocks, :]
        mine[stat * half : (stat + 1) * half, :] = low * upper + high * (1.0 - upper)
        theirs[stat * half : (stat + 1) * half, :] = low * (1.0 - upper) + high * upper


def last_grads_kernel(
    batch, own, other, flag, counts, grad, expand_unit, short_unit, expand_stats, short_stats,
    expand_params, short_params, small, weight, slope, unit,
    expand_affine, short_affine, expand_grad, short_grad, back, edge, message, rows,
):
    upper = flag[0]
    half = own.shape[0] // 3
    for stat in range(3):
        part = slice(stat * half, (stat + 1) * half)
        low = own[part, :] * upper + other[part, :] * (1.0 - upper)
        high = own[part, :] * (1.0 - upper) + other[part, :] * upper
        for block in range(2 * half):
            value = low[block : block + 1, :] if block < half else high[block - half : block - half + 1, :]
            columns = slice(block * LANES, (block + 1) * LANES)
            if stat == 0:
                expand_affine[0:1, columns] = value
            elif stat == 1:
                short_affine[0:1, columns] = value
            else:
                expand_affine[1:2, columns] = value
                short_affine[1:2, columns] = value
    count = total_count(counts, 5)
    for here, columns in chunks(*grad.shape):
        expand_grad[here, columns] = raw_grad(
            grad[here, columns], expand_unit[here, columns], small[here, :], expand_affine, expand_stats,
            expand_params, count, columns,
        ).astype(BF16)
        short_grad[here, columns] = raw_grad(
            grad[here, columns], short_unit[here, columns], small[here, :], short_affine, short_stats,
            short_params, count, columns,
        ).astype(BF16)
    send(expand_grad, short_grad, expand_affine, short_affine)
    back[...] = dot_back(expand_grad[...], weight[...])
    back_pass(back, unit, slope, rows)
    spread_message(message, rows)
    pixels = back.shape[0] // batch
    line = edge.shape[0] // (2 * batch)
    for b in range(batch):
        edge[b * line : (b + 1) * line, :] = back[b * pixels : b * pixels + line, :]
        edge[(batch + b) * line : (batch + b + 1) * line, :] = unit[b * pixels : b * pixels + line, :]


def short_back_kernel(dims, grad, weight, out):
    batch, height, width = dims
    pixels = height * width
    small = dot_back(grad[...], weight[...])
    out[...] = jnp.zeros(out.shape, out.dtype)
    half = width // 2
    for block in range(out.shape[0]):
        columns = slice(block * LANES, (block + 1) * LANES)
        for b in range(batch):
            for i in range(height // 2):
                place = b * pixels // 4 + i * half
                start = b * pixels + 2 * i * width
                out[block, pl.ds(start, half, stride=2), :] = small[place : place + half, columns]


def widen_back_kernel(
    dims, gathered, counts, back, unit, halo, small, small_below, stats, params, weight, out_unit, out_slope,
    affine, grad, out, message, rows, padded, full,
):
    batch, height, width = dims
    pixels = height * width
    half, half_width = height // 2, width // 2
    size = (half + 1) * half_width
    join_sums(gathered, affine)
    count = total_count(counts, 5)
    channels = back.shape[1]
    everything = slice(0, channels)
    line = batch * half_width
    rim = raw_grad(
        halo[:line, :], halo[line:, :], small_below[...], affine, stats, params, count, everything
    ).astype(BF16).astype(F32)
    for b in range(batch):
        stop = (b + 1) * size
        padded[stop - half_width : stop, :] = rim[b * half_width : (b + 1) * half_width]
    padded[batch * size :, :] = jnp.zeros((8, channels), F32)
    small_pixels = half * half_width
    for here, columns in chunks(back.shape[0], channels, chunk=small_pixels):
        value = raw_grad(
            back[here, columns], unit[here, columns], small[here, :], affine, stats, params, count, columns
        ).astype(BF16)
        grad[here, columns] = value
        b = here.start // small_pixels
        padded[b * size : b * size + small_pixels, columns] = value.astype(F32)
    send(grad, affine)
    _, not_last = column_masks(small_pixels, half_width)
    not_last = wide(not_last, channels)

    def moved(down, right):
        pieces = []
        for b in range(batch):
            start = b * size + down * half_width + right
            piece = padded[start : start + small_pixels, :]
            pieces.append(piece * not_last if right else piece)
        return jnp.concatenate(pieces, axis=0).astype(BF16)

    here, right, down, across = moved(0, 0), moved(0, 1), moved(1, 0), moved(1, 1)
    phases = {
        (0, 0): dot_back(here, weight[1, 1]),
        (0, 1): dot_back(here, weight[1, 2]) + dot_back(right, weight[1, 0]),
        (1, 0): dot_back(here, weight[2, 1]) + dot_back(down, weight[0, 1]),
        (1, 1): dot_back(here, weight[2, 2])
        + dot_back(right, weight[2, 0])
        + dot_back(down, weight[0, 2])
        + dot_back(across, weight[0, 0]),
    }
    for (a, e), value in phases.items():
        for b in range(batch):
            for i in range(half):
                place = b * small_pixels + i * half_width
                start = b * pixels + (2 * i + a) * width + e
                for block in range(full.shape[0]):
                    full[block, pl.ds(start, half_width, stride=2), :] = value[
                        place : place + half_width, block * LANES : (block + 1) * LANES
                    ]
    for block in range(full.shape[0]):
        out[:, block * LANES : (block + 1) * LANES] = full[block]
    back_pass(out, out_unit, out_slope, rows)
    spread_message(message, rows)


def block_back_kernel(
    gathered, counts, back, unit, mask, stats, params, weight, short_back, out_unit, out_slope,
    affine, grad, out, message, again, rows,
):
    join_sums(gathered, affine)
    grad_pass(back, unit, mask, affine, stats, params, total_count(counts, 4), grad)
    send(grad, affine)
    short = jnp.concatenate([short_back[block] for block in range(short_back.shape[0])], axis=1)
    out[...] = dot_back(grad[...], weight[...]) + short
    back_pass(out, out_unit, out_slope, rows)
    again[...] = out[...]
    send(again)
    spread_message(message, rows)


def middle_back_kernel(
    dims, flag, gathered, counts, back, unit, mask, stats, params, weight, out_unit, out_slope,
    affine, grad, out, edge, message, rows,
):
    batch, height, width = dims
    pixels = height * width
    upper = flag[0]
    join_sums(gathered, affine)
    grad_pass(back, unit, mask, affine, stats, params, total_count(counts, 4), grad)
    send(grad, affine)
    out[...] = dot_back(grad[...], weight[...])
    back_pass(out, out_unit, out_slope, rows)
    spread_message(message, rows)
    for place, source in ((0, out), (batch, out_unit)):
        for b in range(batch):
            first = source[b * pixels : b * pixels + width, :]
            last = source[(b + 1) * pixels - width : (b + 1) * pixels, :]
            edge[(place + b) * width : (place + b + 1) * width, :] = last * upper + first * (1.0 - upper)


def entry_back_kernel(
    dims, gathered, counts, back, unit, halo, mask, above, below, stats, params, weight, out_unit, out_slope,
    affine, grad, out, message, rows, padded, triple,
):
    batch, height, width = dims
    pixels = height * width
    size = pixels + 2 * width
    join_sums(gathered, affine)
    count = total_count(counts, 4)
    channels = back.shape[1]
    everything = slice(0, channels)
    line = batch * width
    padded[0:8, :] = jnp.zeros((8, channels), F32)
    padded[8 + batch * size :, :] = jnp.zeros((8, channels), F32)
    up = raw_grad(halo[:line, :], halo[line:, :], above[...], affine, stats, params, count, everything)
    down = raw_grad(halo[:line, :], halo[line:, :], below[...], affine, stats, params, count, everything)
    for b in range(batch):
        here = slice(b * width, (b + 1) * width)
        top = 8 + b * size
        padded[top : top + width, :] = up[here]
        padded[top + size - width : top + size, :] = down[here]

    def keep(here, columns, value):
        b = here.start // pixels
        start = 8 + b * size + width + here.start - b * pixels
        padded[start : start + here.stop - here.start, columns] = value

    grad_pass(back, unit, mask, affine, stats, params, count, grad, keep=keep)
    send(grad, affine)
    fill_triple(padded, triple, batch, height + 2, width)
    total = None
    for row_tap in range(3):
        shift = (2 - row_tap) * width
        for col_tap in range(3):
            side = (2 - col_tap) * channels
            left = triple[:, shift : shift + pixels, side : side + channels].reshape(batch * pixels, channels)
            part = dot_back(left, weight[row_tap, col_tap])
            total = part if total is None else total + part
    out[...] = total
    back_pass(out, out_unit, out_slope, rows)
    spread_message(message, rows)


def images_kernel(gathered, counts, back, unit, mask, stats, params, weight, block_back, affine, grad, out):
    join_sums(gathered, affine)
    grad_pass(back, unit, mask, affine, stats, params, total_count(counts, 4), grad)
    send(grad, affine)
    step = 256
    for start in range(0, out.shape[1], step):
        columns = slice(start, start + step)
        value = dot_back(grad[...], weight[columns, :]) + block_back[:, columns]
        out[:, columns] = (value * wide(mask[...], step)).astype(BF16)


def dot_pixels(left, grad):
    return lax.dot_general(left, grad, (((0,), (0,)), ((), ())), preferred_element_type=F32)


def chip_grad(core, left, left_other, grad, grad_other, columns=slice(None)):
    half = left_other.shape[1]
    return dot_pixels(left[:, own_half(core, half)], grad[:, columns]) + dot_pixels(
        left_other[...], grad_other[:, columns]
    )


def deal(place, full, kept, sent):
    groups = len(kept)
    rows, width = full.shape[0] // 2, full.shape[1] // groups
    for group in range(groups):
        columns = slice(group * width, (group + 1) * width)
        mine = place[group]
        sent[group][...] = full[pl.ds(pl.multiple_of((1 - mine) * rows, 16), rows), columns]
        send(sent[group])
        kept[group][...] = full[pl.ds(pl.multiple_of(mine * rows, 16), rows), columns]
        send(kept[group])


def first_wave_kernel(
    core, place, short, short_other, strided, strided_other,
    short_grad, short_grad_other, expand_grad, expand_grad_other,
    kept_a, kept_b, sent_a, sent_b, full,
):
    rows = short_other.shape[1]
    step = 512
    for start in range(0, full.shape[1], step):
        columns = slice(start, start + step)
        full[:rows, columns] = chip_grad(
            core, short, short_other, short_grad, short_grad_other, columns
        ).astype(BF16)
        full[rows:, columns] = chip_grad(
            core, strided, strided_other, expand_grad, expand_grad_other, columns
        ).astype(BF16)
    deal(place, full, (kept_a, kept_b), (sent_a, sent_b))


def second_wave_kernel(
    core, place, taps, taps_other, strided_grad, strided_grad_other, block, block_other, widen_grad, widen_grad_other,
    kept_a, kept_b, sent_a, sent_b, full,
):
    half = taps_other.shape[2] // 3
    channels = 2 * half
    for row_tap in range(3):
        for col_tap in range(3):
            start = pl.multiple_of(col_tap * channels + core[0] * half, LANES)
            own = dot_pixels(taps[row_tap, :, pl.ds(start, half)], strided_grad[...])
            other = dot_pixels(
                taps_other[row_tap, :, col_tap * half : (col_tap + 1) * half], strided_grad_other[...]
            )
            place_row = (3 * row_tap + col_tap) * half
            full[place_row : place_row + half, :] = (own + other).astype(BF16)
    full[9 * half :, :] = chip_grad(core, block, block_other, widen_grad, widen_grad_other).astype(BF16)
    deal(place, full, (kept_a, kept_b), (sent_a, sent_b))


def third_wave_kernel(
    dims, core, place, triple, triple_other, middle_grad, middle_grad_other, act, act_other, closing_grad, closing_grad_other,
    kept_a, kept_b, sent_a, sent_b, full,
):
    batch, height, width = dims
    pixels = height * width
    half = triple_other.shape[2] // 3
    channels = 2 * half
    for row_tap in range(3):
        lines = slice(row_tap * width, row_tap * width + pixels)
        for col_tap in range(3):
            start = pl.multiple_of(col_tap * channels + core[0] * half, LANES)
            own = triple[:, lines, pl.ds(start, half)].reshape(batch * pixels, half)
            other = triple_other[:, lines, col_tap * half : (col_tap + 1) * half].reshape(batch * pixels, half)
            value = dot_pixels(own, middle_grad[...]) + dot_pixels(other, middle_grad_other[...])
            place_row = (3 * row_tap + col_tap) * half
            full[place_row : place_row + half, :] = value.astype(BF16)
    step = full.shape[1]
    for block in range(closing_grad.shape[1] // step):
        columns = slice(block * step, (block + 1) * step)
        start = (9 + block) * half
        full[start : start + half, :] = chip_grad(
            core, act, act_other, closing_grad, closing_grad_other, columns
        ).astype(BF16)
    used = (9 + closing_grad.shape[1] // step) * half
    if used < full.shape[0]:
        full[used:, :] = jnp.zeros((full.shape[0] - used, step), BF16)
    deal(place, full, (kept_a, kept_b), (sent_a, sent_b))


def last_wave_kernel(core, entry_in, entry_in_other, grad, grad_other, out):
    out[...] = chip_grad(core, entry_in, entry_in_other, grad, grad_other).astype(BF16)


def add_halves(first, second):
    return (first.astype(F32) + second.astype(F32)).astype(BF16)


def fold_kernel(groups, place, *refs):
    kept, got, keep, pass_on = (refs[i * groups : (i + 1) * groups] for i in range(4))
    for group in range(groups):
        rows = keep[group].shape[-2]
        for mine, out in ((1 - place[group], pass_on[group]), (place[group], keep[group])):
            here = pl.ds(pl.multiple_of(mine * rows, 16), rows)
            if kept[group].ndim == 3:
                out[...] = add_halves(kept[group][:, here, :], got[group][:, here, :])
            else:
                out[...] = add_halves(kept[group][here, :], got[group][here, :])
            send(out)


def add_kernel(kept, got, out):
    out[...] = add_halves(kept[...], got[...])


def merge_kernel(groups, place, *refs):
    own, got, out = (refs[i * groups : (i + 1) * groups] for i in range(3))
    for group in range(groups):
        rows = own[group].shape[-2]
        for mine, value in ((place[group], own[group]), (1 - place[group], got[group])):
            here = pl.ds(pl.multiple_of(mine * rows, 16), rows)
            if own[group].ndim == 3:
                out[group][:, here, :] = value[...]
            else:
                out[group][here, :] = value[...]


def fill(place, own, got, full):
    width = full.shape[1] // len(own)
    for group in range(len(own)):
        columns = slice(group * width, (group + 1) * width)
        rows = own[group].shape[0]
        for mine, value in ((place[group], own[group]), (1 - place[group], got[group])):
            full[pl.ds(pl.multiple_of(mine * rows, 16), rows), columns] = value[...]


def first_out_kernel(place, own_a, own_b, got_a, got_b, short, expand, full):
    fill(place, (own_a, own_b), (got_a, got_b), full)
    rows = short.shape[0]
    short[...] = full[:rows, :].astype(F32)
    send(short)
    expand[...] = full[rows:, :].astype(F32)


def second_out_kernel(place, own_a, own_b, got_a, got_b, strided, widen, full):
    fill(place, (own_a, own_b), (got_a, got_b), full)
    rows = strided.shape[1]
    for tap in range(9):
        strided[tap] = full[tap * rows : (tap + 1) * rows, :].astype(F32)
    send(strided)
    widen[...] = full[9 * rows :, :].astype(F32)


def third_out_kernel(place, own_a, own_b, got_a, got_b, middle, closing, full):
    fill(place, (own_a, own_b), (got_a, got_b), full)
    rows = middle.shape[1]
    for tap in range(9):
        middle[tap] = full[tap * rows : (tap + 1) * rows, :].astype(F32)
    step = full.shape[1]
    for block in range(closing.shape[1] // step):
        start = (9 + block) * rows
        closing[:, block * step : (block + 1) * step] = full[start : start + rows, :].astype(F32)


def place_of(bits):
    here = lax.axis_index("img")
    return jnp.stack([(here >> bit) & 1 for bit in bits]).astype(jnp.int32)


def stack_pair(pair):
    return [jnp.stack(pair)]


def sum_over_chips(kept, sent, out_kernel, outs, full):
    steps = list(zip(*orders()))
    halvings = 1
    while halvings < len(steps) and kept[0].shape[0] % (16 << halvings) == 0:
        halvings += 1
    merged = False
    for number, bits in enumerate(steps):
        got = [permute_bit(value, bit) for value, bit in zip(sent, bits)]
        following = steps[number + 1] if number + 1 < len(steps) else None
        if following is not None and following[0] == following[1] and not merged:
            kept, got, merged = stack_pair(kept), stack_pair(got), True
        groups = len(kept)
        if number + 1 >= halvings:
            kept = sent = [
                call(add_kernel, [(one.shape, BF16)], one, other, late=None)[0] for one, other in zip(kept, got)
            ]
            continue
        shapes = [value.shape[:-2] + (value.shape[-2] // 2, value.shape[-1]) for value in kept]
        results = call(
            functools.partial(fold_kernel, groups),
            [(shape, BF16) for shape in shapes] * 2,
            place_of(following[:groups]),
            *kept,
            *got,
            smem=(0,),
            late=None,
        )
        kept, sent = results[:groups], results[groups:]
    own = kept
    for number, bits in reversed(list(enumerate(steps[:halvings]))):
        if bits[0] != bits[1] and merged:
            own, merged = [own[0][0], own[0][1]], False
        got = [permute_bit(value, bit) for value, bit in zip(own, bits)]
        groups = len(own)
        if number == 0:
            return call(
                out_kernel, outs, place_of(bits), *own, *got, smem=(0,), scratch=[(full, BF16)], late=None
            )
        shapes = [value.shape[:-2] + (value.shape[-2] * 2, value.shape[-1]) for value in own]
        own = call(
            functools.partial(merge_kernel, groups),
            [(shape, BF16) for shape in shapes],
            place_of(bits[:groups]),
            *own,
            *got,
            smem=(0,),
            late=None,
        )


def sum_over_chips_short(parts):
    members = lax.axis_size("img")
    moved = lax.all_to_all(parts, "img", 0, 0, tiled=True)
    share = jnp.sum(moved.astype(F32), axis=0).astype(BF16)
    spread = jnp.broadcast_to(share[None], (members,) + share.shape)
    return lax.all_to_all(spread, "img", 0, 0, tiled=True).reshape(-1, parts.shape[-1])


def per_device(
    images,
    extents,
    entry_weight,
    middle_weight,
    closing_weight,
    widen_weight,
    strided_weight,
    expand_weight,
    shortcut_weight,
    entry_affine,
    middle_affine,
    closing_affine,
    widen_affine,
    strided_affine,
    expand_affine,
    shortcut_affine,
    cotangent,
):
    batch, height, width, wide_in = images.shape
    dims = (batch, height, width)
    pixels = batch * height * width
    small_pixels = pixels // 4
    chips = lax.axis_size("img")
    devices = chips * lax.axis_size("row")
    row = lax.axis_index("row")
    upper = row == 0
    flag = jnp.where(upper, 1.0, 0.0).astype(F32).reshape(1)
    core = row.astype(jnp.int32).reshape(1)
    local = extents - jnp.stack([row * height, 0]).astype(jnp.int32)
    mid, wider, last = entry_weight.shape[1], widen_weight.shape[1], expand_weight.shape[1]

    def message_rows(channels):
        return max(8, 2 * channels // LANES)

    def message(channels):
        return ((devices, message_rows(channels), LANES), F32)

    def rows(channels):
        return ((message_rows(channels), LANES), F32)

    def stat(channels):
        return ((8, channels), F32)

    def level(count, channels):
        return [((count, channels), BF16), ((count, channels), F32), ((count, channels), F32), stat(channels)]

    def ops(count, *sizes):
        total = 2 * count
        for size in sizes:
            total *= size
        return total

    entry_in, mask, small, above, below, small_below, entry_raw, edge, sent, give = call(
        functools.partial(entry_kernel, dims),
        [
            ((pixels, wide_in), BF16),
            ((pixels, LANES), F32),
            ((small_pixels, LANES), F32),
            ((batch * width, LANES), F32),
            ((batch * width, LANES), F32),
            ((batch * width // 2, LANES), F32),
            ((pixels, mid), F32),
            ((batch * width, mid), F32),
            message(mid),
            ((pixels, wide_in // 2), BF16),
        ],
        local,
        flag,
        core,
        images.reshape(pixels, wide_in),
        entry_weight,
        scratch=[rows(mid)],
        smem=(0, 1, 2),
        late=(3, 4),
        keep=(6, 7, 8),
        flops=ops(pixels, wide_in, mid),
    )
    halo = swap_rows(edge)
    entry_in_other = swap_rows(give)
    counts = gather_all(sent)
    padded_rows = batch * (height + 2) * width
    entry_unit, entry_slope, entry_stats, middle_raw, sent, triple, give = call(
        functools.partial(middle_kernel, dims),
        level(pixels, mid)[1:]
        + [
            ((pixels, mid), F32),
            message(mid),
            ((batch, (height + 2) * width, 3 * mid), BF16),
            ((batch, (height + 2) * width, 3 * mid // 2), BF16),
        ],
        core,
        counts,
        entry_raw,
        halo,
        mask,
        above,
        below,
        entry_affine,
        middle_weight.reshape(3, 3 * mid, mid),
        scratch=[rows(mid), ((padded_rows + 16, mid), F32)],
        smem=(0,),
        late=(8,),
        keep=(3, 4),
        flops=ops(pixels, 9, mid, mid),
    )
    triple_other = swap_rows(give)
    gathered = gather_all(sent)
    middle_act, middle_unit, middle_slope, middle_stats, closing_raw, sent, give = call(
        closing_kernel,
        level(pixels, mid) + [((pixels, wide_in), F32), message(wide_in), ((pixels, mid // 2), BF16)],
        core,
        gathered,
        counts,
        middle_raw,
        mask,
        middle_affine,
        closing_weight,
        scratch=[rows(wide_in)],
        smem=(0,),
        late=(6,),
        keep=(4, 5),
        flops=ops(pixels, mid, wide_in),
    )
    middle_act_other = swap_rows(give)
    gathered = gather_all(sent)
    block_out, closing_unit, block_slope, closing_stats, shortcut_in, widen_raw, edge, sent, give, give_short = call(
        functools.partial(widen_kernel, dims),
        level(pixels, wide_in)
        + [
            ((small_pixels, wide_in), BF16),
            ((pixels, wider), F32),
            ((batch * width, wider), F32),
            message(wider),
            ((pixels, wide_in // 2), BF16),
            ((small_pixels, wide_in // 2), BF16),
        ],
        core,
        gathered,
        counts,
        closing_raw,
        entry_in,
        mask,
        closing_affine,
        widen_weight,
        scratch=[rows(wider), ((wide_in // LANES, pixels, LANES), F32)],
        smem=(0,),
        late=(4, 7),
        keep=(5, 6, 7),
        flops=ops(pixels, wide_in, wider),
    )
    halo = swap_rows(edge)
    block_other, short_other = swap_rows(give), swap_rows(give_short)
    gathered = gather_all(sent)
    shortcut_raw, shortcut_rows = call(
        shortcut_kernel,
        [((small_pixels, last), F32), rows(last)],
        shortcut_in,
        small,
        shortcut_weight,
        late=(0, 2),
        keep=(),
        flops=ops(small_pixels, wide_in, last),
    )
    widen_unit, widen_slope, widen_stats, strided_raw, sent, taps, give = call(
        functools.partial(strided_kernel, dims),
        level(pixels, wider)[1:]
        + [
            ((small_pixels, wider), F32),
            message(wider),
            ((3, small_pixels, 3 * wider), BF16),
            ((3, small_pixels, 3 * wider // 2), BF16),
        ],
        core,
        gathered,
        counts,
        widen_raw,
        halo,
        mask,
        small,
        above,
        widen_affine,
        strided_weight.reshape(3, 3 * wider, wider),
        scratch=[rows(wider), ((wider // LANES, batch * (height + 1) * width + 16, LANES), F32)],
        smem=(0,),
        late=(9,),
        keep=(3, 4),
        flops=ops(small_pixels, 9, wider, wider),
    )
    taps_other = swap_rows(give)
    gathered = gather_all(sent)
    pair_rows = message_rows(last) + 8
    strided_act, strided_unit, strided_slope, strided_stats, expand_raw, mine, theirs, give = call(
        expand_kernel,
        level(small_pixels, wider)
        + [
            ((small_pixels, last), F32),
            ((pair_rows, LANES), F32),
            ((pair_rows, LANES), F32),
            ((small_pixels, wider // 2), BF16),
        ],
        gathered,
        counts,
        strided_raw,
        small,
        strided_affine,
        expand_weight,
        shortcut_rows,
        flag,
        core,
        scratch=[rows(last)],
        smem=(7, 8),
        late=(5, 6),
        keep=(4, 5, 6),
        flops=ops(small_pixels, wider, last),
    )
    strided_act_other = swap_rows(give)
    (sent,) = call(pair_kernel, [((chips, pair_rows, LANES), F32)], mine, swap_rows(theirs), keep=(0,))
    (own_stats,) = call(join_kernel, [stat(last)], gather_img(sent), keep=(0,))
    half_rows = 3 * last // (2 * LANES)
    features, final_grad, expand_unit, shortcut_unit, expand_stats, shortcut_stats, mine, theirs = call(
        final_kernel,
        [
            ((small_pixels, last), BF16),
            ((small_pixels, last), F32),
            ((small_pixels, last), F32),
            ((small_pixels, last), F32),
            stat(last),
            stat(last),
            ((half_rows, LANES), F32),
            ((half_rows, LANES), F32),
        ],
        own_stats,
        swap_rows(own_stats),
        flag,
        expand_raw,
        shortcut_raw,
        small,
        expand_affine,
        shortcut_affine,
        cotangent.reshape(small_pixels, last),
        late=(4, 8),
        keep=(1, 2, 3, 4, 5, 6, 7),
        scratch=[((3 * last // LANES, LANES), F32)],
        smem=(2,),
    )

    joined = mine + swap_rows(theirs)
    own_sums = jnp.sum(gather_img(jnp.broadcast_to(joined[None], (chips,) + joined.shape)), axis=0)
    affine_expand, affine_shortcut, expand_grad, shortcut_grad, strided_back, edge, sent = call(
        functools.partial(last_grads_kernel, batch),
        [
            ((2, last), F32),
            ((2, last), F32),
            ((small_pixels, last), BF16),
            ((small_pixels, last), BF16),
            ((small_pixels, wider), F32),
            ((batch * width, wider), F32),
            message(wider),
        ],
        own_sums,
        swap_rows(own_sums),
        flag,
        counts,
        final_grad,
        expand_unit,
        shortcut_unit,
        expand_stats,
        shortcut_stats,
        expand_affine,
        shortcut_affine,
        small,
        expand_weight,
        strided_slope,
        strided_unit,
        scratch=[rows(wider)],
        smem=(2,),
        late=(12, 13, 14),
        keep=(4, 5, 6),
        flops=ops(small_pixels, wider, last),
    )
    halo = swap_rows(edge)
    gathered = gather_all(sent)

    def small_image(value):
        return value.reshape(batch, height // 2, width // 2, value.shape[-1])

    def image(value):
        return value.reshape(batch, height, width, value.shape[-1])

    (short_back,) = call(
        functools.partial(short_back_kernel, dims),
        [((wide_in // LANES, pixels, LANES), F32)],
        shortcut_grad,
        shortcut_weight,
        late=(0, 1),
        keep=(),
        flops=ops(small_pixels, wide_in, last),
    )
    two = place_of([bits[0] for bits in orders()])

    def wave(kernel, shape, *operands, flops):
        half = (shape[0] // 2, shape[1] // 2)
        results = call(
            kernel,
            [(half, BF16)] * 4,
            core,
            two,
            *operands,
            scratch=[(shape, BF16)],
            smem=(0, 1),
            flops=flops,
            late=None,
        )
        return results[:2], results[2:]

    first_shape = ((wide_in + wider) // 2, last)
    kept, sent_on = wave(
        first_wave_kernel,
        first_shape,
        shortcut_in,
        short_other,
        strided_act,
        strided_act_other,
        shortcut_grad,
        swap_rows(shortcut_grad),
        expand_grad,
        swap_rows(expand_grad),
        flops=ops(2 * small_pixels, *first_shape),
    )
    shortcut_total, expand_total = sum_over_chips(
        kept, sent_on, first_out_kernel, [((wide_in // 2, last), F32), ((wider // 2, last), F32)], first_shape
    )

    affine_strided, strided_grad, widen_back, sent = call(
        functools.partial(widen_back_kernel, dims),
        [((2, wider), F32), ((small_pixels, wider), BF16), ((pixels, wider), F32), message(wider)],
        gathered,
        counts,
        strided_back,
        strided_unit,
        halo,
        small,
        small_below,
        strided_stats,
        strided_affine,
        strided_weight,
        widen_unit,
        widen_slope,
        scratch=[
            rows(wider),
            ((batch * (height // 2 + 1) * width // 2 + 8, wider), F32),
            ((wider // LANES, pixels, LANES), F32),
        ],
        late=(3, 9, 10, 11),
        keep=(2, 3),
        flops=ops(small_pixels, 9, wider, wider),
    )
    gathered = gather_all(sent)
    affine_widen, widen_grad, block_back, sent, block_back_saved = call(
        block_back_kernel,
        [
            ((2, wider), F32),
            ((pixels, wider), BF16),
            ((pixels, wide_in), F32),
            message(wide_in),
            ((pixels, wide_in), F32),
        ],
        gathered,
        counts,
        widen_back,
        widen_unit,
        mask,
        widen_stats,
        widen_affine,
        widen_weight,
        short_back,
        closing_unit,
        block_slope,
        scratch=[rows(wide_in)],
        late=(3, 7, 8, 9, 10),
        keep=(2, 3),
        flops=ops(pixels, wide_in, wider),
    )
    gathered = gather_all(sent)

    second_shape = ((9 * wider + wide_in) // 2, wider)
    kept, sent_on = wave(
        second_wave_kernel,
        second_shape,
        taps,
        taps_other,
        strided_grad,
        swap_rows(strided_grad),
        block_out,
        block_other,
        widen_grad,
        swap_rows(widen_grad),
        flops=ops(2 * small_pixels, *second_shape),
    )
    strided_total, widen_total = sum_over_chips(
        kept, sent_on, second_out_kernel, [((9, wider // 2, wider), F32), ((wide_in // 2, wider), F32)], second_shape
    )

    affine_closing, closing_grad, middle_back, edge, sent = call(
        functools.partial(middle_back_kernel, dims),
        [
            ((2, wide_in), F32),
            ((pixels, wide_in), BF16),
            ((pixels, mid), F32),
            ((2 * batch * width, mid), F32),
            message(mid),
        ],
        flag,
        gathered,
        counts,
        block_back,
        closing_unit,
        mask,
        closing_stats,
        closing_affine,
        closing_weight,
        middle_unit,
        middle_slope,
        scratch=[rows(mid)],
        smem=(0,),
        late=(4, 8, 9, 10),
        keep=(2, 3, 4),
        flops=ops(pixels, wide_in, mid),
    )
    halo = swap_rows(edge)
    gathered = gather_all(sent)
    affine_middle, middle_grad, entry_back, sent = call(
        functools.partial(entry_back_kernel, dims),
        [((2, mid), F32), ((pixels, mid), BF16), ((pixels, mid), F32), message(mid)],
        gathered,
        counts,
        middle_back,
        middle_unit,
        halo,
        mask,
        above,
        below,
        middle_stats,
        middle_affine,
        middle_weight,
        entry_unit,
        entry_slope,
        scratch=[rows(mid), ((padded_rows + 16, mid), F32), ((batch, (height + 2) * width, 3 * mid), BF16)],
        late=(3, 10, 11, 12),
        keep=(2, 3),
        flops=ops(pixels, 9, mid, mid),
    )
    gathered = gather_all(sent)
    affine_entry, entry_grad, image_grads = call(
        images_kernel,
        [((2, mid), F32), ((pixels, mid), BF16), ((pixels, wide_in), BF16)],
        gathered,
        counts,
        entry_back,
        entry_unit,
        mask,
        entry_stats,
        entry_affine,
        entry_weight,
        block_back_saved,
        late=(3, 7, 8),
        keep=(),
        flops=ops(pixels, mid, wide_in),
    )

    third_rows = 9 * mid // 2 + wide_in // 2
    third_shape = (-(-third_rows // 256) * 256, mid)
    kept, sent_on = wave(
        functools.partial(third_wave_kernel, dims),
        third_shape,
        triple,
        triple_other,
        middle_grad,
        swap_rows(middle_grad),
        middle_act,
        middle_act_other,
        closing_grad,
        swap_rows(closing_grad),
        flops=ops(2 * pixels, *third_shape),
    )
    middle_total, closing_total = sum_over_chips(
        kept, sent_on, third_out_kernel, [((9, mid // 2, mid), F32), ((mid // 2, wide_in), F32)], third_shape
    )
    (parts,) = call(
        last_wave_kernel,
        [((wide_in // 2, mid), BF16)],
        core,
        entry_in,
        entry_in_other,
        entry_grad,
        swap_rows(entry_grad),
        smem=(0,),
        flops=ops(2 * pixels, wide_in // 2, mid),
        late=None,
    )
    entry_total = sum_over_chips_short(parts.reshape(chips, -1, mid))
    middle_total = middle_total.reshape(3, 3, mid // 2, mid)
    strided_total = strided_total.reshape(3, 3, wider // 2, wider)
    return (
        small_image(features),
        image(image_grads),
        entry_total.astype(F32),
        middle_total,
        closing_total,
        widen_total,
        strided_total,
        expand_total,
        shortcut_total,
        affine_entry,
        affine_middle,
        affine_closing,
        affine_widen,
        affine_strided,
        affine_expand,
        affine_shortcut,
    )


def solution(mesh):
    image = P("img", "row", None, None)
    return jax.shard_map(
        per_device,
        mesh=mesh,
        in_specs=(image, P("img", None)) + (P(),) * 14 + (image,),
        out_specs=(
            image,
            image,
            P("row", None),
            P(None, None, "row", None),
            P("row", None),
            P("row", None),
            P(None, None, "row", None),
            P("row", None),
            P("row", None),
        )
        + (P(),) * 7,
        check_vma=False,
    )
```

time: 6440 us -> 419 us (0.07)
  blocking collectives: 5520 us -> 49.2 us
  other arithmetic: 333 us -> 9.4 us
  local copies, waits for them, and re-layouts: 254 us -> 24.3 us
  Pallas kernels: 0 us -> 135 us
  waiting for transfers between devices: 231 us -> 112 us
  starting transfers between devices: 13.5 us -> 85.2 us
    unnamed x1 -> x0, blocking collectives: 4710 us -> none
    psum x20 -> x0, blocking collectives: 810 us -> none  [the longest x7 286 us: normalize(): total = lax.psum(jnp.sum(weighted, axis=(0, 1, 2)), ('img', 'row'))]
    concatenate x5 -> x0, other arithmetic: 226 us -> none  [the longest x2 222 us: reduce_grads(): packed = jnp.concatenate(pieces, axis=1)]
    all_gather x2 -> x0, waiting for transfers between devices: 181 us -> none  [reduce_grads(): lax.all_gather(slice_sum.astype(jnp.bfloat16), 'img', axis=1, tiled=True)]
    slice x21 -> x0, local copies, waits for them, and re-layouts: 160 us -> none  [the longest x6 145 us: reduce_grads(): result = totals[0, start:start + amount].reshape(local_shape)]
    pallas_call x0 -> x45, Pallas kernels: none -> 135 us  [call(): pl.pallas_call(body, out_shape=[(pltpu.VMEM if place in keep else pltpu.H...]
    ppermute x6 -> x58, waiting for transfers between devices: 0.02 us -> 80.5 us  [the longest x36 71.6 us: permute_bit(): return lax.ppermute(value, 'img', [(i, i ^ 1 << bit) for i in range(count)])]
  transfers between devices with their start and end apart: 9 -> 68, of which waited for: 3 -> 25; matrix products, arithmetic and copies ran while one was open for 4% -> 3% of each run, Pallas kernels for 0% -> 25%
where the time goes in v1:
time: 419 us; the launch traced here: 417 us
  Pallas kernels  135 us (32%)
  waiting for transfers between devices  112 us (27%)
  starting transfers between devices  85.2 us (20%)
  blocking collectives  49.2 us (12%)
  local copies, waits for them, and re-layouts  24.3 us (6%)
  other arithmetic  9.4 us (2%)
    pallas_call x45, Pallas kernels, call(): pl.pallas_call(body, out_shape=[(pltpu.VMEM if place in keep else pltpu.H...  135 us
    ppermute x36, waiting for transfers between devices, permute_bit(): return lax.ppermute(value, 'img', [(i, i ^ 1 << bit) for i in range(count)])  71.6 us
    ppermute x36, starting transfers between devices, permute_bit(): return lax.ppermute(value, 'img', [(i, i ^ 1 << bit) for i in range(count)])  43.6 us
    all_to_all x8, waiting for transfers between devices, gather_all(): return lax.all_to_all(message, BOTH, 0, 0, tiled=True)  31.7 us
    all_to_all x8, starting transfers between devices, gather_all(): return lax.all_to_all(message, BOTH, 0, 0, tiled=True)  27.1 us
    all_to_all x2, blocking collectives, gather_img(): return lax.all_to_all(message, 'img', 0, 0, tiled=True)  26.8 us
    all_to_all x2, blocking collectives, gather_all(): return lax.all_to_all(message, BOTH, 0, 0, tiled=True)  22.4 us
    unnamed x137, local copies, waits for them, and re-layouts  21.2 us
  transfers between devices with their start and end apart: 68, of which 25 were waited for; matrix products, arithmetic and copies ran while one was open for 3% of the time, Pallas kernels for 25%

profile of v1, /device:TPU:0, one launch (start us, length us, event | category | flops | bytes accessed | tf_op | source)
XLA Modules:
  0.0 416.7 jit_solution(13086332302638415966)
XLA Ops:
  5.1 7.3 %all-to-all-start = ((f32[32,8,128]{2,1,0:T(8,128)}), f32[32,8,128]{2,1,0:T(8,128)S(1)}, u32[]{:S(2)}, u32[]{:S(2)}) async-start(f32[32,8,128]{2,1,0:T(8,128)} %get-tuple-element.151), calls=%async_computation | async-start | bytes 262144 | tf_op jit(solution)/shard_map/all_to_all | solution.py:25
  13.8 6.9 %all-to-all-done.refs_1_.refs_2_.refs_3_ = f32[32,8,128]{2,1,0:T(8,128)S(1)} async-done(((f32[32,8,128]{2,1,0:T(8,128)}), f32[32,8,128]{2,1,0:T(8,128)S(1)}, u32[]{:S(2)}, u32[]{:S(2)}) %all-to-all-start) | async-done | bytes 131104 | tf_op jit(solution)/shard_map/all_to_all | solution.py:25
  25.5 10.0 %all_to_all.70.refs_1_ = f32[32,8,128]{2,1,0:T(8,128)S(1)} all-to-all(f32[32,8,128]{2,1,0:T(8,128)S(1)} %get-tuple-element.157), channel_id=1, replica_groups=mesh['img'=16,'row'=2] {'img','row'}, dimensions={0} | all-to-all | bytes 262144 | tf_op jit(solution)/shard_map/all_to_all | solution.py:25
  37.4 12.4 %all_to_all.71.refs_1_ = f32[32,16,128]{2,1,0:T(8,128)S(1)} all-to-all(f32[32,16,128]{2,1,0:T(8,128)S(1)} %get-tuple-element.159), channel_id=1, replica_groups=mesh['img'=16,'row'=2] {'img','row'}, dimensions={0} | all-to-all | bytes 524288 | tf_op jit(solution)/shard_map/all_to_all | solution.py:25
  49.8 4.9 %shard_map.291 = (bf16[384,1024]{1,0:T(8,128)(2,1)}, f32[384,1024]{1,0:T(8,128)}, f32[384,1024]{1,0:T(8,128)}, f32[8,1024]{1,0:T(8,128)}, bf16[96,1024]{1,0:T(8,...) custom-call(s32[1]{0:T(128)} %bitcast.refs_2_.refs_0_.refs_8_, ...), custom_call_target="tpu_custom_call" | custom-call | flops 402653184 | bytes 9674756 | tf_op jit(solution)/shard_map/pallas_call | solution.py:140
  58.6 6.9 %all-to-all-done.3.refs_1_ = f32[32,8,128]{2,1,0:T(8,128)S(1)} async-done(((f32[32,8,128]{2,1,0:T(8,128)}), f32[32,8,128]{2,1,0:T(8,128)S(1)}, u32[]{:S(2)}, u32[]{:S(2)}) %all-to-all-start.3) | async-done | bytes 131104 | tf_op jit(solution)/shard_map/all_to_all | solution.py:25
  65.5 4.7 %shard_map.292 = (f32[384,512]{1,0:T(8,128)}, f32[384,512]{1,0:T(8,128)}, f32[8,512]{1,0:T(8,128)}, f32[96,512]{1,0:T(8,128)S(1)}, f32[32,8,128]{2,1,0:T(8,128)}...) custom-call(s32[1]{0:T(128)} %bitcast.refs_2_.refs_0_.refs_8_, f32[32,8,128]{2,1,0:T(8,128)S(1)} %all-to-all-done.3.refs_1_, ...), custom_call_target="tpu_custom_call" | custom-call | flops 452984832 | bytes 9383940 | tf_op jit(solution)/shard_map/pallas_call | solution.py:140
  84.7 14.6 %all_to_all.72.refs_0_ = f32[16,40,128]{2,1,0:T(8,128)S(1)} all-to-all(f32[16,40,128]{2,1,0:T(8,128)S(1)} %shard_map.295), channel_id=1, replica_groups=mesh['img'=16,'row'=2] {'img'}, dimensions={0} | all-to-all | bytes 655360 | tf_op jit(solution)/shard_map/all_to_all | solution.py:29
  104.9 12.2 %all_to_all.73 = f32[16,24,128]{2,1,0:T(8,128)S(1)} all-to-all(f32[16,24,128]{2,1,0:T(8,128)S(1)} %broadcast_in_dim.4), channel_id=1, replica_groups=mesh['img'=16,'row'=2] {'img'}, dimensions={0} | all-to-all | bytes 393216 | tf_op jit(solution)/shard_map/all_to_all | solution.py:29
  126.8 6.2 %all-to-all-done.7.refs_0_ = f32[32,8,128]{2,1,0:T(8,128)S(1)} async-done(((f32[32,8,128]{2,1,0:T(8,128)}), f32[32,8,128]{2,1,0:T(8,128)S(1)}, u32[]{:S(2)}, u32[]{:S(2)}) %all-to-all-start.7) | async-done | bytes 131104 | tf_op jit(solution)/shard_map/all_to_all | solution.py:25
  132.9 4.9 %shard_map.299 = (f32[2,512]{1,0:T(2,128)}, bf16[96,512]{1,0:T(8,128)(2,1)}, f32[384,512]{1,0:T(8,128)S(1)}, f32[32,8,128]{2,1,0:T(8,128)}) custom-call(f32[32,8,128]{2,1,0:T(8,128)S(1)} %all-to-all-done.7.refs_0_, f32[32,8,128]{2,1,0:T(8,128)S(1)} %all-to-all-done.refs_1_.refs_2_.refs_3_, f32[96,512]{1,0:T(8,128)S(1)} %get-tuple-element.185.refs_2_, ...), custom_call_target="tpu_custom_call" | custom-call | flops 452984832 | bytes 8146944 | tf_op jit(solution)/shard_map/pallas_call | solution.py:140
  141.4 5.7 %shard_map.324 = (bf16[384,1024]{1,0:T(8,128)(2,1)}, bf16[384,1024]{1,0:T(8,128)(2,1)}, bf16[384,1024]{1,0:T(8,128)(2,1)}, bf16[384,1024]{1,0:T(8,128)(2,1)}) custom-call(s32[1]{0:T(128)} %bitcast.refs_2_.refs_0_.refs_8_, s32[2]{0:T(128)S(1)} %pad_add_fusion.1.refs_1_.refs_0_, bf16[96,1024]{1,0:T(8,128)(2,1)} %get-tuple-element.168.refs_0_.refs_2_, ...), custom_call_target="tpu_custom_call" | custom-call | flops 603979776 | bytes 5160972 | tf_op jit(solution)/shard_map/pallas_call | solution.py:140
  150.9 5.0 %shard_map.300.refs_8_ = f32[8,384,128]{2,1,0:T(8,128)} custom-call(bf16[96,2048]{1,0:T(8,128)(2,1)} %get-tuple-element.194.refs_0_.refs_6_, bf16[1024,2048]{1,0:T(8,128)(2,1)} %refs_1_.1), custom_call_target="tpu_custom_call" | custom-call | flops 402653184 | bytes 6160384 | tf_op jit(solution)/shard_map/pallas_call | solution.py:140
  155.8 5.6 %shard_map.301 = (f32[2,512]{1,0:T(2,128)}, bf16[384,512]{1,0:T(8,128)(2,1)}, f32[384,1024]{1,0:T(8,128)S(1)}, f32[32,16,128]{2,1,0:T(8,128)}, f32[384,1024]{1,0:T(8,128)}) custom-call(f32[32,8,128]{2,1,0:T(8,128)S(1)} %all-to-all-done.8.refs_0_, f32[32,8,128]{2,1,0:T(8,128)S(1)} %all-to-all-done.refs_1_.refs_2_.refs_3_, ...), custom_call_target="tpu_custom_call" | custom-call | flops 402653184 | bytes 11624448 | tf_op jit(solution)/shard_map/pallas_call | solution.py:140
  164.3 6.3 %shard_map.315 = (bf16[1408,256]{1,0:T(8,128)(2,1)}, bf16[1408,256]{1,0:T(8,128)(2,1)}, bf16[1408,256]{1,0:T(8,128)(2,1)}, bf16[1408,256]{1,0:T(8,128)(2,1)}) custom-call(s32[1]{0:T(128)} %bitcast.refs_2_.refs_0_.refs_8_, s32[2]{0:T(128)S(1)} %pad_add_fusion.1.refs_1_.refs_0_, bf16[3,96,1536]{2,1,0:T(8,128)(2,1)} %get-tuple-element.237.refs_2_, ...), custom_call_target="tpu_custom_call" | custom-call | flops 553648128 | bytes 6373388 | tf_op jit(solution)/shard_map/pallas_call | solution.py:140
  184.2 15.7 %collective-permute-done.49 = bf16[192,1024]{1,0:T(8,128)(2,1)S(1)} collective-permute-done((bf16[192,1024]{1,0:T(8,128)(2,1)}, bf16[192,1024]{1,0:T(8,128)(2,1)S(1)}, u32[]{:S(2)}, u32[]{:S(2)}) %collective-permute-start.49) | collective-permute-done | bytes 393248 | tf_op jit(solution)/shard_map/ppermute | solution.py:43
  234.9 7.6 %all-to-all-done.10.refs_0_ = f32[32,8,128]{2,1,0:T(8,128)S(1)} async-done(((f32[32,8,128]{2,1,0:T(8,128)}), f32[32,8,128]{2,1,0:T(8,128)S(1)}, u32[]{:S(2)}, u32[]{:S(2)}) %all-to-all-start.10) | async-done | bytes 131104 | tf_op jit(solution)/shard_map/all_to_all | solution.py:25
  258.2 4.4 %shard_map.306 = (bf16[896,128]{1,0:T(8,128)(2,1)}, bf16[896,128]{1,0:T(8,128)(2,1)}, bf16[896,128]{1,0:T(8,128)(2,1)}, bf16[896,128]{1,0:T(8,128)(2,1)}) custom-call(s32[1]{0:T(128)} %bitcast.refs_2_.refs_0_.refs_8_, s32[2]{0:T(128)S(1)} %pad_add_fusion.1.refs_1_.refs_0_, bf16[3,160,768]{2,1,0:T(8,128)(2,1)} %get-tuple-element.215.refs_2_, ...), custom_call_target="tpu_custom_call" | custom-call | flops 704643072 | bytes 4284428 | tf_op jit(solution)/shard_map/pallas_call | solution.py:140
  330.2 6.2 %all-to-all-start.13 = ((bf16[16,32,256]{2,1,0:T(8,128)(2,1)}), bf16[16,32,256]{2,1,0:T(8,128)(2,1)S(1)}, u32[]{:S(2)}, u32[]{:S(2)}) async-start(bf16[16,32,256]{2,1,0:T(8,128)(2,1)} %broadcast_in_dim.5), calls=%async_computation.13 | async-start | bytes 524288 | tf_op jit(solution)/shard_map/all_to_all | solution.py:1034
  352.7 24.3 %collective-permute-done.22.refs_3_ = bf16[448,128]{1,0:T(8,128)(2,1)S(1)} collective-permute-done((bf16[448,128]{1,0:T(8,128)(2,1)S(1)}, bf16[448,128]{1,0:T(8,128)(2,1)S(1)}, u32[]{:S(2)}, u32[]{:S(2)}) %collective-permute-start.22) | collective-permute-done | bytes 114720 | tf_op jit(solution)/shard_map/ppermute | solution.py:43
  377.7 5.0 %collective-permute-done.23.refs_4_ = bf16[448,128]{1,0:T(8,128)(2,1)S(1)} collective-permute-done((bf16[448,128]{1,0:T(8,128)(2,1)S(1)}, bf16[448,128]{1,0:T(8,128)(2,1)S(1)}, u32[]{:S(2)}, u32[]{:S(2)}) %collective-permute-start.23) | collective-permute-done | bytes 114720 | tf_op jit(solution)/shard_map/ppermute | solution.py:43
  386.1 6.0 %collective-permute-done.24.refs_3_ = bf16[896,128]{1,0:T(8,128)(2,1)S(1)} collective-permute-done((bf16[896,128]{1,0:T(8,128)(2,1)}, bf16[896,128]{1,0:T(8,128)(2,1)S(1)}, u32[]{:S(2)}, u32[]{:S(2)}) %collective-permute-start.24) | collective-permute-done | bytes 229408 | tf_op jit(solution)/shard_map/ppermute | solution.py:43
  404.1 5.5 %shard_map.332 = (f32[512,2048]{1,0:T(8,128)}, f32[256,2048]{1,0:T(8,128)}) custom-call(s32[2]{0:T(128)S(1)} %pad_add_fusion.1.refs_1_.refs_0_, bf16[384,1024]{1,0:T(8,128)(2,1)} %get-tuple-element.275.refs_1_, bf16[384,1024]{1,0:T(8,128)(2,1)} %get-tuple-element.276.refs_2_, bf16[384,1024]{1,0:T(8,128)(2,1)} %copy-done.26, bf16[384,1024]{1,0:T(8,128)(2,1)} %copy-done.27), custom_call_target="tpu_custom_call" | custom-call | bytes 9437192 | tf_op jit(solution)/shard_map/pallas_call | solution.py:140
  411.3 5.2 %shard_map.323 = (f32[9,256,512]{2,1,0:T(8,128)}, f32[512,512]{1,0:T(8,128)}) custom-call(s32[2]{0:T(128)S(1)} %pad_add_fusion.1.refs_1_.refs_0_, bf16[1408,256]{1,0:T(8,128)(2,1)} %get-tuple-element.255.refs_1_, bf16[1408,256]{1,0:T(8,128)(2,1)} %get-tuple-element.256.refs_2_, bf16[1408,256]{1,0:T(8,128)(2,1)} %copy-done.28, bf16[1408,256]{1,0:T(8,128)(2,1)} %copy-done.30), custom_call_target="tpu_custom_call" | custom-call | bytes 8650760 | tf_op jit(solution)/shard_map/pallas_call | solution.py:140
  (317 shorter events, 221.4 us)
Async XLA Ops:
  147.1 24.5 %collective-permute-start.46 = (bf16[384,1024]{1,0:T(8,128)(2,1)}, bf16[384,1024]{1,0:T(8,128)(2,1)}, u32[]{:S(2)}, u32[]{:S(2)}) collective-permute-start(bf16[384,1024]{1,0:T(8,128)(2,1)} %get-tuple-element.265), channel_id=1, source_target_pairs={{0,2},{2,0},{4,6},{6,4},{8,10},{10,8},{12,14},{14,12},{16,18},{18,... | collective-permute-start | bytes 2359304 | tf_op jit(solution)/shard_map/ppermute | solution.py:43
  148.8 22.8 %collective-permute-start.47 = (bf16[384,1024]{1,0:T(8,128)(2,1)}, bf16[384,1024]{1,0:T(8,128)(2,1)}, u32[]{:S(2)}, u32[]{:S(2)}) collective-permute-start(bf16[384,1024]{1,0:T(8,128)(2,1)} %get-tuple-element.266), channel_id=1, source_target_pairs={{0,4},{2,6},{4,0},{6,2},{8,12},{10,14},{12,8},{14,10},{16,20},{18,... | collective-permute-start | bytes 2359304 | tf_op jit(solution)/shard_map/ppermute | solution.py:43
  170.6 35.8 %collective-permute-start.30 = (bf16[1408,256]{1,0:T(8,128)(2,1)}, bf16[1408,256]{1,0:T(8,128)(2,1)S(1)}, u32[]{:S(2)}, u32[]{:S(2)}) collective-permute-start(bf16[1408,256]{1,0:T(8,128)(2,1)} %get-tuple-element.245), channel_id=1, source_target_pairs={{0,2},{2,0},{4,6},{6,4},{8,10},{10,8},{12,14},{14,12},{16,18},{18,... | collective-permute-start | bytes 2162696 | tf_op jit(solution)/shard_map/ppermute | solution.py:43
  171.2 35.2 %collective-permute-start.31 = (bf16[1408,256]{1,0:T(8,128)(2,1)}, bf16[1408,256]{1,0:T(8,128)(2,1)}, u32[]{:S(2)}, u32[]{:S(2)}) collective-permute-start(bf16[1408,256]{1,0:T(8,128)(2,1)} %get-tuple-element.246), channel_id=1, source_target_pairs={{0,4},{2,6},{4,0},{6,2},{8,12},{10,14},{12,8},{14,10},{16,20},{18,... | collective-permute-start | bytes 2162696 | tf_op jit(solution)/shard_map/ppermute | solution.py:43
  175.1 24.8 %collective-permute-start.49 = (bf16[192,1024]{1,0:T(8,128)(2,1)}, bf16[192,1024]{1,0:T(8,128)(2,1)S(1)}, u32[]{:S(2)}, u32[]{:S(2)}) collective-permute-start(bf16[192,1024]{1,0:T(8,128)(2,1)} %get-tuple-element.270), channel_id=1, source_target_pairs={{0,2},{2,0},{4,6},{6,4},{8,10},{10,8},{12,14},{14,12},{16,18},{18,... | collective-permute-start | bytes 1179656 | tf_op jit(solution)/shard_map/ppermute | solution.py:43
  176.8 23.7 %collective-permute-start.48 = (bf16[192,1024]{1,0:T(8,128)(2,1)}, bf16[192,1024]{1,0:T(8,128)(2,1)}, u32[]{:S(2)}, u32[]{:S(2)}) collective-permute-start(bf16[192,1024]{1,0:T(8,128)(2,1)} %get-tuple-element.269), channel_id=1, source_target_pairs={{0,4},{2,6},{4,0},{6,2},{8,12},{10,14},{12,8},{14,10},{16,20},{18,... | collective-permute-start | bytes 1179656 | tf_op jit(solution)/shard_map/ppermute | solution.py:43
  178.3 34.4 %all-to-all-start.9 = ((f32[32,16,128]{2,1,0:T(8,128)}), f32[32,16,128]{2,1,0:T(8,128)S(1)}, u32[]{:S(2)}, u32[]{:S(2)}) async-start(f32[32,16,128]{2,1,0:T(8,128)} %get-tuple-element.197), calls=%async_computation.9 | async-start | bytes 524288 | tf_op jit(solution)/shard_map/all_to_all | solution.py:25
  216.1 41.2 %collective-permute-start.13 = (bf16[384,1024]{1,0:T(8,128)(2,1)}, bf16[384,1024]{1,0:T(8,128)(2,1)S(1)}, u32[]{:S(2)}, u32[]{:S(2)}) collective-permute-start(bf16[384,1024]{1,0:T(8,128)(2,1)} %get-tuple-element.220.refs_8_), channel_id=1, source_target_pairs={{0,1},{1,0},{2,3},{3,2},{4,5},{5,4},{6,7},{7,6},{8,9},{9,8},{10,11... | collective-permute-start | bytes 2359304 | tf_op jit(solution)/shard_map/ppermute | solution.py:21
  224.9 21.3 %collective-permute-start.34 = (bf16[2,352,256]{2,1,0:T(8,128)(2,1)}, bf16[2,352,256]{2,1,0:T(8,128)(2,1)S(1)}, u32[]{:S(2)}, u32[]{:S(2)}) collective-permute-start(bf16[2,352,256]{2,1,0:T(8,128)(2,1)} %get-tuple-element.252), channel_id=1, source_target_pairs={{0,8},{2,10},{4,12},{6,14},{8,0},{10,2},{12,4},{14,6},{16,24},{18,... | collective-permute-start | bytes 1081352 | tf_op jit(solution)/shard_map/ppermute | solution.py:43
  231.8 23.9 %collective-permute-start.10 = (bf16[3,160,384]{2,1,0:T(8,128)(2,1)}, bf16[3,160,384]{2,1,0:T(8,128)(2,1)S(1)}, u32[]{:S(2)}, u32[]{:S(2)}) collective-permute-start(bf16[3,160,384]{2,1,0:T(8,128)(2,1)} %get-tuple-element.216), channel_id=1, source_target_pairs={{0,1},{1,0},{2,3},{3,2},{4,5},{5,4},{6,7},{7,6},{8,9},{9,8},{10,11... | collective-permute-start | bytes 1105928 | tf_op jit(solution)/shard_map/ppermute | solution.py:21
  234.9 36.4 %collective-permute-start.8 = (bf16[384,512]{1,0:T(8,128)(2,1)}, bf16[384,512]{1,0:T(8,128)(2,1)S(1)}, u32[]{:S(2)}, u32[]{:S(2)}) collective-permute-start(bf16[384,512]{1,0:T(8,128)(2,1)} %get-tuple-element.213), channel_id=1, source_target_pairs={{0,1},{1,0},{2,3},{3,2},{4,5},{5,4},{6,7},{7,6},{8,9},{9,8},{10,11... | collective-permute-start | bytes 1179656 | tf_op jit(solution)/shard_map/ppermute | solution.py:21
  255.7 35.7 %collective-permute-start.53 = (bf16[2,96,1024]{2,1,0:T(8,128)(2,1)}, bf16[2,96,1024]{2,1,0:T(8,128)(2,1)S(1)}, u32[]{:S(2)}, u32[]{:S(2)}) collective-permute-start(bf16[2,96,1024]{2,1,0:T(8,128)(2,1)} %shard_map.329.refs_1_), channel_id=1, source_target_pairs={{0,8},{2,10},{4,12},{6,14},{8,0},{10,2},{12,4},{14,6},{16,24},{18,... | collective-permute-start | bytes 1179656 | tf_op jit(solution)/shard_map/ppermute | solution.py:43
  275.2 54.2 %all-to-all-start.12 = ((bf16[16,32,256]{2,1,0:T(8,128)(2,1)}), bf16[16,32,256]{2,1,0:T(8,128)(2,1)S(1)}, u32[]{:S(2)}, u32[]{:S(2)}) async-start(bf16[16,32,256]{2,1,0:T(8,128)(2,1)} %bitcast.45), calls=%async_computation.12 | async-start | bytes 524288 | tf_op jit(solution)/shard_map/all_to_all | solution.py:1031
  282.3 19.9 %collective-permute-start.17 = (bf16[448,128]{1,0:T(8,128)(2,1)}, bf16[448,128]{1,0:T(8,128)(2,1)S(1)}, u32[]{:S(2)}, u32[]{:S(2)}) collective-permute-start(bf16[448,128]{1,0:T(8,128)(2,1)} %get-tuple-element.228), channel_id=1, source_target_pairs={{0,2},{2,0},{4,6},{6,4},{8,10},{10,8},{12,14},{14,12},{16,18},{18,... | collective-permute-start | bytes 344072 | tf_op jit(solution)/shard_map/ppermute | solution.py:43
  295.4 43.4 %collective-permute-start.54 = (bf16[192,1024]{1,0:T(8,128)(2,1)S(1)}, bf16[192,1024]{1,0:T(8,128)(2,1)S(1)}, u32[]{:S(2)}, u32[]{:S(2)}) collective-permute-start(bf16[192,1024]{1,0:T(8,128)(2,1)S(1)} %get-tuple-element.287.refs_1_), channel_id=1, source_target_pairs={{0,4},{2,6},{4,0},{6,2},{8,12},{10,14},{12,8},{14,10},{16,20},{18,... | collective-permute-start | bytes 1179656 | tf_op jit(solution)/shard_map/ppermute | solution.py:43
  296.0 42.8 %collective-permute-start.55 = (bf16[192,1024]{1,0:T(8,128)(2,1)S(1)}, bf16[192,1024]{1,0:T(8,128)(2,1)S(1)}, u32[]{:S(2)}, u32[]{:S(2)}) collective-permute-start(bf16[192,1024]{1,0:T(8,128)(2,1)S(1)} %get-tuple-element.286.refs_2_), channel_id=1, source_target_pairs={{0,2},{2,0},{4,6},{6,4},{8,10},{10,8},{12,14},{14,12},{16,18},{18,... | collective-permute-start | bytes 1179656 | tf_op jit(solution)/shard_map/ppermute | solution.py:43
  301.5 45.3 %collective-permute-start.38 = (bf16[704,256]{1,0:T(8,128)(2,1)S(1)}, bf16[704,256]{1,0:T(8,128)(2,1)}, u32[]{:S(2)}, u32[]{:S(2)}) collective-permute-start(bf16[704,256]{1,0:T(8,128)(2,1)S(1)} %get-tuple-element.289.refs_1_), channel_id=1, source_target_pairs={{0,4},{2,6},{4,0},{6,2},{8,12},{10,14},{12,8},{14,10},{16,20},{18,... | collective-permute-start | bytes 1081352 | tf_op jit(solution)/shard_map/ppermute | solution.py:43
  302.2 44.7 %collective-permute-start.39 = (bf16[704,256]{1,0:T(8,128)(2,1)S(1)}, bf16[704,256]{1,0:T(8,128)(2,1)}, u32[]{:S(2)}, u32[]{:S(2)}) collective-permute-start(bf16[704,256]{1,0:T(8,128)(2,1)S(1)} %get-tuple-element.288.refs_2_), channel_id=1, source_target_pairs={{0,2},{2,0},{4,6},{6,4},{8,10},{10,8},{12,14},{14,12},{16,18},{18,... | collective-permute-start | bytes 1081352 | tf_op jit(solution)/shard_map/ppermute | solution.py:43
  330.2 63.7 %all-to-all-start.13 = ((bf16[16,32,256]{2,1,0:T(8,128)(2,1)}), bf16[16,32,256]{2,1,0:T(8,128)(2,1)S(1)}, u32[]{:S(2)}, u32[]{:S(2)}) async-start(bf16[16,32,256]{2,1,0:T(8,128)(2,1)} %broadcast_in_dim.5), calls=%async_computation.13 | async-start | bytes 524288 | tf_op jit(solution)/shard_map/all_to_all | solution.py:1034
  343.4 58.9 %collective-permute-start.56 = (bf16[384,1024]{1,0:T(8,128)(2,1)}, bf16[384,1024]{1,0:T(8,128)(2,1)S(1)}, u32[]{:S(2)}, u32[]{:S(2)}) collective-permute-start(bf16[384,1024]{1,0:T(8,128)(2,1)} %get-tuple-element.275.refs_1_), channel_id=1, source_target_pairs={{0,2},{2,0},{4,6},{6,4},{8,10},{10,8},{12,14},{14,12},{16,18},{18,... | collective-permute-start | bytes 2359304 | tf_op jit(solution)/shard_map/ppermute | solution.py:43
  345.4 56.9 %collective-permute-start.57 = (bf16[384,1024]{1,0:T(8,128)(2,1)}, bf16[384,1024]{1,0:T(8,128)(2,1)S(1)}, u32[]{:S(2)}, u32[]{:S(2)}) collective-permute-start(bf16[384,1024]{1,0:T(8,128)(2,1)} %get-tuple-element.276.refs_2_), channel_id=1, source_target_pairs={{0,4},{2,6},{4,0},{6,2},{8,12},{10,14},{12,8},{14,10},{16,20},{18,... | collective-permute-start | bytes 2359304 | tf_op jit(solution)/shard_map/ppermute | solution.py:43
  349.9 59.7 %collective-permute-start.40 = (bf16[1408,256]{1,0:T(8,128)(2,1)}, bf16[1408,256]{1,0:T(8,128)(2,1)S(1)}, u32[]{:S(2)}, u32[]{:S(2)}) collective-permute-start(bf16[1408,256]{1,0:T(8,128)(2,1)} %get-tuple-element.255.refs_1_), channel_id=1, source_target_pairs={{0,2},{2,0},{4,6},{6,4},{8,10},{10,8},{12,14},{14,12},{16,18},{18,... | collective-permute-start | bytes 2162696 | tf_op jit(solution)/shard_map/ppermute | solution.py:43
  350.5 59.1 %collective-permute-start.41 = (bf16[1408,256]{1,0:T(8,128)(2,1)}, bf16[1408,256]{1,0:T(8,128)(2,1)S(1)}, u32[]{:S(2)}, u32[]{:S(2)}) collective-permute-start(bf16[1408,256]{1,0:T(8,128)(2,1)} %get-tuple-element.256.refs_2_), channel_id=1, source_target_pairs={{0,4},{2,6},{4,0},{6,2},{8,12},{10,14},{12,8},{14,10},{16,20},{18,... | collective-permute-start | bytes 2162696 | tf_op jit(solution)/shard_map/ppermute | solution.py:43
  350.7 26.3 %collective-permute-start.22 = (bf16[448,128]{1,0:T(8,128)(2,1)S(1)}, bf16[448,128]{1,0:T(8,128)(2,1)S(1)}, u32[]{:S(2)}, u32[]{:S(2)}) collective-permute-start(bf16[448,128]{1,0:T(8,128)(2,1)S(1)} %get-tuple-element.291.refs_1_), channel_id=1, source_target_pairs={{0,4},{2,6},{4,0},{6,2},{8,12},{10,14},{12,8},{14,10},{16,20},{18,... | collective-permute-start | bytes 344072 | tf_op jit(solution)/shard_map/ppermute | solution.py:43
  (112 other events, 946.5 us)

commit v2 on v1

--- a/solution.py
+++ b/solution.py
@@ -27,20 +27,6 @@
 
 def gather_img(message):
     return lax.all_to_all(message, "img", 0, 0, tiled=True)
-
-
-def orders():
-    bits = lax.axis_size("img").bit_length() - 1
-    ascending = list(range(bits))
-    swapped = ascending[:]
-    if bits > 1:
-        swapped[0], swapped[1] = 1, 0
-    return ascending, swapped
-
-
-def permute_bit(value, bit):
-    count = lax.axis_size("img")
-    return lax.ppermute(value, "img", [(i, i ^ (1 << bit)) for i in range(count)])
 
 
 class Late:
@@ -98,9 +84,11 @@
             result.send()
 
 
-def call(kernel, outs, *operands, scratch=(), smem=(), late=(), flops=0, keep=(), limit=24):
+def call(kernel, outs, *operands, scratch=(), smem=(), late=(), flops=0, keep=(), limit=24, after=(), free=False):
     late = [place for place in (range(len(operands)) if late is None else late) if place not in smem]
-    saved = [place for place in range(len(outs)) if place not in keep]
+    used = len(operands)
+    operands += tuple(after)
+    saved = [place for place in range(len(outs)) if place not in keep and not free]
     moved = sum(x.size * x.dtype.itemsize for x in operands) + sum(
         math.prod(shape) * jnp.dtype(dtype).itemsize for shape, dtype in outs
     )
@@ -108,10 +96,11 @@
     def place_of_operand(place):
         if place in smem:
             return pltpu.SMEM
-        return pl.ANY if place in late else pltpu.VMEM
+        return pl.ANY if place in late or place >= used else pltpu.VMEM
 
     operands = [
-        pltpu.with_memory_space_constraint(x, pltpu.HBM) if place in late else x for place, x in enumerate(operands)
+        pltpu.with_memory_space_constraint(x, pltpu.HBM) if place in late or place >= used else x
+        for place, x in enumerate(operands)
     ]
     buffers = [pltpu.VMEM(operands[place].shape, operands[place].dtype) for place in late]
     buffers += [pltpu.VMEM(*outs[place]) for place in saved]
@@ -129,7 +118,7 @@
         for number, place in enumerate(saved):
             number += len(late)
             results[place] = Saved(results[place], space[number], marks[number])
-        kernel(*inputs, *results, *own)
+        kernel(*inputs[:used], *results, *own)
         for place in late:
             inputs[place].ready()
         for place in saved:
@@ -140,11 +129,14 @@
     return pl.pallas_call(
         body,
         out_shape=[
-            (pltpu.VMEM if place in keep else pltpu.HBM)(shape, dtype) for place, (shape, dtype) in enumerate(outs)
+            jax.ShapeDtypeStruct(shape, dtype)
+            if free
+            else (pltpu.VMEM if place in keep else pltpu.HBM)(shape, dtype)
+            for place, (shape, dtype) in enumerate(outs)
         ],
         in_specs=[pl.BlockSpec(memory_space=place_of_operand(place)) for place in range(len(operands))],
         out_specs=[
-            pl.BlockSpec(memory_space=pltpu.VMEM if place in keep else pl.ANY) for place in range(len(outs))
+            pl.BlockSpec(memory_space=pl.ANY if place in saved else pltpu.VMEM) for place in range(len(outs))
         ],
         scratch_shapes=[pltpu.VMEM(shape, dtype) for shape, dtype in scratch] + buffers + semaphores,
         compiler_params=pltpu.CompilerParams(vmem_limit_bytes=limit * MIB),
@@ -289,26 +281,34 @@
     return jnp.where((row < extents[image, 0]) & (column < extents[image, 1]), 1.0, 0.0).astype(F32)
 
 
-def own_half(core, size):
-    return pl.ds(pl.multiple_of(core[0] * size, LANES), size)
-
-
-def other_half(core, size):
-    return pl.ds(pl.multiple_of((1 - core[0]) * size, LANES), size)
-
-
-def give_half(core, value, give):
-    give[...] = value[:, other_half(core, give.shape[1])]
+def core_number():
+    return lax.axis_index("row").astype(jnp.int32)
+
+
+def is_upper():
+    return jnp.where(core_number() == 0, 1.0, 0.0).astype(F32)
+
+
+def own_half(size):
+    return pl.ds(pl.multiple_of(core_number() * size, LANES), size)
+
+
+def other_half(size):
+    return pl.ds(pl.multiple_of((1 - core_number()) * size, LANES), size)
+
+
+def give_half(value, give):
+    give[...] = value[:, other_half(give.shape[1])]
     send(give)
 
 
 def entry_kernel(
-    dims, extents, flag, core, images, weight,
+    dims, extents, images, weight,
     entry_in, mask, small, above, below, small_below, raw, edge, message, give, rows,
 ):
     batch, height, width = dims
     pixels = height * width
-    upper = flag[0]
+    upper = is_upper()
     for b in range(batch):
         mask[b * pixels : (b + 1) * pixels, :] = valid(extents, b, 0, width, (pixels, LANES), 1)
         small[b * pixels // 4 : (b + 1) * pixels // 4, :] = valid(
@@ -324,7 +324,7 @@
         m = wide(mask[here, :], columns.stop - columns.start)
         entry_in[here, columns] = (images[here, columns].astype(F32) * m).astype(BF16)
     send(entry_in, mask, small, above, below, small_below)
-    give_half(core, entry_in, give)
+    give_half(entry_in, give)
     raw[...] = dot(entry_in[...], weight[...])
     for b in range(batch):
         first = raw[b * pixels : b * pixels + width, :]
@@ -368,7 +368,7 @@
 
 
 def middle_kernel(
-    dims, core, gathered, raw, halo, mask, above, below, params, weight,
+    dims, gathered, raw, halo, mask, above, below, params, weight,
     unit, slope, stats, out, message, triple, give, rows, padded,
 ):
     batch, height, width = dims
@@ -396,7 +396,7 @@
     send(unit, slope, stats)
     fill_triple(padded, triple, batch, height + 2, width)
     send(triple)
-    give_taps(core, triple, give)
+    give_taps(triple, give)
     total = None
     for tap in range(3):
         left = triple[:, tap * width : tap * width + pixels, :].reshape(batch * pixels, -1)
@@ -407,29 +407,29 @@
     spread_message(message, rows)
 
 
-def give_taps(core, taps, give):
+def give_taps(taps, give):
     full, half = taps.shape[2] // 3, give.shape[2] // 3
     for tap in range(3):
-        start = pl.multiple_of(tap * full + (1 - core[0]) * half, LANES)
+        start = pl.multiple_of(tap * full + (1 - core_number()) * half, LANES)
         give[:, :, tap * half : (tap + 1) * half] = taps[:, :, pl.ds(start, half)]
     send(give)
 
 
 def closing_kernel(
-    core, gathered, counts, raw, mask, params, weight, act, unit, slope, stats, out, message, give, rows
+    gathered, counts, raw, mask, params, weight, act, unit, slope, stats, out, message, give, rows
 ):
     blocks = raw.shape[1] // LANES
     join_stats(gathered, counts, 4, stats, blocks)
     act_pass(raw, mask, stats, params, unit, slope, act)
     send(unit, slope, act, stats)
-    give_half(core, act, give)
+    give_half(act, give)
     out[...] = dot(act[...], weight[...])
     local_stats(out, mask, rows)
     spread_message(message, rows)
 
 
 def widen_kernel(
-    dims, core, gathered, counts, raw, entry_in, mask, params, weight,
+    dims, gathered, counts, raw, entry_in, mask, params, weight,
     act, unit, slope, stats, short, out, edge, message, give, give_short, rows, even,
 ):
     batch, height, width = dims
@@ -442,7 +442,7 @@
 
     act_pass(raw, mask, stats, params, unit, slope, act, skip=entry_in, keep=keep)
     send(unit, slope, act, stats)
-    give_half(core, act, give)
+    give_half(act, give)
     out[...] = dot(act[...], weight[...])
     for b in range(batch):
         edge[b * width : (b + 1) * width, :] = out[(b + 1) * pixels - width : (b + 1) * pixels, :]
@@ -456,7 +456,7 @@
                 lines.append(even[c // LANES, pl.ds(b * pixels + 2 * i * width, width // 2, stride=2), :])
         short[:, columns] = jnp.concatenate(lines, axis=0).astype(BF16)
     send(short)
-    give_half(core, short, give_short)
+    give_half(short, give_short)
 
 
 def shortcut_kernel(short, small, weight, out, rows):
@@ -466,7 +466,7 @@
 
 
 def strided_kernel(
-    dims, core, gathered, counts, raw, halo, mask, small, above, params, weight,
+    dims, gathered, counts, raw, halo, mask, small, above, params, weight,
     unit, slope, stats, out, message, taps, give, rows, padded,
 ):
     batch, height, width = dims
@@ -510,7 +510,7 @@
                         jnp.concatenate(pieces, axis=0).astype(BF16)
                     )
     send(taps)
-    give_taps(core, taps, give)
+    give_taps(taps, give)
     total = None
     for tap in range(3):
         part = dot(taps[tap], weight[tap])
@@ -521,17 +521,17 @@
 
 
 def expand_kernel(
-    gathered, counts, raw, small, params, weight, short_rows, flag, core,
+    gathered, counts, raw, small, params, weight, short_rows,
     act, unit, slope, stats, out, mine, theirs, give, rows,
 ):
     blocks = raw.shape[1] // LANES
     join_stats(gathered, counts, 5, stats, blocks)
     act_pass(raw, small, stats, params, unit, slope, act)
     send(unit, slope, act, stats)
-    give_half(core, act, give)
+    give_half(act, give)
     out[...] = dot(act[...], weight[...])
     local_stats(out, small, rows)
-    upper = flag[0]
+    upper = is_upper()
     size = rows.shape[0]
     number = jnp.broadcast_to(column_sum(small[...]), (8, LANES))
     mine[:size, :] = rows[...] * upper + short_rows[...] * (1.0 - upper)
@@ -563,10 +563,10 @@
 
 
 def final_kernel(
-    own, other, flag, expand_raw, short_raw, small, expand_params, short_params, cotangent,
+    own, other, expand_raw, short_raw, small, expand_params, short_params, cotangent,
     features, grad, expand_unit, short_unit, expand_stats, short_stats, mine, theirs, rows,
 ):
-    upper = flag[0]
+    upper = is_upper()
     expand_stats[...] = own[...] * upper + other[...] * (1.0 - upper)
     short_stats[...] = own[...] * (1.0 - upper) + other[...] * upper
     height, width = expand_raw.shape
@@ -593,11 +593,11 @@
 
 
 def last_grads_kernel(
-    batch, own, other, flag, counts, grad, expand_unit, short_unit, expand_stats, short_stats,
+    batch, own, other, counts, grad, expand_unit, short_unit, expand_stats, short_stats,
     expand_params, short_params, small, weight, slope, unit,
     expand_affine, short_affine, expand_grad, short_grad, back, edge, message, rows,
 ):
-    upper = flag[0]
+    upper = is_upper()
     half = own.shape[0] // 3
     for stat in range(3):
         part = slice(stat * half, (stat + 1) * half)
@@ -730,12 +730,12 @@
 
 
 def middle_back_kernel(
-    dims, flag, gathered, counts, back, unit, mask, stats, params, weight, out_unit, out_slope,
+    dims, gathered, counts, back, unit, mask, stats, params, weight, out_unit, out_slope,
     affine, grad, out, edge, message, rows,
 ):
     batch, height, width = dims
     pixels = height * width
-    upper = flag[0]
+    upper = is_upper()
     join_sums(gathered, affine)
     grad_pass(back, unit, mask, affine, stats, params, total_count(counts, 4), grad)
     send(grad, affine)
@@ -807,231 +807,271 @@
     return lax.dot_general(left, grad, (((0,), (0,)), ((), ())), preferred_element_type=F32)
 
 
-def chip_grad(core, left, left_other, grad, grad_other, columns=slice(None)):
+def chip_grad(left, left_other, grad, grad_other, columns=slice(None)):
     half = left_other.shape[1]
-    return dot_pixels(left[:, own_half(core, half)], grad[:, columns]) + dot_pixels(
+    return dot_pixels(left[:, own_half(half)], grad[:, columns]) + dot_pixels(
         left_other[...], grad_other[:, columns]
     )
 
 
-def deal(place, full, kept, sent):
-    groups = len(kept)
-    rows, width = full.shape[0] // 2, full.shape[1] // groups
-    for group in range(groups):
-        columns = slice(group * width, (group + 1) * width)
-        mine = place[group]
-        sent[group][...] = full[pl.ds(pl.multiple_of((1 - mine) * rows, 16), rows), columns]
-        send(sent[group])
-        kept[group][...] = full[pl.ds(pl.multiple_of(mine * rows, 16), rows), columns]
-        send(kept[group])
+def bit_half(bit, flip, rows):
+    mine = (lax.axis_index("img").astype(jnp.int32) >> bit) & 1
+    return pl.ds(pl.multiple_of((1 - mine if flip else mine) * rows, 16), rows)
+
+
+def round_part(low, bits, flip, rows):
+    mine = (lax.axis_index("img").astype(jnp.int32) >> low) & ((1 << bits) - 1)
+    return pl.ds(pl.multiple_of((mine ^ flip) * rows, 16), rows)
+
+
+def deal(full, parts):
+    rows, width = parts[0].shape
+    for outs, flip in ((parts[2:], True), (parts[:2], False)):
+        for group, out in enumerate(outs):
+            out[...] = full[bit_half((0, 1)[group], flip, rows), group * width : (group + 1) * width]
 
 
 def first_wave_kernel(
-    core, place, short, short_other, strided, strided_other,
-    short_grad, short_grad_other, expand_grad, expand_grad_other,
-    kept_a, kept_b, sent_a, sent_b, full,
+    short, short_other, strided, strided_other,
+    short_grad, short_grad_other, expand_grad, expand_grad_other, full
 ):
     rows = short_other.shape[1]
     step = 512
     for start in range(0, full.shape[1], step):
         columns = slice(start, start + step)
         full[:rows, columns] = chip_grad(
-            core, short, short_other, short_grad, short_grad_other, columns
+            short, short_other, short_grad, short_grad_other, columns
         ).astype(BF16)
         full[rows:, columns] = chip_grad(
-            core, strided, strided_other, expand_grad, expand_grad_other, columns
+            strided, strided_other, expand_grad, expand_grad_other, columns
         ).astype(BF16)
-    deal(place, full, (kept_a, kept_b), (sent_a, sent_b))
 
 
 def second_wave_kernel(
-    core, place, taps, taps_other, strided_grad, strided_grad_other, block, block_other, widen_grad, widen_grad_other,
-    kept_a, kept_b, sent_a, sent_b, full,
+    taps, taps_other, strided_grad, strided_grad_other, *results
 ):
+    *parts, full = results
     half = taps_other.shape[2] // 3
     channels = 2 * half
     for row_tap in range(3):
         for col_tap in range(3):
-            start = pl.multiple_of(col_tap * channels + core[0] * half, LANES)
+            start = pl.multiple_of(col_tap * channels + core_number() * half, LANES)
             own = dot_pixels(taps[row_tap, :, pl.ds(start, half)], strided_grad[...])
             other = dot_pixels(
                 taps_other[row_tap, :, col_tap * half : (col_tap + 1) * half], strided_grad_other[...]
             )
             place_row = (3 * row_tap + col_tap) * half
             full[place_row : place_row + half, :] = (own + other).astype(BF16)
-    full[9 * half :, :] = chip_grad(core, block, block_other, widen_grad, widen_grad_other).astype(BF16)
-    deal(place, full, (kept_a, kept_b), (sent_a, sent_b))
+    deal(full, parts)
+
+
+def fill_rest(full, row):
+    if row < full.shape[0]:
+        full[row:, :] = jnp.zeros((full.shape[0] - row, full.shape[1]), full.dtype)
 
 
 def third_wave_kernel(
-    dims, core, place, triple, triple_other, middle_grad, middle_grad_other, act, act_other, closing_grad, closing_grad_other,
-    kept_a, kept_b, sent_a, sent_b, full,
+    dims, block, block_other, widen_grad, widen_grad_other, act, act_other, closing_grad,
+    closing_grad_other, triple, triple_other, middle_grad, middle_grad_other, entry_in, entry_in_other, entry_grad,
+    entry_grad_other, *results,
 ):
+    *parts, full = results
     batch, height, width = dims
     pixels = height * width
+    step = full.shape[1]
+    row = 0
+    for left, left_other, grad, grad_other in (
+        (block, block_other, widen_grad, widen_grad_other),
+        (act, act_other, closing_grad, closing_grad_other),
+    ):
+        rows = left_other.shape[1]
+        for start in range(0, grad.shape[1], step):
+            full[row : row + rows, :] = chip_grad(
+                left, left_other, grad, grad_other, slice(start, start + step)
+            ).astype(BF16)
+            row += rows
     half = triple_other.shape[2] // 3
     channels = 2 * half
     for row_tap in range(3):
         lines = slice(row_tap * width, row_tap * width + pixels)
         for col_tap in range(3):
-            start = pl.multiple_of(col_tap * channels + core[0] * half, LANES)
+            start = pl.multiple_of(col_tap * channels + core_number() * half, LANES)
             own = triple[:, lines, pl.ds(start, half)].reshape(batch * pixels, half)
             other = triple_other[:, lines, col_tap * half : (col_tap + 1) * half].reshape(batch * pixels, half)
             value = dot_pixels(own, middle_grad[...]) + dot_pixels(other, middle_grad_other[...])
-            place_row = (3 * row_tap + col_tap) * half
-            full[place_row : place_row + half, :] = value.astype(BF16)
-    step = full.shape[1]
-    for block in range(closing_grad.shape[1] // step):
-        columns = slice(block * step, (block + 1) * step)
-        start = (9 + block) * half
-        full[start : start + half, :] = chip_grad(
-            core, act, act_other, closing_grad, closing_grad_other, columns
-        ).astype(BF16)
-    used = (9 + closing_grad.shape[1] // step) * half
-    if used < full.shape[0]:
-        full[used:, :] = jnp.zeros((full.shape[0] - used, step), BF16)
-    deal(place, full, (kept_a, kept_b), (sent_a, sent_b))
-
-
-def last_wave_kernel(core, entry_in, entry_in_other, grad, grad_other, out):
-    out[...] = chip_grad(core, entry_in, entry_in_other, grad, grad_other).astype(BF16)
-
-
-def add_halves(first, second):
-    return (first.astype(F32) + second.astype(F32)).astype(BF16)
-
-
-def fold_kernel(groups, place, *refs):
-    kept, got, keep, pass_on = (refs[i * groups : (i + 1) * groups] for i in range(4))
-    for group in range(groups):
-        rows = keep[group].shape[-2]
-        for mine, out in ((1 - place[group], pass_on[group]), (place[group], keep[group])):
-            here = pl.ds(pl.multiple_of(mine * rows, 16), rows)
-            if kept[group].ndim == 3:
-                out[...] = add_halves(kept[group][:, here, :], got[group][:, here, :])
-            else:
-                out[...] = add_halves(kept[group][here, :], got[group][here, :])
-            send(out)
-
-
-def add_kernel(kept, got, out):
-    out[...] = add_halves(kept[...], got[...])
-
-
-def merge_kernel(groups, place, *refs):
-    own, got, out = (refs[i * groups : (i + 1) * groups] for i in range(3))
-    for group in range(groups):
-        rows = own[group].shape[-2]
-        for mine, value in ((place[group], own[group]), (1 - place[group], got[group])):
-            here = pl.ds(pl.multiple_of(mine * rows, 16), rows)
-            if own[group].ndim == 3:
-                out[group][:, here, :] = value[...]
-            else:
-                out[group][here, :] = value[...]
-
-
-def fill(place, own, got, full):
-    width = full.shape[1] // len(own)
-    for group in range(len(own)):
-        columns = slice(group * width, (group + 1) * width)
-        rows = own[group].shape[0]
-        for mine, value in ((place[group], own[group]), (1 - place[group], got[group])):
-            full[pl.ds(pl.multiple_of(mine * rows, 16), rows), columns] = value[...]
-
-
-def first_out_kernel(place, own_a, own_b, got_a, got_b, short, expand, full):
-    fill(place, (own_a, own_b), (got_a, got_b), full)
+            full[row : row + half, :] = value.astype(BF16)
+            row += half
+    rows = entry_in_other.shape[1]
+    full[row : row + rows, :] = chip_grad(entry_in, entry_in_other, entry_grad, entry_grad_other).astype(BF16)
+    fill_rest(full, row + rows)
+    deal(full, parts)
+
+
+def added(parts, *index):
+    total = parts[0][index].astype(F32)
+    for part in parts[1:]:
+        total = total + part[index].astype(F32)
+    return total.astype(BF16)
+
+
+def halve_kernel(kept_a, kept_b, got_a, got_b, *outs):
+    rows = outs[0].shape[0]
+    for targets, flip in ((outs[2:], True), (outs[:2], False)):
+        for group, (out, parts) in enumerate(zip(targets, ((kept_a, got_a), (kept_b, got_b)))):
+            out[...] = added(parts, bit_half((1, 0)[group], flip, rows), slice(None))
+
+
+def part_order(count):
+    return list(range(1, count)) + [0]
+
+
+def quarter_kernel(step, kept_a, kept_b, got_a, got_b, *outs):
+    rows = outs[0].shape[1]
+    for flip in part_order(len(outs)):
+        here = round_part(*step, flip, rows)
+        for group, parts in enumerate(((kept_a, got_a), (kept_b, got_b))):
+            outs[flip][group] = added(parts, here, slice(None))
+
+
+def fold_kernel(count, step, *refs):
+    parts, outs = refs[:count], refs[count:]
+    rows = outs[0].shape[1]
+    for flip in part_order(len(outs)):
+        outs[flip][...] = added(parts, slice(None), round_part(*step, flip, rows), slice(None))
+
+
+def add_kernel(*refs):
+    *parts, out = refs
+    out[...] = added(parts, slice(None))
+
+
+def merge_kernel(count, step, *refs):
+    parts, outs = refs[:count], refs[count:]
+    rows = parts[0].shape[1]
+    for flip, part in enumerate(parts):
+        here = round_part(*step, flip, rows)
+        if len(outs) == 1:
+            outs[0][:, here, :] = part[...]
+        else:
+            for group, out in enumerate(outs):
+                out[here, :] = part[group]
+
+
+def double_kernel(own_a, own_b, got_a, got_b, *outs):
+    rows = own_a.shape[0]
+    for group, (out, own, got) in enumerate(zip(outs, (own_a, own_b), (got_a, got_b))):
+        out[bit_half((1, 0)[group], False, rows), :] = own[...]
+        out[bit_half((1, 0)[group], True, rows), :] = got[...]
+
+
+def first_out(full, short, expand):
     rows = short.shape[0]
     short[...] = full[:rows, :].astype(F32)
     send(short)
     expand[...] = full[rows:, :].astype(F32)
 
 
-def second_out_kernel(place, own_a, own_b, got_a, got_b, strided, widen, full):
-    fill(place, (own_a, own_b), (got_a, got_b), full)
+def second_out(full, strided):
     rows = strided.shape[1]
     for tap in range(9):
         strided[tap] = full[tap * rows : (tap + 1) * rows, :].astype(F32)
-    send(strided)
-    widen[...] = full[9 * rows :, :].astype(F32)
-
-
-def third_out_kernel(place, own_a, own_b, got_a, got_b, middle, closing, full):
-    fill(place, (own_a, own_b), (got_a, got_b), full)
+
+
+def third_out(full, widen, closing, middle, entry):
+    step = full.shape[1]
+    row = 0
+    for out in (widen, closing):
+        rows = out.shape[0]
+        for start in range(0, out.shape[1], step):
+            out[:, start : start + step] = full[row : row + rows, :].astype(F32)
+            row += rows
+        send(out)
     rows = middle.shape[1]
     for tap in range(9):
-        middle[tap] = full[tap * rows : (tap + 1) * rows, :].astype(F32)
-    step = full.shape[1]
-    for block in range(closing.shape[1] // step):
-        start = (9 + block) * rows
-        closing[:, block * step : (block + 1) * step] = full[start : start + rows, :].astype(F32)
-
-
-def place_of(bits):
-    here = lax.axis_index("img")
-    return jnp.stack([(here >> bit) & 1 for bit in bits]).astype(jnp.int32)
-
-
-def stack_pair(pair):
-    return [jnp.stack(pair)]
-
-
-def sum_over_chips(kept, sent, out_kernel, outs, full):
-    steps = list(zip(*orders()))
-    halvings = 1
-    while halvings < len(steps) and kept[0].shape[0] % (16 << halvings) == 0:
-        halvings += 1
-    merged = False
-    for number, bits in enumerate(steps):
-        got = [permute_bit(value, bit) for value, bit in zip(sent, bits)]
+        middle[tap] = full[row : row + rows, :].astype(F32)
+        row += rows
+    send(middle)
+    entry[...] = full[row : row + entry.shape[0], :].astype(F32)
+
+
+def out_kernel(finish, own_a, own_b, got_a, got_b, *refs):
+    outs, full = refs[:-1], refs[-1]
+    rows, width = own_a.shape
+    for group, (own, got) in enumerate(((own_a, got_a), (own_b, got_b))):
+        columns = slice(group * width, (group + 1) * width)
+        full[bit_half((0, 1)[group], False, rows), columns] = own[...]
+        full[bit_half((0, 1)[group], True, rows), columns] = got[...]
+    finish(full, *outs)
+
+
+def rounds():
+    bits = lax.axis_size("img").bit_length() - 1
+    return [(low, min(2, bits - low)) for low in range(2, bits, 2)]
+
+
+def to_chip(value, flip):
+    count = lax.axis_size("img")
+    return lax.ppermute(value, "img", [(i, i ^ flip) for i in range(count)])
+
+
+def sum_over_chips(order, parts, finish, outs, shape):
+    steps = rounds()
+
+    def run(kernel, shapes, *operands, scratch=(), free=True):
+        results = call(kernel, shapes, *operands, free=free, after=(order[0],), scratch=scratch)
+        order[0] = results[0]
+        return results
+
+    def exchange(values, low):
+        return [to_chip(value, number << low) for number, value in enumerate(values, 1)]
+
+    rows, width = shape[0] // 2, shape[1] // 2
+    kept, sent = parts[:2], parts[2:]
+    got = [to_chip(sent[0], 1), to_chip(sent[1], 2)]
+    yield None
+    rows //= 2
+    results = run(halve_kernel, [((rows, width), BF16)] * 4, *kept, *got)
+    kept, sent = results[:2], results[2:]
+    got = [to_chip(sent[0], 2), to_chip(sent[1], 1)]
+    yield None
+    low, bits = steps[0]
+    rows >>= bits
+    parts = run(functools.partial(quarter_kernel, steps[0]), [((2, rows, width), BF16)] * (1 << bits), *kept, *got)
+    dealt = 1
+    for number, (low, bits) in enumerate(steps):
+        if number < dealt:
+            got = exchange(parts[1:], low)
+        else:
+            got = exchange([parts[0]] * ((1 << bits) - 1), low)
+        yield None
+        parts = [parts[0]] + got
         following = steps[number + 1] if number + 1 < len(steps) else None
-        if following is not None and following[0] == following[1] and not merged:
-            kept, got, merged = stack_pair(kept), stack_pair(got), True
-        groups = len(kept)
-        if number + 1 >= halvings:
-            kept = sent = [
-                call(add_kernel, [(one.shape, BF16)], one, other, late=None)[0] for one, other in zip(kept, got)
-            ]
-            continue
-        shapes = [value.shape[:-2] + (value.shape[-2] // 2, value.shape[-1]) for value in kept]
-        results = call(
-            functools.partial(fold_kernel, groups),
-            [(shape, BF16) for shape in shapes] * 2,
-            place_of(following[:groups]),
-            *kept,
-            *got,
-            smem=(0,),
-            late=None,
-        )
-        kept, sent = results[:groups], results[groups:]
-    own = kept
-    for number, bits in reversed(list(enumerate(steps[:halvings]))):
-        if bits[0] != bits[1] and merged:
-            own, merged = [own[0][0], own[0][1]], False
-        got = [permute_bit(value, bit) for value, bit in zip(own, bits)]
-        groups = len(own)
-        if number == 0:
-            return call(
-                out_kernel, outs, place_of(bits), *own, *got, smem=(0,), scratch=[(full, BF16)], late=None
+        if following is not None and number + 1 == dealt and rows % (16 << following[1]) == 0:
+            rows >>= following[1]
+            dealt += 1
+            parts = run(
+                functools.partial(fold_kernel, len(parts), following),
+                [((2, rows, width), BF16)] * (1 << following[1]),
+                *parts,
             )
-        shapes = [value.shape[:-2] + (value.shape[-2] * 2, value.shape[-1]) for value in own]
-        own = call(
-            functools.partial(merge_kernel, groups),
-            [(shape, BF16) for shape in shapes],
-            place_of(bits[:groups]),
-            *own,
-            *got,
-            smem=(0,),
-            late=None,
-        )
-
-
-def sum_over_chips_short(parts):
-    members = lax.axis_size("img")
-    moved = lax.all_to_all(parts, "img", 0, 0, tiled=True)
-    share = jnp.sum(moved.astype(F32), axis=0).astype(BF16)
-    spread = jnp.broadcast_to(share[None], (members,) + share.shape)
-    return lax.all_to_all(spread, "img", 0, 0, tiled=True).reshape(-1, parts.shape[-1])
+        else:
+            parts = run(add_kernel, [((2, rows, width), BF16)], *parts)
+    (share,) = parts
+    for number in reversed(range(dealt)):
+        low, bits = steps[number]
+        got = exchange([share] * ((1 << bits) - 1), low)
+        yield None
+        rows <<= bits
+        shapes = [((2, rows, width), BF16)] if number > 0 else [((rows, width), BF16)] * 2
+        own = run(functools.partial(merge_kernel, 1 + len(got), steps[number]), shapes, share, *got)
+        share = own[0]
+    got = [to_chip(own[0], 2), to_chip(own[1], 1)]
+    yield None
+    rows *= 2
+    own = run(double_kernel, [((rows, width), BF16)] * 2, *own, *got)
+    got = [to_chip(own[0], 1), to_chip(own[1], 2)]
+    yield None
+    yield run(functools.partial(out_kernel, finish), outs, *own, *got, scratch=[(shape, BF16)], free=False)
 
 
 def per_device(
@@ -1060,9 +1100,6 @@
     chips = lax.axis_size("img")
     devices = chips * lax.axis_size("row")
     row = lax.axis_index("row")
-    upper = row == 0
-    flag = jnp.where(upper, 1.0, 0.0).astype(F32).reshape(1)
-    core = row.astype(jnp.int32).reshape(1)
     local = extents - jnp.stack([row * height, 0]).astype(jnp.int32)
     mid, wider, last = entry_weight.shape[1], widen_weight.shape[1], expand_weight.shape[1]
 
@@ -1102,13 +1139,11 @@
             ((pixels, wide_in // 2), BF16),
         ],
         local,
-        flag,
-        core,
         images.reshape(pixels, wide_in),
         entry_weight,
         scratch=[rows(mid)],
-        smem=(0, 1, 2),
-        late=(3, 4),
+        smem=(0,),
+        late=(1, 2,),
         keep=(6, 7, 8),
         flops=ops(pixels, wide_in, mid),
     )
@@ -1125,7 +1160,6 @@
             ((batch, (height + 2) * width, 3 * mid), BF16),
             ((batch, (height + 2) * width, 3 * mid // 2), BF16),
         ],
-        core,
         counts,
         entry_raw,
         halo,
@@ -1135,8 +1169,8 @@
         entry_affine,
         middle_weight.reshape(3, 3 * mid, mid),
         scratch=[rows(mid), ((padded_rows + 16, mid), F32)],
-        smem=(0,),
-        late=(8,),
+
+        late=(7,),
         keep=(3, 4),
         flops=ops(pixels, 9, mid, mid),
     )
@@ -1145,7 +1179,6 @@
     middle_act, middle_unit, middle_slope, middle_stats, closing_raw, sent, give = call(
         closing_kernel,
         level(pixels, mid) + [((pixels, wide_in), F32), message(wide_in), ((pixels, mid // 2), BF16)],
-        core,
         gathered,
         counts,
         middle_raw,
@@ -1153,8 +1186,8 @@
         middle_affine,
         closing_weight,
         scratch=[rows(wide_in)],
-        smem=(0,),
-        late=(6,),
+
+        late=(5,),
         keep=(4, 5),
         flops=ops(pixels, mid, wide_in),
     )
@@ -1171,7 +1204,6 @@
             ((pixels, wide_in // 2), BF16),
             ((small_pixels, wide_in // 2), BF16),
         ],
-        core,
         gathered,
         counts,
         closing_raw,
@@ -1180,8 +1212,8 @@
         closing_affine,
         widen_weight,
         scratch=[rows(wider), ((wide_in // LANES, pixels, LANES), F32)],
-        smem=(0,),
-        late=(4, 7),
+
+        late=(3, 6,),
         keep=(5, 6, 7),
         flops=ops(pixels, wide_in, wider),
     )
@@ -1207,7 +1239,6 @@
             ((3, small_pixels, 3 * wider), BF16),
             ((3, small_pixels, 3 * wider // 2), BF16),
         ],
-        core,
         gathered,
         counts,
         widen_raw,
@@ -1218,8 +1249,8 @@
         widen_affine,
         strided_weight.reshape(3, 3 * wider, wider),
         scratch=[rows(wider), ((wider // LANES, batch * (height + 1) * width + 16, LANES), F32)],
-        smem=(0,),
-        late=(9,),
+
+        late=(8,),
         keep=(3, 4),
         flops=ops(small_pixels, 9, wider, wider),
     )
@@ -1242,11 +1273,9 @@
         strided_affine,
         expand_weight,
         shortcut_rows,
-        flag,
-        core,
         scratch=[rows(last)],
-        smem=(7, 8),
-        late=(5, 6),
+
+        late=(5, 6,),
         keep=(4, 5, 6),
         flops=ops(small_pixels, wider, last),
     )
@@ -1268,17 +1297,16 @@
         ],
         own_stats,
         swap_rows(own_stats),
-        flag,
         expand_raw,
         shortcut_raw,
         small,
         expand_affine,
         shortcut_affine,
         cotangent.reshape(small_pixels, last),
-        late=(4, 8),
+        late=(3, 7,),
         keep=(1, 2, 3, 4, 5, 6, 7),
         scratch=[((3 * last // LANES, LANES), F32)],
-        smem=(2,),
+
     )
 
     joined = mine + swap_rows(theirs)
@@ -1296,7 +1324,6 @@
         ],
         own_sums,
         swap_rows(own_sums),
-        flag,
         counts,
         final_grad,
         expand_unit,
@@ -1310,8 +1337,8 @@
         strided_slope,
         strided_unit,
         scratch=[rows(wider)],
-        smem=(2,),
-        late=(12, 13, 14),
+
+        late=(11, 12, 13,),
         keep=(4, 5, 6),
         flops=ops(small_pixels, wider, last),
     )
@@ -1324,36 +1351,37 @@
     def image(value):
         return value.reshape(batch, height, width, value.shape[-1])
 
-    (short_back,) = call(
-        functools.partial(short_back_kernel, dims),
-        [((wide_in // LANES, pixels, LANES), F32)],
-        shortcut_grad,
-        shortcut_weight,
-        late=(0, 1),
-        keep=(),
-        flops=ops(small_pixels, wide_in, last),
-    )
-    two = place_of([bits[0] for bits in orders()])
-
-    def wave(kernel, shape, *operands, flops):
-        half = (shape[0] // 2, shape[1] // 2)
-        results = call(
+    order = [affine_expand]
+
+    def move(wave, times=1):
+        for _ in range(times):
+            result = next(wave)
+        return result
+
+
+    def wave_parts(kernel, shape, *operands, flops):
+        parts = call(
             kernel,
-            [(half, BF16)] * 4,
-            core,
-            two,
+            [((shape[0] // 2, shape[1] // 2), BF16)] * 4,
             *operands,
             scratch=[(shape, BF16)],
-            smem=(0, 1),
             flops=flops,
             late=None,
+            free=True,
+            after=(order[0],),
         )
-        return results[:2], results[2:]
+        order[0] = parts[0]
+        return parts
+
+    def moving_sum(parts, shape, finish, outs):
+        moving = sum_over_chips(order, parts, finish, outs, shape)
+        move(moving)
+        return moving
 
     first_shape = ((wide_in + wider) // 2, last)
-    kept, sent_on = wave(
+    (first,) = call(
         first_wave_kernel,
-        first_shape,
+        [(first_shape, BF16)],
         shortcut_in,
         short_other,
         strided_act,
@@ -1362,11 +1390,13 @@
         swap_rows(shortcut_grad),
         expand_grad,
         swap_rows(expand_grad),
+
         flops=ops(2 * small_pixels, *first_shape),
-    )
-    shortcut_total, expand_total = sum_over_chips(
-        kept, sent_on, first_out_kernel, [((wide_in // 2, last), F32), ((wider // 2, last), F32)], first_shape
-    )
+        late=None,
+        after=(order[0],),
+    )
+    order[0] = first
+    first = lax.psum(first, "img")
 
     affine_strided, strided_grad, widen_back, sent = call(
         functools.partial(widen_back_kernel, dims),
@@ -1390,9 +1420,23 @@
         ],
         late=(3, 9, 10, 11),
         keep=(2, 3),
+        after=(order[0],),
         flops=ops(small_pixels, 9, wider, wider),
     )
     gathered = gather_all(sent)
+    order[0] = affine_strided
+    strided_grad_other = swap_rows(strided_grad)
+    (short_back,) = call(
+        functools.partial(short_back_kernel, dims),
+        [((wide_in // LANES, pixels, LANES), F32)],
+        shortcut_grad,
+        shortcut_weight,
+        late=(0, 1),
+        keep=(),
+        after=(order[0],),
+        flops=ops(small_pixels, wide_in, last),
+    )
+    order[0] = short_back
     affine_widen, widen_grad, block_back, sent, block_back_saved = call(
         block_back_kernel,
         [
@@ -1416,27 +1460,24 @@
         scratch=[rows(wide_in)],
         late=(3, 7, 8, 9, 10),
         keep=(2, 3),
+        after=(order[0],),
         flops=ops(pixels, wide_in, wider),
     )
     gathered = gather_all(sent)
 
-    second_shape = ((9 * wider + wide_in) // 2, wider)
-    kept, sent_on = wave(
+    order[0] = affine_widen
+    widen_grad_other = swap_rows(widen_grad)
+    second_shape = (9 * wider // 2, wider)
+    second_parts = wave_parts(
         second_wave_kernel,
         second_shape,
         taps,
         taps_other,
         strided_grad,
-        swap_rows(strided_grad),
-        block_out,
-        block_other,
-        widen_grad,
-        swap_rows(widen_grad),
+        strided_grad_other,
         flops=ops(2 * small_pixels, *second_shape),
     )
-    strided_total, widen_total = sum_over_chips(
-        kept, sent_on, second_out_kernel, [((9, wider // 2, wider), F32), ((wide_in // 2, wider), F32)], second_shape
-    )
+    second = moving_sum(second_parts, second_shape, second_out, [((9, wider // 2, wider), F32)])
 
     affine_closing, closing_grad, middle_back, edge, sent = call(
         functools.partial(middle_back_kernel, dims),
@@ -1447,7 +1488,6 @@
             ((2 * batch * width, mid), F32),
             message(mid),
         ],
-        flag,
         gathered,
         counts,
         block_back,
@@ -1459,13 +1499,16 @@
         middle_unit,
         middle_slope,
         scratch=[rows(mid)],
-        smem=(0,),
-        late=(4, 8, 9, 10),
+
+        late=(3, 7, 8, 9,),
         keep=(2, 3, 4),
+        after=(order[0],),
         flops=ops(pixels, wide_in, mid),
     )
     halo = swap_rows(edge)
     gathered = gather_all(sent)
+    order[0] = affine_closing
+    closing_grad_other = swap_rows(closing_grad)
     affine_middle, middle_grad, entry_back, sent = call(
         functools.partial(entry_back_kernel, dims),
         [((2, mid), F32), ((pixels, mid), BF16), ((pixels, mid), F32), message(mid)],
@@ -1485,9 +1528,13 @@
         scratch=[rows(mid), ((padded_rows + 16, mid), F32), ((batch, (height + 2) * width, 3 * mid), BF16)],
         late=(3, 10, 11, 12),
         keep=(2, 3),
+        after=(order[0],),
         flops=ops(pixels, 9, mid, mid),
     )
     gathered = gather_all(sent)
+    order[0] = affine_middle
+    middle_grad_other = swap_rows(middle_grad)
+    move(second)
     affine_entry, entry_grad, image_grads = call(
         images_kernel,
         [((2, mid), F32), ((pixels, mid), BF16), ((pixels, wide_in), BF16)],
@@ -1502,46 +1549,74 @@
         block_back_saved,
         late=(3, 7, 8),
         keep=(),
+        after=(order[0],),
         flops=ops(pixels, mid, wide_in),
     )
 
-    third_rows = 9 * mid // 2 + wide_in // 2
-    third_shape = (-(-third_rows // 256) * 256, mid)
-    kept, sent_on = wave(
+    order[0] = affine_entry
+    third_sizes = (wide_in // 2 * wider // mid, wide_in // 2, 9 * mid // 2, wide_in // 2)
+    third_shape = (-(-sum(third_sizes) // 256) * 256, mid)
+    third_parts = wave_parts(
         functools.partial(third_wave_kernel, dims),
         third_shape,
+        block_out,
+        block_other,
+        widen_grad,
+        widen_grad_other,
+        middle_act,
+        middle_act_other,
+        closing_grad,
+        closing_grad_other,
         triple,
         triple_other,
         middle_grad,
-        swap_rows(middle_grad),
-        middle_act,
-        middle_act_other,
-        closing_grad,
-        swap_rows(closing_grad),
-        flops=ops(2 * pixels, *third_shape),
-    )
-    middle_total, closing_total = sum_over_chips(
-        kept, sent_on, third_out_kernel, [((9, mid // 2, mid), F32), ((mid // 2, wide_in), F32)], third_shape
-    )
-    (parts,) = call(
-        last_wave_kernel,
-        [((wide_in // 2, mid), BF16)],
-        core,
+        middle_grad_other,
         entry_in,
         entry_in_other,
         entry_grad,
         swap_rows(entry_grad),
-        smem=(0,),
-        flops=ops(2 * pixels, wide_in // 2, mid),
-        late=None,
-    )
-    entry_total = sum_over_chips_short(parts.reshape(chips, -1, mid))
+        flops=ops(2 * pixels, *third_shape),
+    )
+    third = moving_sum(
+        third_parts,
+        third_shape,
+        third_out,
+        [
+            ((wide_in // 2, wider), F32),
+            ((mid // 2, wide_in), F32),
+            ((9, mid // 2, mid), F32),
+            ((wide_in // 2, mid), F32),
+        ],
+    )
+    totals = {}
+    for name in "bcbcbcbcbcbac":
+        if name == "a":
+            totals["a"] = call(
+                first_out,
+                [((wide_in // 2, last), F32), ((wider // 2, last), F32)],
+                first,
+                late=None,
+                after=(order[0],),
+            )
+            order[0] = totals["a"][0]
+        elif name not in totals:
+            result = move(second if name == "b" else third)
+            if result is not None:
+                totals[name] = result
+    for name, moving in (("b", second), ("c", third)):
+        while name not in totals:
+            result = move(moving)
+            if result is not None:
+                totals[name] = result
+    shortcut_total, expand_total = totals["a"]
+    (strided_total,) = totals["b"]
+    widen_total, closing_total, middle_total, entry_total = totals["c"]
     middle_total = middle_total.reshape(3, 3, mid // 2, mid)
     strided_total = strided_total.reshape(3, 3, wider // 2, wider)
     return (
         small_image(features),
         image(image_grads),
-        entry_total.astype(F32),
+        entry_total,
         middle_total,
         closing_total,
         widen_total,

time: 419 us -> 363 us (0.87)
  Pallas kernels: 135 us -> 83.2 us
  between operations: 1.95 us -> 14.8 us
  other arithmetic: 9.4 us -> 0.11 us
  starting transfers between devices: 85.2 us -> 76 us
    pallas_call x45 -> x33, Pallas kernels: 135 us -> 83.2 us  [call(): pl.pallas_call(body, out_shape=[jax.ShapeDtypeStruct(shape, dtype) if fre...]
    ppermute x36 -> x28, waiting for transfers between devices: 71.6 us -> 54.1 us  [to_chip(): return lax.ppermute(value, 'img', [(i, i ^ flip) for i in range(count)])]
    all_to_all x2 -> x0, starting transfers between devices: 9.87 us -> none  [the longest x1 6.22 us: sum_over_chips_short(): lax.all_to_all(spread, 'img', 0, 0, tiled=True).reshape(-1, parts.shape[-1])]
    psum x0 -> x1, waiting for transfers between devices: none -> 9.51 us  [per_device(): first = lax.psum(first, 'img')]
    another operation x8 -> x0, other arithmetic: 8.41 us -> none  [the longest x6 8.25 us: stack_pair(): return [jnp.stack(pair)]]
    all_to_all x8, waiting for transfers between devices: 31.7 us -> 39.8 us  [gather_all(): return lax.all_to_all(message, BOTH, 0, 0, tiled=True)]
    ppermute x36 -> x28, starting transfers between devices: 43.6 us -> 38.8 us  [to_chip(): return lax.ppermute(value, 'img', [(i, i ^ flip) for i in range(count)])]
    all_to_all x8, starting transfers between devices: 27.1 us -> 31.8 us  [gather_all(): return lax.all_to_all(message, BOTH, 0, 0, tiled=True)]
  transfers between devices with their start and end apart: 68 -> 59, of which waited for: 25 -> 31; matrix products, arithmetic and copies ran while one was open for 3% -> 0% of each run, Pallas kernels for 25% -> 14%
where the time goes in v2:
time: 363 us; the launch traced here: 361 us
  waiting for transfers between devices  114 us (31%)
  Pallas kernels  83.2 us (23%)
  starting transfers between devices  76 us (21%)
  blocking collectives  49.2 us (14%)
  local copies, waits for them, and re-layouts  23 us (6%)
  between operations  14.8 us (4%)
    pallas_call x33, Pallas kernels, call(): pl.pallas_call(body, out_shape=[jax.ShapeDtypeStruct(shape, dtype) if fre...  83.2 us
    ppermute x28, waiting for transfers between devices, to_chip(): return lax.ppermute(value, 'img', [(i, i ^ flip) for i in range(count)])  54.1 us
    all_to_all x8, waiting for transfers between devices, gather_all(): return lax.all_to_all(message, BOTH, 0, 0, tiled=True)  39.8 us
    ppermute x28, starting transfers between devices, to_chip(): return lax.ppermute(value, 'img', [(i, i ^ flip) for i in range(count)])  38.8 us
    all_to_all x8, starting transfers between devices, gather_all(): return lax.all_to_all(message, BOTH, 0, 0, tiled=True)  31.8 us
    all_to_all x2, blocking collectives, gather_img(): return lax.all_to_all(message, 'img', 0, 0, tiled=True)  26.8 us
    unnamed x123, local copies, waits for them, and re-layouts  23 us
    all_to_all x2, blocking collectives, gather_all(): return lax.all_to_all(message, BOTH, 0, 0, tiled=True)  22.4 us
  transfers between devices with their start and end apart: 59, of which 31 were waited for; matrix products, arithmetic and copies ran while one was open for 0% of the time, Pallas kernels for 14%

profile of v2, /device:TPU:0, one launch (start us, length us, event | category | flops | bytes accessed | tf_op | source)
XLA Modules:
  0.0 360.6 jit_solution(8523075206982730078)
XLA Ops:
  11.8 7.3 %all-to-all-start = ((f32[32,8,128]{2,1,0:T(8,128)}), f32[32,8,128]{2,1,0:T(8,128)S(1)}, u32[]{:S(2)}, u32[]{:S(2)}) async-start(f32[32,8,128]{2,1,0:T(8,128)} %get-tuple-element.141), calls=%async_computation | async-start | bytes 262144 | tf_op jit(solution)/shard_map/all_to_all | solution.py:25
  20.4 6.9 %all-to-all-done.refs_0_.refs_1_.refs_2_ = f32[32,8,128]{2,1,0:T(8,128)S(1)} async-done(((f32[32,8,128]{2,1,0:T(8,128)}), f32[32,8,128]{2,1,0:T(8,128)S(1)}, u32[]{:S(2)}, u32[]{:S(2)}) %all-to-all-start) | async-done | bytes 131104 | tf_op jit(solution)/shard_map/all_to_all | solution.py:25
  32.8 10.0 %all_to_all.60.refs_0_ = f32[32,8,128]{2,1,0:T(8,128)S(1)} all-to-all(f32[32,8,128]{2,1,0:T(8,128)S(1)} %get-tuple-element.147), channel_id=1, replica_groups=mesh['img'=16,'row'=2] {'img','row'}, dimensions={0} | all-to-all | bytes 262144 | tf_op jit(solution)/shard_map/all_to_all | solution.py:25
  44.6 12.4 %all_to_all.61.refs_0_ = f32[32,16,128]{2,1,0:T(8,128)S(1)} all-to-all(f32[32,16,128]{2,1,0:T(8,128)S(1)} %get-tuple-element.149), channel_id=1, replica_groups=mesh['img'=16,'row'=2] {'img','row'}, dimensions={0} | all-to-all | bytes 524288 | tf_op jit(solution)/shard_map/all_to_all | solution.py:25
  57.0 4.9 %shard_map.291 = (bf16[384,1024]{1,0:T(8,128)(2,1)}, f32[384,1024]{1,0:T(8,128)}, f32[384,1024]{1,0:T(8,128)}, f32[8,1024]{1,0:T(8,128)}, bf16[96,1024]{1,0:T(8,...) custom-call(f32[32,16,128]{2,1,0:T(8,128)S(1)} %all_to_all.61.refs_0, ...), custom_call_target="tpu_custom_call" | custom-call | flops 402653184 | bytes 9674752 | tf_op jit(solution)/shard_map/pallas_call | solution.py:129
  65.9 6.9 %all-to-all-done.3.refs_0_ = f32[32,8,128]{2,1,0:T(8,128)S(1)} async-done(((f32[32,8,128]{2,1,0:T(8,128)}), f32[32,8,128]{2,1,0:T(8,128)S(1)}, u32[]{:S(2)}, u32[]{:S(2)}) %all-to-all-start.3) | async-done | bytes 131104 | tf_op jit(solution)/shard_map/all_to_all | solution.py:25
  72.8 4.7 %shard_map.292 = (f32[384,512]{1,0:T(8,128)}, f32[384,512]{1,0:T(8,128)}, f32[8,512]{1,0:T(8,128)}, f32[96,512]{1,0:T(8,128)S(1)}, f32[32,8,128]{2,1,0:T(8,128)}...) custom-call(f32[32,8,128]{2,1,0:T(8,128)S(1)} %all-to-all-done.3.refs_0_, ...), custom_call_target="tpu_custom_call" | custom-call | flops 452984832 | bytes 9383936 | tf_op jit(solution)/shard_map/pallas_call | solution.py:129
  92.0 14.6 %all_to_all.62.refs_0_ = f32[16,40,128]{2,1,0:T(8,128)S(1)} all-to-all(f32[16,40,128]{2,1,0:T(8,128)S(1)} %shard_map.295), channel_id=1, replica_groups=mesh['img'=16,'row'=2] {'img'}, dimensions={0} | all-to-all | bytes 655360 | tf_op jit(solution)/shard_map/all_to_all | solution.py:29
  112.1 12.2 %all_to_all.63 = f32[16,24,128]{2,1,0:T(8,128)S(1)} all-to-all(f32[16,24,128]{2,1,0:T(8,128)S(1)} %broadcast_in_dim.2), channel_id=1, replica_groups=mesh['img'=16,'row'=2] {'img'}, dimensions={0} | all-to-all | bytes 393216 | tf_op jit(solution)/shard_map/all_to_all | solution.py:29
  134.8 5.1 %shard_map.299.refs_12_ = bf16[768,2048]{1,0:T(8,128)(2,1)} custom-call(bf16[96,1024]{1,0:T(8,128)(2,1)} %get-tuple-element.158.refs_0_, bf16[96,512]{1,0:T(8,128)(2,1)} %copy-done.55, bf16[96,512]{1,0:T(8,128)(2,1)} %get-tuple-element.182.refs_2_, bf16[96,256]{1,0:T(8,128)(2,1)} %copy-done.56, bf16[96,2048]{1,0:T(8,128)(2,1)} %get-tuple-element.184.refs_4_.refs_0_, ...), custom_call_target="tpu_custom_call" | custom-call | flops 603979776 | bytes 5177344 | tf_op jit(solution)/shard_map/pallas_call | solution.py:129
  140.5 4.9 %shard_map.300 = (f32[2,512]{1,0:T(2,128)}, bf16[96,512]{1,0:T(8,128)(2,1)}, f32[384,512]{1,0:T(8,128)S(1)}, f32[32,8,128]{2,1,0:T(8,128)}) custom-call(f32[32,8,128]{2,1,0:T(8,128)S(1)} %all-to-all-done.7.refs_0_, f32[32,8,128]{2,1,0:T(8,128)S(1)} %all-to-all-done.refs_0_.refs_1_.refs_2_, f32[96,512]{1,0:T(8,128)S(1)} %get-tuple-element.175.refs_2_, ...), custom_call_target="tpu_custom_call" | custom-call | flops 452984832 | bytes 11292672 | tf_op jit(solution)/shard_map/pallas_call | solution.py:129
  145.4 5.4 %all-to-all-start.8 = ((f32[32,8,128]{2,1,0:T(8,128)}), f32[32,8,128]{2,1,0:T(8,128)S(1)}, u32[]{:S(2)}, u32[]{:S(2)}) async-start(f32[32,8,128]{2,1,0:T(8,128)} %get-tuple-element.187), calls=%async_computation.8 | async-start | bytes 262144 | tf_op jit(solution)/shard_map/all_to_all | solution.py:25
  151.1 5.0 %shard_map.301.refs_8_.refs_11_ = f32[8,384,128]{2,1,0:T(8,128)} custom-call(bf16[96,2048]{1,0:T(8,128)(2,1)} %get-tuple-element.184.refs_4_.refs_0_, bf16[1024,2048]{1,0:T(8,128)(2,1)} %refs_1_.1, f32[2,512]{1,0:T(2,128)} %get-tuple-element.138.refs_2_), custom_call_target="tpu_custom_call" | custom-call | flops 402653184 | bytes 6164480 | tf_op jit(solution)/shard_map/pallas_call | solution.py:129
  159.0 5.6 %shard_map.302 = (f32[2,512]{1,0:T(2,128)}, bf16[384,512]{1,0:T(8,128)(2,1)}, f32[384,1024]{1,0:T(8,128)S(1)}, f32[32,16,128]{2,1,0:T(8,128)}, f32[384,1024]{1,0:T(8,128)}) custom-call(f32[32,8,128]{2,1,0:T(8,128)S(1)} %all-to-all-done.8.refs_0_, f32[32,8,128]{2,1,0:T(8,128)S(1)} %all-to-all-done.refs_0_.refs_1_.refs_2_, ...), custom_call_target="tpu_custom_call" | custom-call | flops 402653184 | bytes 13197312 | tf_op jit(solution)/shard_map/pallas_call | solution.py:129
  187.9 13.8 %all-to-all-done.10.refs_0_ = f32[32,8,128]{2,1,0:T(8,128)S(1)} async-done(((f32[32,8,128]{2,1,0:T(8,128)}), f32[32,8,128]{2,1,0:T(8,128)S(1)}, u32[]{:S(2)}, u32[]{:S(2)}) %all-to-all-start.10) | async-done | bytes 131104 | tf_op jit(solution)/shard_map/all_to_all | solution.py:25
  206.5 4.8 %all-to-all-start.11 = ((f32[32,8,128]{2,1,0:T(8,128)}), f32[32,8,128]{2,1,0:T(8,128)S(1)}, u32[]{:S(2)}, u32[]{:S(2)}) async-start(f32[32,8,128]{2,1,0:T(8,128)} %get-tuple-element.210), calls=%async_computation.11 | async-start | bytes 262144 | tf_op jit(solution)/shard_map/all_to_all | solution.py:25
  225.4 5.5 %shard_map.308 = (bf16[1664,128]{1,0:T(8,128)(2,1)S(1)}, bf16[1664,128]{1,0:T(8,128)(2,1)S(1)}, bf16[1664,128]{1,0:T(8,128)(2,1)S(1)}, bf16[1664,128]{1,0:T(8,128)(2,1)S(1)}) custom-call(bf16[384,1024]{1,0:T(8,128)(2,1)} %get-tuple-element.220.refs_0_, bf16[384,512]{1,0:T(8,128)(2,1)} %collective-permute-done.16.refs_1_, ...), custom_call_target="tpu_custom_call" | custom-call | flops 1308622848 | bytes 8611840 | tf_op jit(solution)/shard_map/pallas_call | solution.py:129
  235.7 16.4 %collective-permute-done.26.refs_2_ = bf16[576,256]{1,0:T(8,128)(2,1)S(1)} collective-permute-done((bf16[576,256]{1,0:T(8,128)(2,1)S(1)}, bf16[576,256]{1,0:T(8,128)(2,1)S(1)}, u32[]{:S(2)}, u32[]{:S(2)}) %collective-permute-start.26) | collective-permute-done | bytes 294944 | tf_op jit(solution)/shard_map/ppermute | solution.py:1014
  261.3 6.9 %collective-permute-done.31.refs_2_ = bf16[2,144,256]{2,1,0:T(8,128)(2,1)S(1)} collective-permute-done((bf16[2,144,256]{2,1,0:T(8,128)(2,1)S(1)}, bf16[2,144,256]{2,1,0:T(8,128)(2,1)S(1)}, u32[]{:S(2)}, u32[]{:S(2)}) %collective-permute-start.31) | collective-permute-done | bytes 147488 | tf_op jit(solution)/shard_map/ppermute | solution.py:1014
  276.7 7.9 %collective-permute-done.37.refs_2_ = bf16[2,144,256]{2,1,0:T(8,128)(2,1)S(1)} collective-permute-done((bf16[2,144,256]{2,1,0:T(8,128)(2,1)S(1)}, bf16[2,144,256]{2,1,0:T(8,128)(2,1)S(1)}, u32[]{:S(2)}, u32[]{:S(2)}) %collective-permute-start.37) | collective-permute-done | bytes 147488 | tf_op jit(solution)/shard_map/ppermute | solution.py:1014
  311.4 5.9 %collective-permute-done.39.refs_1_ = bf16[2,208,128]{2,1,0:T(8,128)(2,1)S(1)} collective-permute-done((bf16[2,208,128]{2,1,0:T(8,128)(2,1)}, bf16[2,208,128]{2,1,0:T(8,128)(2,1)S(1)}, u32[]{:S(2)}, u32[]{:S(2)}) %collective-permute-start.39) | collective-permute-done | bytes 106528 | tf_op jit(solution)/shard_map/ppermute | solution.py:1014
  317.3 7.8 %collective-permute-done.40.refs_2_ = bf16[2,208,128]{2,1,0:T(8,128)(2,1)S(1)} collective-permute-done((bf16[2,208,128]{2,1,0:T(8,128)(2,1)}, bf16[2,208,128]{2,1,0:T(8,128)(2,1)S(1)}, u32[]{:S(2)}, u32[]{:S(2)}) %collective-permute-start.40) | collective-permute-done | bytes 106528 | tf_op jit(solution)/shard_map/ppermute | solution.py:1014
  336.1 9.5 %all-reduce.2.cloned.1.call-done.refs_0_ = bf16[768,2048]{1,0:T(8,128)(2,1)} async-done(((bf16[768,2048]{1,0:T(8,128)(2,1)}), bf16[768,2048]{1,0:T(8,128)(2,1)}) %all-reduce.2.cloned.1.call-update) | async-done | bytes 3145744 | tf_op jit(solution)/shard_map/psum | solution.py:1399
  345.6 4.9 %shard_map.319 = (f32[512,2048]{1,0:T(8,128)}, f32[256,2048]{1,0:T(8,128)}) custom-call(bf16[768,2048]{1,0:T(8,128)(2,1)} %all-reduce.2.cloned.1.call-done.refs_0_, bf16[1664,128]{1,0:T(8,128)(2,1)} %copy-done.7), custom_call_target="tpu_custom_call" | custom-call | bytes 9863168 | tf_op jit(solution)/shard_map/pallas_call | solution.py:129
  (260 shorter events, 156.8 us)
Async XLA Ops:
  11.8 15.5 %all-to-all-start = ((f32[32,8,128]{2,1,0:T(8,128)}), f32[32,8,128]{2,1,0:T(8,128)S(1)}, u32[]{:S(2)}, u32[]{:S(2)}) async-start(f32[32,8,128]{2,1,0:T(8,128)} %get-tuple-element.141), calls=%async_computation | async-start | bytes 262144 | tf_op jit(solution)/shard_map/all_to_all | solution.py:25
  150.7 17.5 %collective-permute-start.11 = (bf16[3,96,768]{2,1,0:T(8,128)(2,1)}, bf16[3,96,768]{2,1,0:T(8,128)(2,1)S(1)}, u32[]{:S(2)}, u32[]{:S(2)}) collective-permute-start(bf16[3,96,768]{2,1,0:T(8,128)(2,1)} %get-tuple-element.199), channel_id=1, source_target_pairs={{0,1},{1,0},{2,3},{3,2},{4,5},{5,4},{6,7},{7,6},{8,9},{9,8},{10,11... | collective-permute-start | bytes 1327112 | tf_op jit(solution)/shard_map/ppermute | solution.py:21
  167.5 178.2 %all-reduce.2.cloned.1.call-start = ((), (), s32[]{:S(2)}) async-start(), calls=%async_computation.12 | async-start | bytes 6291456 | tf_op jit(solution)/shard_map/psum | solution.py:1399
  174.7 36.7 %collective-permute-start.14 = (bf16[1152,256]{1,0:T(8,128)(2,1)}, bf16[1152,256]{1,0:T(8,128)(2,1)S(1)}, u32[]{:S(2)}, u32[]{:S(2)}) collective-permute-start(bf16[1152,256]{1,0:T(8,128)(2,1)} %get-tuple-element.215), channel_id=1, source_target_pairs={{0,2},{2,0},{4,6},{6,4},{8,10},{10,8},{12,14},{14,12},{16,18},{18,... | collective-permute-start | bytes 1769480 | tf_op jit(solution)/shard_map/ppermute | solution.py:1014
  176.5 35.4 %collective-permute-start.15 = (bf16[1152,256]{1,0:T(8,128)(2,1)}, bf16[1152,256]{1,0:T(8,128)(2,1)}, u32[]{:S(2)}, u32[]{:S(2)}) collective-permute-start(bf16[1152,256]{1,0:T(8,128)(2,1)} %get-tuple-element.216), channel_id=1, source_target_pairs={{0,4},{2,6},{4,0},{6,2},{8,12},{10,14},{12,8},{14,10},{16,20},{18,... | collective-permute-start | bytes 1769480 | tf_op jit(solution)/shard_map/ppermute | solution.py:1014
  178.0 33.4 %collective-permute-start.22 = (bf16[384,512]{1,0:T(8,128)(2,1)}, bf16[384,512]{1,0:T(8,128)(2,1)}, u32[]{:S(2)}, u32[]{:S(2)}) collective-permute-start(bf16[384,512]{1,0:T(8,128)(2,1)} %get-tuple-element.229), channel_id=1, source_target_pairs={{0,1},{1,0},{2,3},{3,2},{4,5},{5,4},{6,7},{7,6},{8,9},{9,8},{10,11... | collective-permute-start | bytes 1179656 | tf_op jit(solution)/shard_map/ppermute | solution.py:21
  182.1 42.6 %collective-permute-start.19 = (bf16[384,1024]{1,0:T(8,128)(2,1)}, bf16[384,1024]{1,0:T(8,128)(2,1)}, u32[]{:S(2)}, u32[]{:S(2)}) collective-permute-start(bf16[384,1024]{1,0:T(8,128)(2,1)} %get-tuple-element.225.refs_6_), channel_id=1, source_target_pairs={{0,1},{1,0},{2,3},{3,2},{4,5},{5,4},{6,7},{7,6},{8,9},{9,8},{10,11... | collective-permute-start | bytes 2359304 | tf_op jit(solution)/shard_map/ppermute | solution.py:21
  182.6 19.1 %all-to-all-start.10 = ((f32[32,8,128]{2,1,0:T(8,128)}), f32[32,8,128]{2,1,0:T(8,128)S(1)}, u32[]{:S(2)}, u32[]{:S(2)}) async-start(f32[32,8,128]{2,1,0:T(8,128)} %get-tuple-element.203), calls=%async_computation.10 | async-start | bytes 262144 | tf_op jit(solution)/shard_map/all_to_all | solution.py:25
  187.7 35.3 %collective-permute-start.20 = (bf16[3,160,384]{2,1,0:T(8,128)(2,1)}, bf16[3,160,384]{2,1,0:T(8,128)(2,1)}, u32[]{:S(2)}, u32[]{:S(2)}) collective-permute-start(bf16[3,160,384]{2,1,0:T(8,128)(2,1)} %get-tuple-element.227), channel_id=1, source_target_pairs={{0,1},{1,0},{2,3},{3,2},{4,5},{5,4},{6,7},{7,6},{8,9},{9,8},{10,11... | collective-permute-start | bytes 1105928 | tf_op jit(solution)/shard_map/ppermute | solution.py:21
  231.6 25.6 %collective-permute-start.24 = (bf16[1664,128]{1,0:T(8,128)(2,1)S(1)}, bf16[1664,128]{1,0:T(8,128)(2,1)S(1)}, u32[]{:S(2)}, u32[]{:S(2)}) collective-permute-start(bf16[1664,128]{1,0:T(8,128)(2,1)S(1)} %get-tuple-element.234), channel_id=1, source_target_pairs={{0,2},{2,0},{4,6},{6,4},{8,10},{10,8},{12,14},{14,12},{16,18},{18,... | collective-permute-start | bytes 1277960 | tf_op jit(solution)/shard_map/ppermute | solution.py:1014
  231.7 25.5 %collective-permute-start.25 = (bf16[1664,128]{1,0:T(8,128)(2,1)S(1)}, bf16[1664,128]{1,0:T(8,128)(2,1)S(1)}, u32[]{:S(2)}, u32[]{:S(2)}) collective-permute-start(bf16[1664,128]{1,0:T(8,128)(2,1)S(1)} %get-tuple-element.235), channel_id=1, source_target_pairs={{0,4},{2,6},{4,0},{6,2},{8,12},{10,14},{12,8},{14,10},{16,20},{18,... | collective-permute-start | bytes 1277960 | tf_op jit(solution)/shard_map/ppermute | solution.py:1014
  232.8 19.3 %collective-permute-start.26 = (bf16[576,256]{1,0:T(8,128)(2,1)S(1)}, bf16[576,256]{1,0:T(8,128)(2,1)S(1)}, u32[]{:S(2)}, u32[]{:S(2)}) collective-permute-start(bf16[576,256]{1,0:T(8,128)(2,1)S(1)} %copy-done.48), channel_id=1, source_target_pairs={{0,4},{2,6},{4,0},{6,2},{8,12},{10,14},{12,8},{14,10},{16,20},{18,... | collective-permute-start | bytes 884744 | tf_op jit(solution)/shard_map/ppermute | solution.py:1014
  233.8 18.3 %collective-permute-start.27 = (bf16[576,256]{1,0:T(8,128)(2,1)S(1)}, bf16[576,256]{1,0:T(8,128)(2,1)S(1)}, u32[]{:S(2)}, u32[]{:S(2)}) collective-permute-start(bf16[576,256]{1,0:T(8,128)(2,1)S(1)} %get-tuple-element.238), channel_id=1, source_target_pairs={{0,2},{2,0},{4,6},{6,4},{8,10},{10,8},{12,14},{14,12},{16,18},{18,... | collective-permute-start | bytes 884744 | tf_op jit(solution)/shard_map/ppermute | solution.py:1014
  253.2 15.0 %collective-permute-start.31 = (bf16[2,144,256]{2,1,0:T(8,128)(2,1)S(1)}, bf16[2,144,256]{2,1,0:T(8,128)(2,1)S(1)}, u32[]{:S(2)}, u32[]{:S(2)}) collective-permute-start(bf16[2,144,256]{2,1,0:T(8,128)(2,1)S(1)} %get-tuple-element.245), channel_id=1, source_target_pairs={{0,16},{2,18},{4,20},{6,22},{8,24},{10,26},{12,28},{14,30},{16,0},... | collective-permute-start | bytes 442376 | tf_op jit(solution)/shard_map/ppermute | solution.py:1014
  259.1 15.7 %collective-permute-start.28 = (bf16[832,128]{1,0:T(8,128)(2,1)S(1)}, bf16[832,128]{1,0:T(8,128)(2,1)S(1)}, u32[]{:S(2)}, u32[]{:S(2)}) collective-permute-start(bf16[832,128]{1,0:T(8,128)(2,1)S(1)} %get-tuple-element.242), channel_id=1, source_target_pairs={{0,4},{2,6},{4,0},{6,2},{8,12},{10,14},{12,8},{14,10},{16,20},{18,... | collective-permute-start | bytes 638984 | tf_op jit(solution)/shard_map/ppermute | solution.py:1014
  260.0 14.8 %collective-permute-start.29 = (bf16[832,128]{1,0:T(8,128)(2,1)S(1)}, bf16[832,128]{1,0:T(8,128)(2,1)S(1)}, u32[]{:S(2)}, u32[]{:S(2)}) collective-permute-start(bf16[832,128]{1,0:T(8,128)(2,1)S(1)} %get-tuple-element.243), channel_id=1, source_target_pairs={{0,2},{2,0},{4,6},{6,4},{8,10},{10,8},{12,14},{14,12},{16,18},{18,... | collective-permute-start | bytes 638984 | tf_op jit(solution)/shard_map/ppermute | solution.py:1014
  285.5 17.9 %collective-permute-start.42 = (bf16[576,256]{1,0:T(8,128)(2,1)S(1)}, bf16[576,256]{1,0:T(8,128)(2,1)S(1)}, u32[]{:S(2)}, u32[]{:S(2)}) collective-permute-start(bf16[576,256]{1,0:T(8,128)(2,1)S(1)} %get-tuple-element.251.refs_4_.refs_0_), channel_id=1, source_target_pairs={{0,4},{2,6},{4,0},{6,2},{8,12},{10,14},{12,8},{14,10},{16,20},{18,... | collective-permute-start | bytes 884744 | tf_op jit(solution)/shard_map/ppermute | solution.py:1014
  286.3 17.1 %collective-permute-start.43 = (bf16[576,256]{1,0:T(8,128)(2,1)S(1)}, bf16[576,256]{1,0:T(8,128)(2,1)S(1)}, u32[]{:S(2)}, u32[]{:S(2)}) collective-permute-start(bf16[576,256]{1,0:T(8,128)(2,1)S(1)} %get-tuple-element.252.refs_1_), channel_id=1, source_target_pairs={{0,2},{2,0},{4,6},{6,4},{8,10},{10,8},{12,14},{14,12},{16,18},{18,... | collective-permute-start | bytes 884744 | tf_op jit(solution)/shard_map/ppermute | solution.py:1014
  304.5 23.9 %collective-permute-start.46 = (bf16[1152,256]{1,0:T(8,128)(2,1)S(1)}, bf16[1152,256]{1,0:T(8,128)(2,1)S(1)}, u32[]{:S(2)}, u32[]{:S(2)}) collective-permute-start(bf16[1152,256]{1,0:T(8,128)(2,1)S(1)} %get-tuple-element.253.refs_4_.refs_0_), channel_id=1, source_target_pairs={{0,2},{2,0},{4,6},{6,4},{8,10},{10,8},{12,14},{14,12},{16,18},{18,... | collective-permute-start | bytes 1769480 | tf_op jit(solution)/shard_map/ppermute | solution.py:1014
  306.5 22.3 %collective-permute-start.47 = (bf16[1152,256]{1,0:T(8,128)(2,1)S(1)}, bf16[1152,256]{1,0:T(8,128)(2,1)S(1)}, u32[]{:S(2)}, u32[]{:S(2)}) collective-permute-start(bf16[1152,256]{1,0:T(8,128)(2,1)S(1)} %get-tuple-element.256.refs_1_), channel_id=1, source_target_pairs={{0,4},{2,6},{4,0},{6,2},{8,12},{10,14},{12,8},{14,10},{16,20},{18,... | collective-permute-start | bytes 1769480 | tf_op jit(solution)/shard_map/ppermute | solution.py:1014
  309.0 16.1 %collective-permute-start.40 = (bf16[2,208,128]{2,1,0:T(8,128)(2,1)}, bf16[2,208,128]{2,1,0:T(8,128)(2,1)S(1)}, u32[]{:S(2)}, u32[]{:S(2)}) collective-permute-start(bf16[2,208,128]{2,1,0:T(8,128)(2,1)} %copy-done.17), channel_id=1, source_target_pairs={{0,16},{2,18},{4,20},{6,22},{8,24},{10,26},{12,28},{14,30},{16,0},... | collective-permute-start | bytes 319496 | tf_op jit(solution)/shard_map/ppermute | solution.py:1014
  309.0 16.1 %collective-permute-start.41 = (bf16[2,208,128]{2,1,0:T(8,128)(2,1)}, bf16[2,208,128]{2,1,0:T(8,128)(2,1)S(1)}, u32[]{:S(2)}, u32[]{:S(2)}) collective-permute-start(bf16[2,208,128]{2,1,0:T(8,128)(2,1)} %copy-done.17), channel_id=1, source_target_pairs={{0,24},{2,26},{4,28},{6,30},{8,16},{10,18},{12,20},{14,22},{16,8},... | collective-permute-start | bytes 319496 | tf_op jit(solution)/shard_map/ppermute | solution.py:1014
  334.5 16.0 %collective-permute-start.48 = (bf16[1664,128]{1,0:T(8,128)(2,1)S(1)}, bf16[1664,128]{1,0:T(8,128)(2,1)S(1)}, u32[]{:S(2)}, u32[]{:S(2)}) collective-permute-start(bf16[1664,128]{1,0:T(8,128)(2,1)S(1)} %get-tuple-element.257.refs_1_.refs_0_), channel_id=1, source_target_pairs={{0,2},{2,0},{4,6},{6,4},{8,10},{10,8},{12,14},{14,12},{16,18},{18,... | collective-permute-start | bytes 1277960 | tf_op jit(solution)/shard_map/ppermute | solution.py:1014
  335.6 14.9 %collective-permute-start.49 = (bf16[1664,128]{1,0:T(8,128)(2,1)S(1)}, bf16[1664,128]{1,0:T(8,128)(2,1)S(1)}, u32[]{:S(2)}, u32[]{:S(2)}) collective-permute-start(bf16[1664,128]{1,0:T(8,128)(2,1)S(1)} %get-tuple-element.258.refs_1_), channel_id=1, source_target_pairs={{0,4},{2,6},{4,0},{6,2},{8,12},{10,14},{12,8},{14,10},{16,20},{18,... | collective-permute-start | bytes 1277960 | tf_op jit(solution)/shard_map/ppermute | solution.py:1014
  (96 other events, 714.2 us)
Sparse Core Ops, SparseCore 0:
  174.4 171.1 all-reduce.1

commit v3 on v2

--- a/solution.py
+++ b/solution.py
@@ -99,7 +99,7 @@
         return pl.ANY if place in late or place >= used else pltpu.VMEM
 
     operands = [
-        pltpu.with_memory_space_constraint(x, pltpu.HBM) if place in late or place >= used else x
+        pltpu.with_memory_space_constraint(x, pltpu.HBM) if place in late or (place >= used and in_hbm(x)) else x
         for place, x in enumerate(operands)
     ]
     buffers = [pltpu.VMEM(operands[place].shape, operands[place].dtype) for place in late]
@@ -126,7 +126,7 @@
         for place in saved:
             results[place].copy.wait()
 
-    return pl.pallas_call(
+    results = pl.pallas_call(
         body,
         out_shape=[
             jax.ShapeDtypeStruct(shape, dtype)
@@ -142,6 +142,15 @@
         compiler_params=pltpu.CompilerParams(vmem_limit_bytes=limit * MIB),
         cost_estimate=pl.CostEstimate(flops=flops, bytes_accessed=moved, transcendentals=0),
     )(*operands)
+    HELD.extend(results[place] for place in saved)
+    return results
+
+
+HELD = []
+
+
+def in_hbm(value):
+    return any(value is held for held in HELD)
 
 
 def dot(left, right):
@@ -814,21 +823,29 @@
     )
 
 
-def bit_half(bit, flip, rows):
+class View:
+    def __init__(self, refs, group):
+        self.ref = refs[group] if len(refs) > 1 else refs[0]
+        self.lead = () if len(refs) > 1 else (group,)
+        self.rows = self.ref.shape[-2]
+
+    def __getitem__(self, here):
+        return self.ref[self.lead + (here, slice(None))]
+
+    def __setitem__(self, here, value):
+        self.ref[self.lead + (here, slice(None))] = value
+
+
+def half_rows(bit, flip, rows):
     mine = (lax.axis_index("img").astype(jnp.int32) >> bit) & 1
     return pl.ds(pl.multiple_of((1 - mine if flip else mine) * rows, 16), rows)
-
-
-def round_part(low, bits, flip, rows):
-    mine = (lax.axis_index("img").astype(jnp.int32) >> low) & ((1 << bits) - 1)
-    return pl.ds(pl.multiple_of((mine ^ flip) * rows, 16), rows)
 
 
 def deal(full, parts):
     rows, width = parts[0].shape
     for outs, flip in ((parts[2:], True), (parts[:2], False)):
-        for group, out in enumerate(outs):
-            out[...] = full[bit_half((0, 1)[group], flip, rows), group * width : (group + 1) * width]
+        for group, (out, bit) in enumerate(zip(outs, steps()[0])):
+            out[...] = full[half_rows(bit, flip, rows), group * width : (group + 1) * width]
 
 
 def first_wave_kernel(
@@ -870,12 +887,10 @@
         full[row:, :] = jnp.zeros((full.shape[0] - row, full.shape[1]), full.dtype)
 
 
-def third_wave_kernel(
+def third_early_kernel(
     dims, block, block_other, widen_grad, widen_grad_other, act, act_other, closing_grad,
-    closing_grad_other, triple, triple_other, middle_grad, middle_grad_other, entry_in, entry_in_other, entry_grad,
-    entry_grad_other, *results,
+    closing_grad_other, triple, triple_other, middle_grad, middle_grad_other, full,
 ):
-    *parts, full = results
     batch, height, width = dims
     pixels = height * width
     step = full.shape[1]
@@ -901,67 +916,48 @@
             value = dot_pixels(own, middle_grad[...]) + dot_pixels(other, middle_grad_other[...])
             full[row : row + half, :] = value.astype(BF16)
             row += half
-    rows = entry_in_other.shape[1]
+
+
+def third_wave_kernel(early, entry_in, entry_in_other, entry_grad, entry_grad_other, *results):
+    *parts, full = results
+    row, rows = early.shape[0], entry_in_other.shape[1]
     full[row : row + rows, :] = chip_grad(entry_in, entry_in_other, entry_grad, entry_grad_other).astype(BF16)
     fill_rest(full, row + rows)
+    full[:row, :] = early[...]
     deal(full, parts)
 
 
-def added(parts, *index):
-    total = parts[0][index].astype(F32)
-    for part in parts[1:]:
-        total = total + part[index].astype(F32)
-    return total.astype(BF16)
-
-
-def halve_kernel(kept_a, kept_b, got_a, got_b, *outs):
-    rows = outs[0].shape[0]
-    for targets, flip in ((outs[2:], True), (outs[:2], False)):
-        for group, (out, parts) in enumerate(zip(targets, ((kept_a, got_a), (kept_b, got_b)))):
-            out[...] = added(parts, bit_half((1, 0)[group], flip, rows), slice(None))
-
-
-def part_order(count):
-    return list(range(1, count)) + [0]
-
-
-def quarter_kernel(step, kept_a, kept_b, got_a, got_b, *outs):
-    rows = outs[0].shape[1]
-    for flip in part_order(len(outs)):
-        here = round_part(*step, flip, rows)
-        for group, parts in enumerate(((kept_a, got_a), (kept_b, got_b))):
-            outs[flip][group] = added(parts, here, slice(None))
-
-
-def fold_kernel(count, step, *refs):
-    parts, outs = refs[:count], refs[count:]
-    rows = outs[0].shape[1]
-    for flip in part_order(len(outs)):
-        outs[flip][...] = added(parts, slice(None), round_part(*step, flip, rows), slice(None))
-
-
-def add_kernel(*refs):
-    *parts, out = refs
-    out[...] = added(parts, slice(None))
-
-
-def merge_kernel(count, step, *refs):
-    parts, outs = refs[:count], refs[count:]
-    rows = parts[0].shape[1]
-    for flip, part in enumerate(parts):
-        here = round_part(*step, flip, rows)
-        if len(outs) == 1:
-            outs[0][:, here, :] = part[...]
-        else:
-            for group, out in enumerate(outs):
-                out[here, :] = part[group]
-
-
-def double_kernel(own_a, own_b, got_a, got_b, *outs):
-    rows = own_a.shape[0]
-    for group, (out, own, got) in enumerate(zip(outs, (own_a, own_b), (got_a, got_b))):
-        out[bit_half((1, 0)[group], False, rows), :] = own[...]
-        out[bit_half((1, 0)[group], True, rows), :] = got[...]
+def split_refs(refs, sizes):
+    parts, start = [], 0
+    for size in sizes:
+        parts.append(refs[start : start + size])
+        start += size
+    return parts
+
+
+def added(first, second):
+    return (first.astype(F32) + second.astype(F32)).astype(BF16)
+
+
+def halve_kernel(sizes, bits, *refs):
+    kept, got, keep, pass_on = split_refs(refs, sizes)
+    for outs, flip in ((pass_on, True), (keep, False)):
+        for group, bit in enumerate(bits):
+            out, first, second = View(outs, group), View(kept, group), View(got, group)
+            here = half_rows(bit, flip, out.rows)
+            out[:] = added(first[here], second[here])
+
+
+def add_kernel(kept, got, out):
+    out[...] = added(kept[...], got[...])
+
+
+def double_kernel(sizes, bits, *refs):
+    own, got, outs = split_refs(refs, sizes)
+    for group, bit in enumerate(bits):
+        out, first, second = View(outs, group), View(own, group), View(got, group)
+        out[half_rows(bit, False, first.rows)] = first[:]
+        out[half_rows(bit, True, first.rows)] = second[:]
 
 
 def first_out(full, short, expand):
@@ -994,84 +990,83 @@
     entry[...] = full[row : row + entry.shape[0], :].astype(F32)
 
 
-def out_kernel(finish, own_a, own_b, got_a, got_b, *refs):
+def out_kernel(finish, bits, own_a, own_b, got_a, got_b, *refs):
     outs, full = refs[:-1], refs[-1]
     rows, width = own_a.shape
-    for group, (own, got) in enumerate(((own_a, got_a), (own_b, got_b))):
+    for group, (bit, own, got) in enumerate(zip(bits, (own_a, own_b), (got_a, got_b))):
         columns = slice(group * width, (group + 1) * width)
-        full[bit_half((0, 1)[group], False, rows), columns] = own[...]
-        full[bit_half((0, 1)[group], True, rows), columns] = got[...]
+        full[half_rows(bit, False, rows), columns] = own[...]
+        full[half_rows(bit, True, rows), columns] = got[...]
     finish(full, *outs)
 
 
-def rounds():
+def steps():
     bits = lax.axis_size("img").bit_length() - 1
-    return [(low, min(2, bits - low)) for low in range(2, bits, 2)]
-
-
-def to_chip(value, flip):
+    return [(0, 1), (1, 0)] + [(bit, bit) for bit in range(2, bits)]
+
+
+def to_chip(value, bit):
     count = lax.axis_size("img")
-    return lax.ppermute(value, "img", [(i, i ^ flip) for i in range(count)])
-
-
-def sum_over_chips(order, parts, finish, outs, shape):
-    steps = rounds()
-
-    def run(kernel, shapes, *operands, scratch=(), free=True):
-        results = call(kernel, shapes, *operands, free=free, after=(order[0],), scratch=scratch)
-        order[0] = results[0]
-        return results
-
-    def exchange(values, low):
-        return [to_chip(value, number << low) for number, value in enumerate(values, 1)]
-
-    rows, width = shape[0] // 2, shape[1] // 2
-    kept, sent = parts[:2], parts[2:]
-    got = [to_chip(sent[0], 1), to_chip(sent[1], 2)]
-    yield None
-    rows //= 2
-    results = run(halve_kernel, [((rows, width), BF16)] * 4, *kept, *got)
-    kept, sent = results[:2], results[2:]
-    got = [to_chip(sent[0], 2), to_chip(sent[1], 1)]
-    yield None
-    low, bits = steps[0]
-    rows >>= bits
-    parts = run(functools.partial(quarter_kernel, steps[0]), [((2, rows, width), BF16)] * (1 << bits), *kept, *got)
-    dealt = 1
-    for number, (low, bits) in enumerate(steps):
-        if number < dealt:
-            got = exchange(parts[1:], low)
+    return lax.ppermute(value, "img", [(i, i ^ (1 << bit)) for i in range(count)])
+
+
+def exchange(values, bits):
+    return [to_chip(value, bit) for value, bit in zip(values, bits)]
+
+
+def run_after(order, kernel, shapes, *operands, scratch=(), free=True):
+    results = call(kernel, shapes, *operands, free=free, after=(order[0],), scratch=scratch)
+    order[0] = results[0]
+    return results
+
+
+def group_shapes(bits, rows, width):
+    return [((2, rows, width), BF16)] if bits[0] == bits[1] else [((rows, width), BF16)] * 2
+
+
+def halve(order, kept, got, bits, rows, width):
+    shapes = group_shapes(bits, rows, width)
+    sizes = (len(kept), len(got), len(shapes), len(shapes))
+    results = run_after(order, functools.partial(halve_kernel, sizes, bits), shapes * 2, *kept, *got)
+    return results[: len(shapes)], results[len(shapes) :]
+
+
+def sum_over_chips(order, kept, sent, number, shape, finish=None):
+    todo = steps()
+    rows, width = shape[0] >> (number + 1), shape[1] // 2
+    halvings = number + 1
+    for number in range(number, len(todo)):
+        got = exchange(sent, todo[number])
+        yield None
+        following = todo[number + 1] if number + 1 < len(todo) else None
+        if following is not None and number + 1 == halvings and (number == 0 or rows % 32 == 0):
+            halvings += 1
+            rows //= 2
+            kept, sent = halve(order, kept, got, following, rows, width)
         else:
-            got = exchange([parts[0]] * ((1 << bits) - 1), low)
+            kept = sent = run_after(order, add_kernel, [((2, rows, width), BF16)], kept[0], got[0])
+    own = kept
+    for number in reversed(range(1, halvings)):
+        got = exchange(own, todo[number])
         yield None
-        parts = [parts[0]] + got
-        following = steps[number + 1] if number + 1 < len(steps) else None
-        if following is not None and number + 1 == dealt and rows % (16 << following[1]) == 0:
-            rows >>= following[1]
-            dealt += 1
-            parts = run(
-                functools.partial(fold_kernel, len(parts), following),
-                [((2, rows, width), BF16)] * (1 << following[1]),
-                *parts,
-            )
-        else:
-            parts = run(add_kernel, [((2, rows, width), BF16)], *parts)
-    (share,) = parts
-    for number in reversed(range(dealt)):
-        low, bits = steps[number]
-        got = exchange([share] * ((1 << bits) - 1), low)
+        rows *= 2
+        shapes = group_shapes(todo[number - 1], rows, width)
+        sizes = (len(own), len(got), len(shapes))
+        own = run_after(order, functools.partial(double_kernel, sizes, todo[number]), shapes, *own, *got)
+    if finish is not None:
+        got = exchange(own, todo[0])
         yield None
-        rows <<= bits
-        shapes = [((2, rows, width), BF16)] if number > 0 else [((rows, width), BF16)] * 2
-        own = run(functools.partial(merge_kernel, 1 + len(got), steps[number]), shapes, share, *got)
-        share = own[0]
-    got = [to_chip(own[0], 2), to_chip(own[1], 1)]
-    yield None
-    rows *= 2
-    own = run(double_kernel, [((rows, width), BF16)] * 2, *own, *got)
-    got = [to_chip(own[0], 1), to_chip(own[1], 2)]
-    yield None
-    yield run(functools.partial(out_kernel, finish), outs, *own, *got, scratch=[(shape, BF16)], free=False)
+        kernel, outs = finish
+        own = run_after(
+            order,
+            functools.partial(out_kernel, kernel, todo[0]),
+            outs,
+            *own,
+            *got,
+            scratch=[(shape, BF16)],
+            free=False,
+        )
+    yield own
 
 
 def per_device(
@@ -1353,12 +1348,6 @@
 
     order = [affine_expand]
 
-    def move(wave, times=1):
-        for _ in range(times):
-            result = next(wave)
-        return result
-
-
     def wave_parts(kernel, shape, *operands, flops):
         parts = call(
             kernel,
@@ -1372,11 +1361,6 @@
         )
         order[0] = parts[0]
         return parts
-
-    def moving_sum(parts, shape, finish, outs):
-        moving = sum_over_chips(order, parts, finish, outs, shape)
-        move(moving)
-        return moving
 
     first_shape = ((wide_in + wider) // 2, last)
     (first,) = call(
@@ -1477,7 +1461,7 @@
         strided_grad_other,
         flops=ops(2 * small_pixels, *second_shape),
     )
-    second = moving_sum(second_parts, second_shape, second_out, [((9, wider // 2, wider), F32)])
+    second_got = exchange(second_parts[2:], steps()[0])
 
     affine_closing, closing_grad, middle_back, edge, sent = call(
         functools.partial(middle_back_kernel, dims),
@@ -1534,7 +1518,31 @@
     gathered = gather_all(sent)
     order[0] = affine_middle
     middle_grad_other = swap_rows(middle_grad)
-    move(second)
+    third_sizes = (wide_in // 2 * wider // mid, wide_in // 2, 9 * mid // 2, wide_in // 2)
+    third_shape = (-(-sum(third_sizes) // 256) * 256, mid)
+    (third_early,) = call(
+        functools.partial(third_early_kernel, dims),
+        [((sum(third_sizes[:3]), mid), BF16)],
+        block_out,
+        block_other,
+        widen_grad,
+        widen_grad_other,
+        middle_act,
+        middle_act_other,
+        closing_grad,
+        closing_grad_other,
+        triple,
+        triple_other,
+        middle_grad,
+        middle_grad_other,
+        flops=ops(2 * pixels, *third_shape),
+        late=None,
+        after=(order[0],),
+    )
+    order[0] = third_early
+    second_kept, second_sent = halve(
+        order, second_parts[:2], second_got, steps()[1], second_shape[0] // 4, second_shape[1] // 2
+    )
     affine_entry, entry_grad, image_grads = call(
         images_kernel,
         [((2, mid), F32), ((pixels, mid), BF16), ((pixels, wide_in), BF16)],
@@ -1554,63 +1562,64 @@
     )
 
     order[0] = affine_entry
-    third_sizes = (wide_in // 2 * wider // mid, wide_in // 2, 9 * mid // 2, wide_in // 2)
-    third_shape = (-(-sum(third_sizes) // 256) * 256, mid)
     third_parts = wave_parts(
-        functools.partial(third_wave_kernel, dims),
+        third_wave_kernel,
         third_shape,
-        block_out,
-        block_other,
-        widen_grad,
-        widen_grad_other,
-        middle_act,
-        middle_act_other,
-        closing_grad,
-        closing_grad_other,
-        triple,
-        triple_other,
-        middle_grad,
-        middle_grad_other,
+        third_early,
         entry_in,
         entry_in_other,
         entry_grad,
         swap_rows(entry_grad),
-        flops=ops(2 * pixels, *third_shape),
-    )
-    third = moving_sum(
-        third_parts,
-        third_shape,
-        third_out,
+        flops=ops(2 * pixels, wide_in // 2, mid),
+    )
+
+    second_result = ((9, wider // 2, wider), F32)
+
+    def most(second_parts, third_parts):
+        order = [third_parts[0]]
+        waves = {
+            "b": sum_over_chips(
+                order, second_parts[:2], second_parts[2:], 1, second_shape, (second_out, [second_result])
+            ),
+            "c": sum_over_chips(order, third_parts[:2], third_parts[2:], 0, third_shape),
+        }
+        sums = {}
+        for name in "bc" + 16 * "bc":
+            if name not in sums:
+                result = next(waves[name])
+                if result is not None:
+                    sums[name] = list(result)
+        return sums["b"], sums["c"]
+
+    def none(second_parts, third_parts):
+        del second_parts, third_parts
+        half = (third_shape[0] // 2, third_shape[1] // 2)
+        return [jnp.zeros(*second_result)], [jnp.zeros(half, BF16)] * 2
+
+    (strided_total,), third_own = lax.cond(local[0, 1] > 0, most, none, [*second_kept, *second_sent], list(third_parts))
+    third_got = exchange(third_own, steps()[0])
+    shortcut_total, expand_total = call(
+        first_out,
+        [((wide_in // 2, last), F32), ((wider // 2, last), F32)],
+        first,
+        late=None,
+        after=(third_own[0],),
+    )
+    order[0] = shortcut_total
+    widen_total, closing_total, middle_total, entry_total = run_after(
+        order,
+        functools.partial(out_kernel, third_out, steps()[0]),
         [
             ((wide_in // 2, wider), F32),
             ((mid // 2, wide_in), F32),
             ((9, mid // 2, mid), F32),
             ((wide_in // 2, mid), F32),
         ],
-    )
-    totals = {}
-    for name in "bcbcbcbcbcbac":
-        if name == "a":
-            totals["a"] = call(
-                first_out,
-                [((wide_in // 2, last), F32), ((wider // 2, last), F32)],
-                first,
-                late=None,
-                after=(order[0],),
-            )
-            order[0] = totals["a"][0]
-        elif name not in totals:
-            result = move(second if name == "b" else third)
-            if result is not None:
-                totals[name] = result
-    for name, moving in (("b", second), ("c", third)):
-        while name not in totals:
-            result = move(moving)
-            if result is not None:
-                totals[name] = result
-    shortcut_total, expand_total = totals["a"]
-    (strided_total,) = totals["b"]
-    widen_total, closing_total, middle_total, entry_total = totals["c"]
+        *third_own,
+        *third_got,
+        scratch=[(third_shape, BF16)],
+        free=False,
+    )
     middle_total = middle_total.reshape(3, 3, mid // 2, mid)
     strided_total = strided_total.reshape(3, 3, wider // 2, wider)
     return (

time: 363 us -> 350 us (0.964)
  starting transfers between devices: 76 us -> 63.8 us
  local copies, waits for them, and re-layouts: 23 us -> 10.8 us
  waiting for transfers between devices: 114 us -> 125 us
    ppermute x28 -> x24, waiting for transfers between devices: 54.1 us -> 78.9 us  [to_chip(): return lax.ppermute(value, 'img', [(i, i ^ 1 << bit) for i in range(count)])]
    unnamed x123 -> x87, local copies, waits for them, and re-layouts: 23 us -> 10.2 us
    ppermute x28 -> x24, starting transfers between devices: 38.8 us -> 27.8 us  [to_chip(): return lax.ppermute(value, 'img', [(i, i ^ 1 << bit) for i in range(count)])]
    psum x1, waiting for transfers between devices: 9.51 us -> 0.01 us  [per_device(): first = lax.psum(first, 'img')]
    all_to_all x8, waiting for transfers between devices: 39.8 us -> 36.1 us  [gather_all(): return lax.all_to_all(message, BOTH, 0, 0, tiled=True)]
    pallas_call x33 -> x38, Pallas kernels: 83.2 us -> 84.6 us  [call(): pl.pallas_call(body, out_shape=[jax.ShapeDtypeStruct(shape, dtype) if fre...]
  transfers between devices with their start and end apart: 59 -> 55, of which waited for: 31 -> 37; matrix products, arithmetic and copies ran while one was open for 0% -> 0% of each run, Pallas kernels for 14% -> 15%
where the time goes in v3:
time: 350 us; the launch traced here: 349 us
  waiting for transfers between devices  125 us (36%)
  Pallas kernels  84.6 us (24%)
  starting transfers between devices  63.8 us (18%)
  blocking collectives  49.2 us (14%)
  between operations  15.3 us (4%)
  local copies, waits for them, and re-layouts  10.8 us (3%)
    pallas_call x38, Pallas kernels, call(): pl.pallas_call(body, out_shape=[jax.ShapeDtypeStruct(shape, dtype) if fre...  84.6 us
    ppermute x24, waiting for transfers between devices, to_chip(): return lax.ppermute(value, 'img', [(i, i ^ 1 << bit) for i in range(count)])  78.9 us
    all_to_all x8, waiting for transfers between devices, gather_all(): return lax.all_to_all(message, BOTH, 0, 0, tiled=True)  36.1 us
    all_to_all x8, starting transfers between devices, gather_all(): return lax.all_to_all(message, BOTH, 0, 0, tiled=True)  31.3 us
    ppermute x24, starting transfers between devices, to_chip(): return lax.ppermute(value, 'img', [(i, i ^ 1 << bit) for i in range(count)])  27.8 us
    all_to_all x2, blocking collectives, gather_img(): return lax.all_to_all(message, 'img', 0, 0, tiled=True)  26.8 us
    all_to_all x2, blocking collectives, gather_all(): return lax.all_to_all(message, BOTH, 0, 0, tiled=True)  22.4 us
    unnamed x87, local copies, waits for them, and re-layouts  10.2 us
  transfers between devices with their start and end apart: 55, of which 37 were waited for; matrix products, arithmetic and copies ran while one was open for 0% of the time, Pallas kernels for 15%

profile of v3, /device:TPU:0, one launch (start us, length us, event | category | flops | bytes accessed | tf_op | source)
XLA Modules:
  0.0 348.5 jit_solution(10296219353772470446)
XLA Ops:
  11.8 7.3 %all-to-all-start = ((f32[32,8,128]{2,1,0:T(8,128)}), f32[32,8,128]{2,1,0:T(8,128)S(1)}, u32[]{:S(2)}, u32[]{:S(2)}) async-start(f32[32,8,128]{2,1,0:T(8,128)} %get-tuple-element.169), calls=%async_computation | async-start | bytes 262144 | tf_op jit(solution)/shard_map/all_to_all | solution.py:25
  20.4 6.9 %all-to-all-done.refs_0_.refs_1_.refs_2_ = f32[32,8,128]{2,1,0:T(8,128)S(1)} async-done(((f32[32,8,128]{2,1,0:T(8,128)}), f32[32,8,128]{2,1,0:T(8,128)S(1)}, u32[]{:S(2)}, u32[]{:S(2)}) %all-to-all-start) | async-done | bytes 131104 | tf_op jit(solution)/shard_map/all_to_all | solution.py:25
  32.8 10.0 %all_to_all.60.refs_0_ = f32[32,8,128]{2,1,0:T(8,128)S(1)} all-to-all(f32[32,8,128]{2,1,0:T(8,128)S(1)} %get-tuple-element.175), channel_id=1, replica_groups=mesh['img'=16,'row'=2] {'img','row'}, dimensions={0} | all-to-all | bytes 262144 | tf_op jit(solution)/shard_map/all_to_all | solution.py:25
  44.6 12.4 %all_to_all.61.refs_0_ = f32[32,16,128]{2,1,0:T(8,128)S(1)} all-to-all(f32[32,16,128]{2,1,0:T(8,128)S(1)} %get-tuple-element.177), channel_id=1, replica_groups=mesh['img'=16,'row'=2] {'img','row'}, dimensions={0} | all-to-all | bytes 524288 | tf_op jit(solution)/shard_map/all_to_all | solution.py:25
  57.0 4.9 %shard_map.291 = (bf16[384,1024]{1,0:T(8,128)(2,1)}, f32[384,1024]{1,0:T(8,128)}, f32[384,1024]{1,0:T(8,128)}, f32[8,1024]{1,0:T(8,128)}, bf16[96,1024]{1,0:T(8,...) custom-call(f32[32,16,128]{2,1,0:T(8,128)S(1)} %all_to_all.61.refs_0, ...), custom_call_target="tpu_custom_call" | custom-call | flops 402653184 | bytes 9674752 | tf_op jit(solution)/shard_map/pallas_call | solution.py:129
  65.9 6.9 %all-to-all-done.3.refs_0_ = f32[32,8,128]{2,1,0:T(8,128)S(1)} async-done(((f32[32,8,128]{2,1,0:T(8,128)}), f32[32,8,128]{2,1,0:T(8,128)S(1)}, u32[]{:S(2)}, u32[]{:S(2)}) %all-to-all-start.3) | async-done | bytes 131104 | tf_op jit(solution)/shard_map/all_to_all | solution.py:25
  92.0 14.6 %all_to_all.62.refs_0_ = f32[16,40,128]{2,1,0:T(8,128)S(1)} all-to-all(f32[16,40,128]{2,1,0:T(8,128)S(1)} %shard_map.295), channel_id=1, replica_groups=mesh['img'=16,'row'=2] {'img'}, dimensions={0} | all-to-all | bytes 655360 | tf_op jit(solution)/shard_map/all_to_all | solution.py:29
  112.2 12.2 %all_to_all.63 = f32[16,24,128]{2,1,0:T(8,128)S(1)} all-to-all(f32[16,24,128]{2,1,0:T(8,128)S(1)} %broadcast_in_dim.2), channel_id=1, replica_groups=mesh['img'=16,'row'=2] {'img'}, dimensions={0} | all-to-all | bytes 393216 | tf_op jit(solution)/shard_map/all_to_all | solution.py:29
  135.3 5.1 %shard_map.299.refs_12_ = bf16[768,2048]{1,0:T(8,128)(2,1)} custom-call(bf16[96,1024]{1,0:T(8,128)(2,1)} %get-tuple-element.186.refs_0_, bf16[96,512]{1,0:T(8,128)(2,1)} %copy-done.33, bf16[96,512]{1,0:T(8,128)(2,1)} %get-tuple-element.210.refs_2_, bf16[96,256]{1,0:T(8,128)(2,1)} %copy-done.34, bf16[96,2048]{1,0:T(8,128)(2,1)} %get-tuple-element.212.refs_4_.refs_0_, ...), custom_call_target="tpu_custom_call" | custom-call | flops 603979776 | bytes 5177344 | tf_op jit(solution)/shard_map/pallas_call | solution.py:129
  141.2 4.9 %shard_map.300 = (f32[2,512]{1,0:T(2,128)}, bf16[96,512]{1,0:T(8,128)(2,1)}, f32[384,512]{1,0:T(8,128)S(1)}, f32[32,8,128]{2,1,0:T(8,128)}) custom-call(f32[32,8,128]{2,1,0:T(8,128)S(1)} %all-to-all-done.7.refs_0_, f32[32,8,128]{2,1,0:T(8,128)S(1)} %all-to-all-done.refs_0_.refs_1_.refs_2_, f32[96,512]{1,0:T(8,128)S(1)} %copy-done.8, ...), custom_call_target="tpu_custom_call" | custom-call | flops 452984832 | bytes 11292672 | tf_op jit(solution)/shard_map/pallas_call | solution.py:129
  146.8 5.2 %all-to-all-start.8 = ((f32[32,8,128]{2,1,0:T(8,128)}), f32[32,8,128]{2,1,0:T(8,128)S(1)}, u32[]{:S(2)}, u32[]{:S(2)}) async-start(f32[32,8,128]{2,1,0:T(8,128)} %get-tuple-element.215), calls=%async_computation.8 | async-start | bytes 262144 | tf_op jit(solution)/shard_map/all_to_all | solution.py:25
  152.0 5.0 %shard_map.301.refs_8_.refs_11_ = f32[8,384,128]{2,1,0:T(8,128)} custom-call(bf16[96,2048]{1,0:T(8,128)(2,1)} %get-tuple-element.212.refs_4_.refs_0_, bf16[1024,2048]{1,0:T(8,128)(2,1)} %refs_1_.1, f32[2,512]{1,0:T(2,128)} %get-tuple-element.166.refs_2_), custom_call_target="tpu_custom_call" | custom-call | flops 402653184 | bytes 6164480 | tf_op jit(solution)/shard_map/pallas_call | solution.py:129
  160.2 5.7 %shard_map.302 = (f32[2,512]{1,0:T(2,128)}, bf16[384,512]{1,0:T(8,128)(2,1)}, f32[384,1024]{1,0:T(8,128)S(1)}, f32[32,16,128]{2,1,0:T(8,128)}, f32[384,1024]{1,0:T(8,128)}) custom-call(f32[32,8,128]{2,1,0:T(8,128)S(1)} %all-to-all-done.8.refs_0_, f32[32,8,128]{2,1,0:T(8,128)S(1)} %all-to-all-done.refs_0_.refs_1_.refs_2_, ...), custom_call_target="tpu_custom_call" | custom-call | flops 402653184 | bytes 13197312 | tf_op jit(solution)/shard_map/pallas_call | solution.py:129
  177.1 9.0 %all-to-all-done.9.refs_0_ = f32[32,16,128]{2,1,0:T(8,128)S(1)} async-done(((f32[32,16,128]{2,1,0:T(8,128)}), f32[32,16,128]{2,1,0:T(8,128)S(1)}, u32[]{:S(2)}, u32[]{:S(2)}) %all-to-all-start.9) | async-done | bytes 262176 | tf_op jit(solution)/shard_map/all_to_all | solution.py:25
  198.8 5.0 %all-to-all-done.10.refs_0_ = f32[32,8,128]{2,1,0:T(8,128)S(1)} async-done(((f32[32,8,128]{2,1,0:T(8,128)}), f32[32,8,128]{2,1,0:T(8,128)S(1)}, u32[]{:S(2)}, u32[]{:S(2)}) %all-to-all-start.10) | async-done | bytes 131104 | tf_op jit(solution)/shard_map/all_to_all | solution.py:25
  212.3 5.3 %shard_map.306.refs_4_.refs_0_ = bf16[2688,256]{1,0:T(8,128)(2,1)} custom-call(bf16[384,1024]{1,0:T(8,128)(2,1)} %get-tuple-element.245.refs_0_, bf16[384,512]{1,0:T(8,128)(2,1)} %collective-permute-done.36.refs_1_, bf16[384,512]{1,0:T(8,128)(2,1)} %get-tuple-element.247.refs_2_, bf16[384,512]{1,0:T(8,128)(2,1)} %collective-permute-done.37.refs_3_, ...), custom_call_target="tpu_custom_call" | custom-call | flops 1308622848 | bytes 6711296 | tf_op jit(solution)/shard_map/pallas_call | solution.py:129
  228.4 99.8 %conditional.1 = (bf16[1664,128]{1,0:T(8,128)(2,1)S(1)}, bf16[1664,128]{1,0:T(8,128)(2,1)S(1)}, f32[3,3,256,512]{3,2,1,0:T(8,128)}) conditional(s32[]{:T(128)} %bitcast.8, () %tuple.18, (bf16[1664,128]{1,0:T(8,128)(2,1)S(1)}, bf16[1664,128]{1,0:T(8,128)(2,1)S(1)}, bf16[576,256]{1,0:T(8,128)(2,1)S(1)}, bf16[576,256]{1,0:T(8,128)(2,1)S(1)}, ...), branch_computations={%region_1.0_spmd, %region_2.0_spmd} | conditional | bytes 52405048 | solution.py:1599
  232.5 5.8 %collective-permute-done.2.refs_2_ = bf16[576,256]{1,0:T(8,128)(2,1)S(1)} collective-permute-done((bf16[576,256]{1,0:T(8,128)(2,1)S(1)}, bf16[576,256]{1,0:T(8,128)(2,1)S(1)}, u32[]{:S(2)}, u32[]{:S(2)}) %collective-permute-start.2) | collective-permute-done | bytes 294944 | tf_op jit(solution)/shard_map/cond/branch_1_fun/ppermute | solution.py:1010
  240.9 7.8 %collective-permute-done.refs_2_ = bf16[1664,128]{1,0:T(8,128)(2,1)S(1)} collective-permute-done((bf16[1664,128]{1,0:T(8,128)(2,1)S(1)}, bf16[1664,128]{1,0:T(8,128)(2,1)S(1)}, u32[]{:S(2)}, u32[]{:S(2)}) %collective-permute-start) | collective-permute-done | bytes 426016 | tf_op jit(solution)/shard_map/cond/branch_1_fun/ppermute | solution.py:1010
  264.8 9.2 %collective-permute-done.10.refs_1_ = bf16[2,144,256]{2,1,0:T(8,128)(2,1)S(1)} collective-permute-done((bf16[2,144,256]{2,1,0:T(8,128)(2,1)S(1)}, bf16[2,144,256]{2,1,0:T(8,128)(2,1)S(1)}, u32[]{:S(2)}, u32[]{:S(2)}) %collective-permute-start.10) | collective-permute-done | bytes 147488 | tf_op jit(solution)/shard_map/cond/branch_1_fun/ppermute | solution.py:1010
  276.6 5.8 %collective-permute-done.9.refs_1_ = bf16[2,208,128]{2,1,0:T(8,128)(2,1)S(1)} collective-permute-done((bf16[2,208,128]{2,1,0:T(8,128)(2,1)S(1)}, bf16[2,208,128]{2,1,0:T(8,128)(2,1)S(1)}, u32[]{:S(2)}, u32[]{:S(2)}) %collective-permute-start.9) | collective-permute-done | bytes 106528 | tf_op jit(solution)/shard_map/cond/branch_1_fun/ppermute | solution.py:1010
  288.7 13.4 %collective-permute-done.11.refs_1_ = bf16[2,208,128]{2,1,0:T(8,128)(2,1)S(1)} collective-permute-done((bf16[2,208,128]{2,1,0:T(8,128)(2,1)S(1)}, bf16[2,208,128]{2,1,0:T(8,128)(2,1)S(1)}, u32[]{:S(2)}, u32[]{:S(2)}) %collective-permute-start.11) | collective-permute-done | bytes 106528 | tf_op jit(solution)/shard_map/cond/branch_1_fun/ppermute | solution.py:1010
  303.9 16.0 %collective-permute-done.13.refs_1_ = bf16[2,416,128]{2,1,0:T(8,128)(2,1)S(1)} collective-permute-done((bf16[2,416,128]{2,1,0:T(8,128)(2,1)S(1)}, bf16[2,416,128]{2,1,0:T(8,128)(2,1)S(1)}, u32[]{:S(2)}, u32[]{:S(2)}) %collective-permute-start.13) | collective-permute-done | bytes 213024 | tf_op jit(solution)/shard_map/cond/branch_1_fun/ppermute | solution.py:1010
  330.3 4.9 %shard_map.310 = (f32[512,2048]{1,0:T(8,128)}, f32[256,2048]{1,0:T(8,128)}) custom-call(bf16[768,2048]{1,0:T(8,128)(2,1)} %all-reduce.2.cloned.1.call-done.refs_0_, bf16[1664,128]{1,0:T(8,128)(2,1)S(1)} %get-tuple-element.267.refs_1_.refs_0_), custom_call_target="tpu_custom_call" | custom-call | bytes 9863168 | tf_op jit(solution)/shard_map/pallas_call | solution.py:129
  (223 shorter events, 149.9 us)
Async XLA Ops:
  11.8 15.5 %all-to-all-start = ((f32[32,8,128]{2,1,0:T(8,128)}), f32[32,8,128]{2,1,0:T(8,128)S(1)}, u32[]{:S(2)}, u32[]{:S(2)}) async-start(f32[32,8,128]{2,1,0:T(8,128)} %get-tuple-element.169), calls=%async_computation | async-start | bytes 262144 | tf_op jit(solution)/shard_map/all_to_all | solution.py:25
  61.9 10.8 %all-to-all-start.3 = ((f32[32,8,128]{2,1,0:T(8,128)}), f32[32,8,128]{2,1,0:T(8,128)S(1)}, u32[]{:S(2)}, u32[]{:S(2)}) async-start(f32[32,8,128]{2,1,0:T(8,128)} %get-tuple-element.180), calls=%async_computation.3 | async-start | bytes 262144 | tf_op jit(solution)/shard_map/all_to_all | solution.py:25
  146.0 184.2 %all-reduce.2.cloned.1.call-start = ((), (), s32[]{:S(2)}) async-start(), calls=%async_computation.12 | async-start | bytes 6291456 | tf_op jit(solution)/shard_map/psum | solution.py:1383
  146.8 13.5 %all-to-all-start.8 = ((f32[32,8,128]{2,1,0:T(8,128)}), f32[32,8,128]{2,1,0:T(8,128)S(1)}, u32[]{:S(2)}, u32[]{:S(2)}) async-start(f32[32,8,128]{2,1,0:T(8,128)} %get-tuple-element.215), calls=%async_computation.8 | async-start | bytes 262144 | tf_op jit(solution)/shard_map/all_to_all | solution.py:25
  165.9 20.2 %all-to-all-start.9 = ((f32[32,16,128]{2,1,0:T(8,128)}), f32[32,16,128]{2,1,0:T(8,128)S(1)}, u32[]{:S(2)}, u32[]{:S(2)}) async-start(f32[32,16,128]{2,1,0:T(8,128)} %get-tuple-element.221), calls=%async_computation.9 | async-start | bytes 524288 | tf_op jit(solution)/shard_map/all_to_all | solution.py:25
  169.9 27.4 %collective-permute-start.40 = (bf16[3,160,384]{2,1,0:T(8,128)(2,1)}, bf16[3,160,384]{2,1,0:T(8,128)(2,1)}, u32[]{:S(2)}, u32[]{:S(2)}) collective-permute-start(bf16[3,160,384]{2,1,0:T(8,128)(2,1)} %get-tuple-element.252), channel_id=1, source_target_pairs={{0,1},{1,0},{2,3},{3,2},{4,5},{5,4},{6,7},{7,6},{8,9},{9,8},{10,11... | collective-permute-start | bytes 1105928 | tf_op jit(solution)/shard_map/ppermute | solution.py:21
  190.2 22.0 %collective-permute-start.39 = (bf16[384,1024]{1,0:T(8,128)(2,1)}, bf16[384,1024]{1,0:T(8,128)(2,1)}, u32[]{:S(2)}, u32[]{:S(2)}) collective-permute-start(bf16[384,1024]{1,0:T(8,128)(2,1)} %get-tuple-element.250.refs_6_), channel_id=1, source_target_pairs={{0,1},{1,0},{2,3},{3,2},{4,5},{5,4},{6,7},{7,6},{8,9},{9,8},{10,11... | collective-permute-start | bytes 2359304 | tf_op jit(solution)/shard_map/ppermute | solution.py:21
  190.2 18.2 %collective-permute-start.36 = (bf16[384,512]{1,0:T(8,128)(2,1)}, bf16[384,512]{1,0:T(8,128)(2,1)}, u32[]{:S(2)}, u32[]{:S(2)}) collective-permute-start(bf16[384,512]{1,0:T(8,128)(2,1)} %get-tuple-element.246), channel_id=1, source_target_pairs={{0,1},{1,0},{2,3},{3,2},{4,5},{5,4},{6,7},{7,6},{8,9},{9,8},{10,11... | collective-permute-start | bytes 1179656 | tf_op jit(solution)/shard_map/ppermute | solution.py:21
  191.3 12.5 %all-to-all-start.10 = ((f32[32,8,128]{2,1,0:T(8,128)}), f32[32,8,128]{2,1,0:T(8,128)S(1)}, u32[]{:S(2)}, u32[]{:S(2)}) async-start(f32[32,8,128]{2,1,0:T(8,128)} %get-tuple-element.231), calls=%async_computation.10 | async-start | bytes 262144 | tf_op jit(solution)/shard_map/all_to_all | solution.py:25
  195.4 22.2 %collective-permute-start.34 = (bf16[1152,256]{1,0:T(8,128)(2,1)}, bf16[1152,256]{1,0:T(8,128)(2,1)S(1)}, u32[]{:S(2)}, u32[]{:S(2)}) collective-permute-start(bf16[1152,256]{1,0:T(8,128)(2,1)} %copy-done.26), channel_id=1, source_target_pairs={{0,2},{2,0},{4,6},{6,4},{8,10},{10,8},{12,14},{14,12},{16,18},{18,... | collective-permute-start | bytes 1769480 | tf_op jit(solution)/shard_map/ppermute | solution.py:1010
  197.3 21.3 %collective-permute-start.35 = (bf16[1152,256]{1,0:T(8,128)(2,1)}, bf16[1152,256]{1,0:T(8,128)(2,1)S(1)}, u32[]{:S(2)}, u32[]{:S(2)}) collective-permute-start(bf16[1152,256]{1,0:T(8,128)(2,1)} %copy-done.25), channel_id=1, source_target_pairs={{0,4},{2,6},{4,0},{6,2},{8,12},{10,14},{12,8},{14,10},{16,20},{18,... | collective-permute-start | bytes 1769480 | tf_op jit(solution)/shard_map/ppermute | solution.py:1010
  198.7 13.4 %collective-permute-start.37 = (bf16[384,512]{1,0:T(8,128)(2,1)}, bf16[384,512]{1,0:T(8,128)(2,1)}, u32[]{:S(2)}, u32[]{:S(2)}) collective-permute-start(bf16[384,512]{1,0:T(8,128)(2,1)} %get-tuple-element.247.refs_2_), channel_id=1, source_target_pairs={{0,1},{1,0},{2,3},{3,2},{4,5},{5,4},{6,7},{7,6},{8,9},{9,8},{10,11... | collective-permute-start | bytes 1179656 | tf_op jit(solution)/shard_map/ppermute | solution.py:21
  208.7 11.5 %all-to-all-start.11 = ((f32[32,8,128]{2,1,0:T(8,128)}), f32[32,8,128]{2,1,0:T(8,128)S(1)}, u32[]{:S(2)}, u32[]{:S(2)}) async-start(f32[32,8,128]{2,1,0:T(8,128)} %get-tuple-element.238), calls=%async_computation.11 | async-start | bytes 262144 | tf_op jit(solution)/shard_map/all_to_all | solution.py:25
  212.2 12.6 %collective-permute-start.42 = (bf16[384,512]{1,0:T(8,128)(2,1)}, bf16[384,512]{1,0:T(8,128)(2,1)}, u32[]{:S(2)}, u32[]{:S(2)}) collective-permute-start(bf16[384,512]{1,0:T(8,128)(2,1)} %get-tuple-element.257), channel_id=1, source_target_pairs={{0,1},{1,0},{2,3},{3,2},{4,5},{5,4},{6,7},{7,6},{8,9},{9,8},{10,11... | collective-permute-start | bytes 1179656 | tf_op jit(solution)/shard_map/ppermute | solution.py:21
  230.5 18.2 %collective-permute-start = (bf16[1664,128]{1,0:T(8,128)(2,1)S(1)}, bf16[1664,128]{1,0:T(8,128)(2,1)S(1)}, u32[]{:S(2)}, u32[]{:S(2)}) collective-permute-start(bf16[1664,128]{1,0:T(8,128)(2,1)S(1)} %get-tuple-element.19), channel_id=1, source_target_pairs={{0,2},{2,0},{4,6},{6,4},{8,10},{10,8},{12,14},{14,12},{16,18},{18,... | collective-permute-start | bytes 1277960 | tf_op jit(solution)/shard_map/cond/branch_1_fun/ppermute | solution.py:1010
  231.8 17.0 %collective-permute-start.1 = (bf16[1664,128]{1,0:T(8,128)(2,1)S(1)}, bf16[1664,128]{1,0:T(8,128)(2,1)S(1)}, u32[]{:S(2)}, u32[]{:S(2)}) collective-permute-start(bf16[1664,128]{1,0:T(8,128)(2,1)S(1)} %get-tuple-element.20), channel_id=1, source_target_pairs={{0,4},{2,6},{4,0},{6,2},{8,12},{10,14},{12,8},{14,10},{16,20},{18,... | collective-permute-start | bytes 1277960 | tf_op jit(solution)/shard_map/cond/branch_1_fun/ppermute | solution.py:1010
  239.8 11.3 %collective-permute-start.6 = (bf16[2,288,256]{2,1,0:T(8,128)(2,1)S(1)}, bf16[2,288,256]{2,1,0:T(8,128)(2,1)S(1)}, u32[]{:S(2)}, u32[]{:S(2)}) collective-permute-start(bf16[2,288,256]{2,1,0:T(8,128)(2,1)S(1)} %get-tuple-element.30), channel_id=1, source_target_pairs={{0,8},{2,10},{4,12},{6,14},{8,0},{10,2},{12,4},{14,6},{16,24},{18,... | collective-permute-start | bytes 884744 | tf_op jit(solution)/shard_map/cond/branch_1_fun/ppermute | solution.py:1010
  260.2 13.8 %collective-permute-start.10 = (bf16[2,144,256]{2,1,0:T(8,128)(2,1)S(1)}, bf16[2,144,256]{2,1,0:T(8,128)(2,1)S(1)}, u32[]{:S(2)}, u32[]{:S(2)}) collective-permute-start(bf16[2,144,256]{2,1,0:T(8,128)(2,1)S(1)} %branch_1_fun.18.refs_2_.refs_0_), channel_id=1, source_target_pairs={{0,16},{2,18},{4,20},{6,22},{8,24},{10,26},{12,28},{14,30},{16,0},... | collective-permute-start | bytes 442376 | tf_op jit(solution)/shard_map/cond/branch_1_fun/ppermute | solution.py:1010
  284.1 18.0 %collective-permute-start.14 = (bf16[576,256]{1,0:T(8,128)(2,1)S(1)}, bf16[576,256]{1,0:T(8,128)(2,1)S(1)}, u32[]{:S(2)}, u32[]{:S(2)}) collective-permute-start(bf16[576,256]{1,0:T(8,128)(2,1)S(1)} %get-tuple-element.37.refs_2_.refs_0_), channel_id=1, source_target_pairs={{0,4},{2,6},{4,0},{6,2},{8,12},{10,14},{12,8},{14,10},{16,20},{18,... | collective-permute-start | bytes 884744 | tf_op jit(solution)/shard_map/cond/branch_1_fun/ppermute | solution.py:1010
  284.8 17.3 %collective-permute-start.15 = (bf16[576,256]{1,0:T(8,128)(2,1)S(1)}, bf16[576,256]{1,0:T(8,128)(2,1)S(1)}, u32[]{:S(2)}, u32[]{:S(2)}) collective-permute-start(bf16[576,256]{1,0:T(8,128)(2,1)S(1)} %get-tuple-element.38.refs_1_), channel_id=1, source_target_pairs={{0,2},{2,0},{4,6},{6,4},{8,10},{10,8},{12,14},{14,12},{16,18},{18,... | collective-permute-start | bytes 884744 | tf_op jit(solution)/shard_map/cond/branch_1_fun/ppermute | solution.py:1010
  287.2 14.9 %collective-permute-start.11 = (bf16[2,208,128]{2,1,0:T(8,128)(2,1)S(1)}, bf16[2,208,128]{2,1,0:T(8,128)(2,1)S(1)}, u32[]{:S(2)}, u32[]{:S(2)}) collective-permute-start(bf16[2,208,128]{2,1,0:T(8,128)(2,1)S(1)} %branch_1_fun.21.refs_2_.refs_0_), channel_id=1, source_target_pairs={{0,16},{2,18},{4,20},{6,22},{8,24},{10,26},{12,28},{14,30},{16,0},... | collective-permute-start | bytes 319496 | tf_op jit(solution)/shard_map/cond/branch_1_fun/ppermute | solution.py:1010
  302.2 20.4 %collective-permute-start.18 = (bf16[1152,256]{1,0:T(8,128)(2,1)S(1)}, bf16[1152,256]{1,0:T(8,128)(2,1)S(1)}, u32[]{:S(2)}, u32[]{:S(2)}) collective-permute-start(bf16[1152,256]{1,0:T(8,128)(2,1)S(1)} %get-tuple-element.39.refs_2_.refs_0_), channel_id=1, source_target_pairs={{0,2},{2,0},{4,6},{6,4},{8,10},{10,8},{12,14},{14,12},{16,18},{18,... | collective-permute-start | bytes 1769480 | tf_op jit(solution)/shard_map/cond/branch_1_fun/ppermute | solution.py:1010
  302.3 20.3 %collective-permute-start.19 = (bf16[1152,256]{1,0:T(8,128)(2,1)S(1)}, bf16[1152,256]{1,0:T(8,128)(2,1)S(1)}, u32[]{:S(2)}, u32[]{:S(2)}) collective-permute-start(bf16[1152,256]{1,0:T(8,128)(2,1)S(1)} %get-tuple-element.42.refs_1_), channel_id=1, source_target_pairs={{0,4},{2,6},{4,0},{6,2},{8,12},{10,14},{12,8},{14,10},{16,20},{18,... | collective-permute-start | bytes 1769480 | tf_op jit(solution)/shard_map/cond/branch_1_fun/ppermute | solution.py:1010
  303.9 16.0 %collective-permute-start.13 = (bf16[2,416,128]{2,1,0:T(8,128)(2,1)S(1)}, bf16[2,416,128]{2,1,0:T(8,128)(2,1)S(1)}, u32[]{:S(2)}, u32[]{:S(2)}) collective-permute-start(bf16[2,416,128]{2,1,0:T(8,128)(2,1)S(1)} %branch_1_fun.23.refs_4_.refs_0_), channel_id=1, source_target_pairs={{0,8},{2,10},{4,12},{6,14},{8,0},{10,2},{12,4},{14,6},{16,24},{18,... | collective-permute-start | bytes 638984 | tf_op jit(solution)/shard_map/cond/branch_1_fun/ppermute | solution.py:1010
  (74 other events, 523.9 us)
Sparse Core Ops, SparseCore 0:
  153.0 167.2 all-reduce.1

commit v4 on v3

--- a/solution.py
+++ b/solution.py
@@ -1165,7 +1165,7 @@
         middle_weight.reshape(3, 3 * mid, mid),
         scratch=[rows(mid), ((padded_rows + 16, mid), F32)],
 
-        late=(7,),
+        late=(3, 4, 5, 6, 7),
         keep=(3, 4),
         flops=ops(pixels, 9, mid, mid),
     )
@@ -1348,7 +1348,7 @@
 
     order = [affine_expand]
 
-    def wave_parts(kernel, shape, *operands, flops):
+    def wave_parts(kernel, shape, *operands, flops, free=True):
         parts = call(
             kernel,
             [((shape[0] // 2, shape[1] // 2), BF16)] * 4,
@@ -1356,7 +1356,7 @@
             scratch=[(shape, BF16)],
             flops=flops,
             late=None,
-            free=True,
+            free=free,
             after=(order[0],),
         )
         order[0] = parts[0]
@@ -1460,6 +1460,7 @@
         strided_grad,
         strided_grad_other,
         flops=ops(2 * small_pixels, *second_shape),
+        free=False,
     )
     second_got = exchange(second_parts[2:], steps()[0])
 

time: 350 us -> 346 us (0.989)
  local copies, waits for them, and re-layouts: 10.8 us -> 4.4 us
    unnamed x87 -> x73, local copies, waits for them, and re-layouts: 10.2 us -> 3.8 us
where the time goes in v4:
time: 346 us; the launch traced here: 345 us
  waiting for transfers between devices  127 us (37%)
  Pallas kernels  86.8 us (25%)
  starting transfers between devices  62 us (18%)
  blocking collectives  49.2 us (14%)
  between operations  15.3 us (4%)
  local copies, waits for them, and re-layouts  4.4 us (1%)
    pallas_call x38, Pallas kernels, call(): pl.pallas_call(body, out_shape=[jax.ShapeDtypeStruct(shape, dtype) if fre...  86.8 us
    ppermute x24, waiting for transfers between devices, to_chip(): return lax.ppermute(value, 'img', [(i, i ^ 1 << bit) for i in range(count)])  81 us
    all_to_all x8, waiting for transfers between devices, gather_all(): return lax.all_to_all(message, BOTH, 0, 0, tiled=True)  36.2 us
    all_to_all x8, starting transfers between devices, gather_all(): return lax.all_to_all(message, BOTH, 0, 0, tiled=True)  30.5 us
    all_to_all x2, blocking collectives, gather_img(): return lax.all_to_all(message, 'img', 0, 0, tiled=True)  26.8 us
    ppermute x24, starting transfers between devices, to_chip(): return lax.ppermute(value, 'img', [(i, i ^ 1 << bit) for i in range(count)])  26.5 us
    all_to_all x2, blocking collectives, gather_all(): return lax.all_to_all(message, BOTH, 0, 0, tiled=True)  22.4 us
    ppermute x22, waiting for transfers between devices, swap_rows(): lax.ppermute(value, 'row', [(i, (i + 1) % count) for i in range(count)])  8.82 us
  transfers between devices with their start and end apart: 55, of which 37 were waited for; matrix products, arithmetic and copies ran while one was open for 0% of the time, Pallas kernels for 15%

profile of v4, /device:TPU:0, one launch (start us, length us, event | category | flops | bytes accessed | tf_op | source)
XLA Modules:
  0.0 344.5 jit_solution(7641069780564940722)
XLA Ops:
  11.8 7.3 %all-to-all-start = ((f32[32,8,128]{2,1,0:T(8,128)}), f32[32,8,128]{2,1,0:T(8,128)S(1)}, u32[]{:S(2)}, u32[]{:S(2)}) async-start(f32[32,8,128]{2,1,0:T(8,128)} %get-tuple-element.169), calls=%async_computation | async-start | bytes 262144 | tf_op jit(solution)/shard_map/all_to_all | solution.py:25
  20.4 6.9 %all-to-all-done.refs_0_.refs_1_.refs_2_ = f32[32,8,128]{2,1,0:T(8,128)S(1)} async-done(((f32[32,8,128]{2,1,0:T(8,128)}), f32[32,8,128]{2,1,0:T(8,128)S(1)}, u32[]{:S(2)}, u32[]{:S(2)}) %all-to-all-start) | async-done | bytes 131104 | tf_op jit(solution)/shard_map/all_to_all | solution.py:25
  30.5 10.0 %all_to_all.60.refs_0_ = f32[32,8,128]{2,1,0:T(8,128)S(1)} all-to-all(f32[32,8,128]{2,1,0:T(8,128)S(1)} %get-tuple-element.175), channel_id=1, replica_groups=mesh['img'=16,'row'=2] {'img','row'}, dimensions={0} | all-to-all | bytes 262144 | tf_op jit(solution)/shard_map/all_to_all | solution.py:25
  42.4 12.4 %all_to_all.61.refs_0_ = f32[32,16,128]{2,1,0:T(8,128)S(1)} all-to-all(f32[32,16,128]{2,1,0:T(8,128)S(1)} %get-tuple-element.177), channel_id=1, replica_groups=mesh['img'=16,'row'=2] {'img','row'}, dimensions={0} | all-to-all | bytes 524288 | tf_op jit(solution)/shard_map/all_to_all | solution.py:25
  54.8 4.9 %shard_map.291 = (bf16[384,1024]{1,0:T(8,128)(2,1)}, f32[384,1024]{1,0:T(8,128)}, f32[384,1024]{1,0:T(8,128)}, f32[8,1024]{1,0:T(8,128)}, bf16[96,1024]{1,0:T(8,...) custom-call(f32[32,16,128]{2,1,0:T(8,128)S(1)} %all_to_all.61.refs_0, ...), custom_call_target="tpu_custom_call" | custom-call | flops 402653184 | bytes 9674752 | tf_op jit(solution)/shard_map/pallas_call | solution.py:129
  63.6 6.9 %all-to-all-done.3.refs_0_ = f32[32,8,128]{2,1,0:T(8,128)S(1)} async-done(((f32[32,8,128]{2,1,0:T(8,128)}), f32[32,8,128]{2,1,0:T(8,128)S(1)}, u32[]{:S(2)}, u32[]{:S(2)}) %all-to-all-start.3) | async-done | bytes 131104 | tf_op jit(solution)/shard_map/all_to_all | solution.py:25
  89.7 14.6 %all_to_all.62.refs_0_ = f32[16,40,128]{2,1,0:T(8,128)S(1)} all-to-all(f32[16,40,128]{2,1,0:T(8,128)S(1)} %shard_map.295), channel_id=1, replica_groups=mesh['img'=16,'row'=2] {'img'}, dimensions={0} | all-to-all | bytes 655360 | tf_op jit(solution)/shard_map/all_to_all | solution.py:29
  109.9 12.2 %all_to_all.63 = f32[16,24,128]{2,1,0:T(8,128)S(1)} all-to-all(f32[16,24,128]{2,1,0:T(8,128)S(1)} %broadcast_in_dim.2), channel_id=1, replica_groups=mesh['img'=16,'row'=2] {'img'}, dimensions={0} | all-to-all | bytes 393216 | tf_op jit(solution)/shard_map/all_to_all | solution.py:29
  132.4 5.1 %shard_map.299.refs_12_ = bf16[768,2048]{1,0:T(8,128)(2,1)} custom-call(bf16[96,1024]{1,0:T(8,128)(2,1)} %get-tuple-element.186.refs_0_, bf16[96,512]{1,0:T(8,128)(2,1)} %copy-done.26, bf16[96,512]{1,0:T(8,128)(2,1)} %get-tuple-element.210.refs_2_, bf16[96,256]{1,0:T(8,128)(2,1)} %copy-done.27, bf16[96,2048]{1,0:T(8,128)(2,1)} %get-tuple-element.212.refs_4_.refs_0_, ...), custom_call_target="tpu_custom_call" | custom-call | flops 603979776 | bytes 5177344 | tf_op jit(solution)/shard_map/pallas_call | solution.py:129
  138.2 4.9 %shard_map.300 = (f32[2,512]{1,0:T(2,128)}, bf16[96,512]{1,0:T(8,128)(2,1)}, f32[384,512]{1,0:T(8,128)S(1)}, f32[32,8,128]{2,1,0:T(8,128)}) custom-call(f32[32,8,128]{2,1,0:T(8,128)S(1)} %all-to-all-done.7.refs_0_, f32[32,8,128]{2,1,0:T(8,128)S(1)} %all-to-all-done.refs_0_.refs_1_.refs_2_, f32[96,512]{1,0:T(8,128)S(1)} %get-tuple-element.203.refs_2_, ...), custom_call_target="tpu_custom_call" | custom-call | flops 452984832 | bytes 11292672 | tf_op jit(solution)/shard_map/pallas_call | solution.py:129
  143.9 5.1 %all-to-all-start.8 = ((f32[32,8,128]{2,1,0:T(8,128)}), f32[32,8,128]{2,1,0:T(8,128)S(1)}, u32[]{:S(2)}, u32[]{:S(2)}) async-start(f32[32,8,128]{2,1,0:T(8,128)} %get-tuple-element.215), calls=%async_computation.8 | async-start | bytes 262144 | tf_op jit(solution)/shard_map/all_to_all | solution.py:25
  149.0 5.0 %shard_map.301.refs_8_.refs_11_ = f32[8,384,128]{2,1,0:T(8,128)} custom-call(bf16[96,2048]{1,0:T(8,128)(2,1)} %get-tuple-element.212.refs_4_.refs_0_, bf16[1024,2048]{1,0:T(8,128)(2,1)} %refs_1_.1, f32[2,512]{1,0:T(2,128)} %get-tuple-element.166.refs_2_), custom_call_target="tpu_custom_call" | custom-call | flops 402653184 | bytes 6164480 | tf_op jit(solution)/shard_map/pallas_call | solution.py:129
  157.2 5.6 %shard_map.302 = (f32[2,512]{1,0:T(2,128)}, bf16[384,512]{1,0:T(8,128)(2,1)}, f32[384,1024]{1,0:T(8,128)S(1)}, f32[32,16,128]{2,1,0:T(8,128)}, f32[384,1024]{1,0:T(8,128)}) custom-call(f32[32,8,128]{2,1,0:T(8,128)S(1)} %all-to-all-done.8.refs_0_, f32[32,8,128]{2,1,0:T(8,128)S(1)} %all-to-all-done.refs_0_.refs_1_.refs_2_, ...), custom_call_target="tpu_custom_call" | custom-call | flops 402653184 | bytes 13197312 | tf_op jit(solution)/shard_map/pallas_call | solution.py:129
  174.0 9.1 %all-to-all-done.9.refs_0_ = f32[32,16,128]{2,1,0:T(8,128)S(1)} async-done(((f32[32,16,128]{2,1,0:T(8,128)}), f32[32,16,128]{2,1,0:T(8,128)S(1)}, u32[]{:S(2)}, u32[]{:S(2)}) %all-to-all-start.9) | async-done | bytes 262176 | tf_op jit(solution)/shard_map/all_to_all | solution.py:25
  195.2 5.0 %all-to-all-done.10.refs_0_ = f32[32,8,128]{2,1,0:T(8,128)S(1)} async-done(((f32[32,8,128]{2,1,0:T(8,128)}), f32[32,8,128]{2,1,0:T(8,128)S(1)}, u32[]{:S(2)}, u32[]{:S(2)}) %all-to-all-start.10) | async-done | bytes 131104 | tf_op jit(solution)/shard_map/all_to_all | solution.py:25
  207.8 5.4 %shard_map.306.refs_4_.refs_0_ = bf16[2688,256]{1,0:T(8,128)(2,1)} custom-call(bf16[384,1024]{1,0:T(8,128)(2,1)} %get-tuple-element.245.refs_0_, bf16[384,512]{1,0:T(8,128)(2,1)} %collective-permute-done.36.refs_1_, bf16[384,512]{1,0:T(8,128)(2,1)} %get-tuple-element.247.refs_2_, bf16[384,512]{1,0:T(8,128)(2,1)} %collective-permute-done.37.refs_3_, ...), custom_call_target="tpu_custom_call" | custom-call | flops 1308622848 | bytes 6711296 | tf_op jit(solution)/shard_map/pallas_call | solution.py:129
  224.5 99.8 %conditional.1 = (bf16[1664,128]{1,0:T(8,128)(2,1)S(1)}, bf16[1664,128]{1,0:T(8,128)(2,1)S(1)}, f32[3,3,256,512]{3,2,1,0:T(8,128)}) conditional(s32[]{:T(128)} %bitcast.8, () %tuple.18, (bf16[1664,128]{1,0:T(8,128)(2,1)S(1)}, bf16[1664,128]{1,0:T(8,128)(2,1)S(1)}, bf16[576,256]{1,0:T(8,128)(2,1)S(1)}, bf16[576,256]{1,0:T(8,128)(2,1)S(1)}, ...), branch_computations={%region_1.0_spmd, %region_2.0_spmd} | conditional | bytes 52405048 | solution.py:1600
  228.6 5.8 %collective-permute-done.2.refs_2_ = bf16[576,256]{1,0:T(8,128)(2,1)S(1)} collective-permute-done((bf16[576,256]{1,0:T(8,128)(2,1)S(1)}, bf16[576,256]{1,0:T(8,128)(2,1)S(1)}, u32[]{:S(2)}, u32[]{:S(2)}) %collective-permute-start.2) | collective-permute-done | bytes 294944 | tf_op jit(solution)/shard_map/cond/branch_1_fun/ppermute | solution.py:1010
  237.2 7.7 %collective-permute-done.refs_2_ = bf16[1664,128]{1,0:T(8,128)(2,1)S(1)} collective-permute-done((bf16[1664,128]{1,0:T(8,128)(2,1)S(1)}, bf16[1664,128]{1,0:T(8,128)(2,1)S(1)}, u32[]{:S(2)}, u32[]{:S(2)}) %collective-permute-start) | collective-permute-done | bytes 426016 | tf_op jit(solution)/shard_map/cond/branch_1_fun/ppermute | solution.py:1010
  260.6 9.7 %collective-permute-done.10.refs_1_ = bf16[2,144,256]{2,1,0:T(8,128)(2,1)S(1)} collective-permute-done((bf16[2,144,256]{2,1,0:T(8,128)(2,1)S(1)}, bf16[2,144,256]{2,1,0:T(8,128)(2,1)S(1)}, u32[]{:S(2)}, u32[]{:S(2)}) %collective-permute-start.10) | collective-permute-done | bytes 147488 | tf_op jit(solution)/shard_map/cond/branch_1_fun/ppermute | solution.py:1010
  272.5 6.2 %collective-permute-done.9.refs_1_ = bf16[2,208,128]{2,1,0:T(8,128)(2,1)S(1)} collective-permute-done((bf16[2,208,128]{2,1,0:T(8,128)(2,1)S(1)}, bf16[2,208,128]{2,1,0:T(8,128)(2,1)S(1)}, u32[]{:S(2)}, u32[]{:S(2)}) %collective-permute-start.9) | collective-permute-done | bytes 106528 | tf_op jit(solution)/shard_map/cond/branch_1_fun/ppermute | solution.py:1010
  285.1 13.2 %collective-permute-done.11.refs_1_ = bf16[2,208,128]{2,1,0:T(8,128)(2,1)S(1)} collective-permute-done((bf16[2,208,128]{2,1,0:T(8,128)(2,1)S(1)}, bf16[2,208,128]{2,1,0:T(8,128)(2,1)S(1)}, u32[]{:S(2)}, u32[]{:S(2)}) %collective-permute-start.11) | collective-permute-done | bytes 106528 | tf_op jit(solution)/shard_map/cond/branch_1_fun/ppermute | solution.py:1010
  299.8 16.1 %collective-permute-done.13.refs_1_ = bf16[2,416,128]{2,1,0:T(8,128)(2,1)S(1)} collective-permute-done((bf16[2,416,128]{2,1,0:T(8,128)(2,1)S(1)}, bf16[2,416,128]{2,1,0:T(8,128)(2,1)S(1)}, u32[]{:S(2)}, u32[]{:S(2)}) %collective-permute-start.13) | collective-permute-done | bytes 213024 | tf_op jit(solution)/shard_map/cond/branch_1_fun/ppermute | solution.py:1010
  326.3 4.9 %shard_map.310 = (f32[512,2048]{1,0:T(8,128)}, f32[256,2048]{1,0:T(8,128)}) custom-call(bf16[768,2048]{1,0:T(8,128)(2,1)} %all-reduce.2.cloned.1.call-done.refs_0_, bf16[1664,128]{1,0:T(8,128)(2,1)S(1)} %get-tuple-element.267.refs_1_.refs_0_), custom_call_target="tpu_custom_call" | custom-call | bytes 9863168 | tf_op jit(solution)/shard_map/pallas_call | solution.py:129
  (209 shorter events, 145.2 us)
Async XLA Ops:
  11.8 15.5 %all-to-all-start = ((f32[32,8,128]{2,1,0:T(8,128)}), f32[32,8,128]{2,1,0:T(8,128)S(1)}, u32[]{:S(2)}, u32[]{:S(2)}) async-start(f32[32,8,128]{2,1,0:T(8,128)} %get-tuple-element.169), calls=%async_computation | async-start | bytes 262144 | tf_op jit(solution)/shard_map/all_to_all | solution.py:25
  59.6 10.8 %all-to-all-start.3 = ((f32[32,8,128]{2,1,0:T(8,128)}), f32[32,8,128]{2,1,0:T(8,128)S(1)}, u32[]{:S(2)}, u32[]{:S(2)}) async-start(f32[32,8,128]{2,1,0:T(8,128)} %get-tuple-element.180), calls=%async_computation.3 | async-start | bytes 262144 | tf_op jit(solution)/shard_map/all_to_all | solution.py:25
  143.1 183.2 %all-reduce.2.cloned.1.call-start = ((), (), s32[]{:S(2)}) async-start(), calls=%async_computation.12 | async-start | bytes 6291456 | tf_op jit(solution)/shard_map/psum | solution.py:1383
  143.9 13.4 %all-to-all-start.8 = ((f32[32,8,128]{2,1,0:T(8,128)}), f32[32,8,128]{2,1,0:T(8,128)S(1)}, u32[]{:S(2)}, u32[]{:S(2)}) async-start(f32[32,8,128]{2,1,0:T(8,128)} %get-tuple-element.215), calls=%async_computation.8 | async-start | bytes 262144 | tf_op jit(solution)/shard_map/all_to_all | solution.py:25
  162.9 20.2 %all-to-all-start.9 = ((f32[32,16,128]{2,1,0:T(8,128)}), f32[32,16,128]{2,1,0:T(8,128)S(1)}, u32[]{:S(2)}, u32[]{:S(2)}) async-start(f32[32,16,128]{2,1,0:T(8,128)} %get-tuple-element.221), calls=%async_computation.9 | async-start | bytes 524288 | tf_op jit(solution)/shard_map/all_to_all | solution.py:25
  166.8 26.9 %collective-permute-start.40 = (bf16[3,160,384]{2,1,0:T(8,128)(2,1)}, bf16[3,160,384]{2,1,0:T(8,128)(2,1)}, u32[]{:S(2)}, u32[]{:S(2)}) collective-permute-start(bf16[3,160,384]{2,1,0:T(8,128)(2,1)} %get-tuple-element.252), channel_id=1, source_target_pairs={{0,1},{1,0},{2,3},{3,2},{4,5},{5,4},{6,7},{7,6},{8,9},{9,8},{10,11... | collective-permute-start | bytes 1105928 | tf_op jit(solution)/shard_map/ppermute | solution.py:21
  186.5 20.6 %collective-permute-start.39 = (bf16[384,1024]{1,0:T(8,128)(2,1)}, bf16[384,1024]{1,0:T(8,128)(2,1)}, u32[]{:S(2)}, u32[]{:S(2)}) collective-permute-start(bf16[384,1024]{1,0:T(8,128)(2,1)} %get-tuple-element.250.refs_6_), channel_id=1, source_target_pairs={{0,1},{1,0},{2,3},{3,2},{4,5},{5,4},{6,7},{7,6},{8,9},{9,8},{10,11... | collective-permute-start | bytes 2359304 | tf_op jit(solution)/shard_map/ppermute | solution.py:21
  186.6 17.3 %collective-permute-start.36 = (bf16[384,512]{1,0:T(8,128)(2,1)}, bf16[384,512]{1,0:T(8,128)(2,1)}, u32[]{:S(2)}, u32[]{:S(2)}) collective-permute-start(bf16[384,512]{1,0:T(8,128)(2,1)} %get-tuple-element.246), channel_id=1, source_target_pairs={{0,1},{1,0},{2,3},{3,2},{4,5},{5,4},{6,7},{7,6},{8,9},{9,8},{10,11... | collective-permute-start | bytes 1179656 | tf_op jit(solution)/shard_map/ppermute | solution.py:21
  187.6 12.6 %all-to-all-start.10 = ((f32[32,8,128]{2,1,0:T(8,128)}), f32[32,8,128]{2,1,0:T(8,128)S(1)}, u32[]{:S(2)}, u32[]{:S(2)}) async-start(f32[32,8,128]{2,1,0:T(8,128)} %get-tuple-element.231), calls=%async_computation.10 | async-start | bytes 262144 | tf_op jit(solution)/shard_map/all_to_all | solution.py:25
  191.9 22.1 %collective-permute-start.34 = (bf16[1152,256]{1,0:T(8,128)(2,1)}, bf16[1152,256]{1,0:T(8,128)(2,1)S(1)}, u32[]{:S(2)}, u32[]{:S(2)}) collective-permute-start(bf16[1152,256]{1,0:T(8,128)(2,1)} %get-tuple-element.243), channel_id=1, source_target_pairs={{0,2},{2,0},{4,6},{6,4},{8,10},{10,8},{12,14},{14,12},{16,18},{18,... | collective-permute-start | bytes 1769480 | tf_op jit(solution)/shard_map/ppermute | solution.py:1010
  193.7 21.4 %collective-permute-start.35 = (bf16[1152,256]{1,0:T(8,128)(2,1)}, bf16[1152,256]{1,0:T(8,128)(2,1)S(1)}, u32[]{:S(2)}, u32[]{:S(2)}) collective-permute-start(bf16[1152,256]{1,0:T(8,128)(2,1)} %get-tuple-element.244), channel_id=1, source_target_pairs={{0,4},{2,6},{4,0},{6,2},{8,12},{10,14},{12,8},{14,10},{16,20},{18,... | collective-permute-start | bytes 1769480 | tf_op jit(solution)/shard_map/ppermute | solution.py:1010
  195.2 11.7 %collective-permute-start.37 = (bf16[384,512]{1,0:T(8,128)(2,1)S(1)}, bf16[384,512]{1,0:T(8,128)(2,1)}, u32[]{:S(2)}, u32[]{:S(2)}) collective-permute-start(bf16[384,512]{1,0:T(8,128)(2,1)S(1)} %copy-done.19), channel_id=1, source_target_pairs={{0,1},{1,0},{2,3},{3,2},{4,5},{5,4},{6,7},{7,6},{8,9},{9,8},{10,11... | collective-permute-start | bytes 1179656 | tf_op jit(solution)/shard_map/ppermute | solution.py:21
  204.1 12.2 %all-to-all-start.11 = ((f32[32,8,128]{2,1,0:T(8,128)}), f32[32,8,128]{2,1,0:T(8,128)S(1)}, u32[]{:S(2)}, u32[]{:S(2)}) async-start(f32[32,8,128]{2,1,0:T(8,128)} %get-tuple-element.238), calls=%async_computation.11 | async-start | bytes 262144 | tf_op jit(solution)/shard_map/all_to_all | solution.py:25
  206.9 14.0 %collective-permute-start.42 = (bf16[384,512]{1,0:T(8,128)(2,1)}, bf16[384,512]{1,0:T(8,128)(2,1)S(1)}, u32[]{:S(2)}, u32[]{:S(2)}) collective-permute-start(bf16[384,512]{1,0:T(8,128)(2,1)} %get-tuple-element.257), channel_id=1, source_target_pairs={{0,1},{1,0},{2,3},{3,2},{4,5},{5,4},{6,7},{7,6},{8,9},{9,8},{10,11... | collective-permute-start | bytes 1179656 | tf_op jit(solution)/shard_map/ppermute | solution.py:21
  226.5 18.4 %collective-permute-start = (bf16[1664,128]{1,0:T(8,128)(2,1)S(1)}, bf16[1664,128]{1,0:T(8,128)(2,1)S(1)}, u32[]{:S(2)}, u32[]{:S(2)}) collective-permute-start(bf16[1664,128]{1,0:T(8,128)(2,1)S(1)} %get-tuple-element.19), channel_id=1, source_target_pairs={{0,2},{2,0},{4,6},{6,4},{8,10},{10,8},{12,14},{14,12},{16,18},{18,... | collective-permute-start | bytes 1277960 | tf_op jit(solution)/shard_map/cond/branch_1_fun/ppermute | solution.py:1010
  227.9 17.0 %collective-permute-start.1 = (bf16[1664,128]{1,0:T(8,128)(2,1)S(1)}, bf16[1664,128]{1,0:T(8,128)(2,1)S(1)}, u32[]{:S(2)}, u32[]{:S(2)}) collective-permute-start(bf16[1664,128]{1,0:T(8,128)(2,1)S(1)} %get-tuple-element.20), channel_id=1, source_target_pairs={{0,4},{2,6},{4,0},{6,2},{8,12},{10,14},{12,8},{14,10},{16,20},{18,... | collective-permute-start | bytes 1277960 | tf_op jit(solution)/shard_map/cond/branch_1_fun/ppermute | solution.py:1010
  235.9 11.2 %collective-permute-start.6 = (bf16[2,288,256]{2,1,0:T(8,128)(2,1)S(1)}, bf16[2,288,256]{2,1,0:T(8,128)(2,1)S(1)}, u32[]{:S(2)}, u32[]{:S(2)}) collective-permute-start(bf16[2,288,256]{2,1,0:T(8,128)(2,1)S(1)} %get-tuple-element.30), channel_id=1, source_target_pairs={{0,8},{2,10},{4,12},{6,14},{8,0},{10,2},{12,4},{14,6},{16,24},{18,... | collective-permute-start | bytes 884744 | tf_op jit(solution)/shard_map/cond/branch_1_fun/ppermute | solution.py:1010
  256.4 13.9 %collective-permute-start.10 = (bf16[2,144,256]{2,1,0:T(8,128)(2,1)S(1)}, bf16[2,144,256]{2,1,0:T(8,128)(2,1)S(1)}, u32[]{:S(2)}, u32[]{:S(2)}) collective-permute-start(bf16[2,144,256]{2,1,0:T(8,128)(2,1)S(1)} %branch_1_fun.18.refs_2_.refs_0_), channel_id=1, source_target_pairs={{0,16},{2,18},{4,20},{6,22},{8,24},{10,26},{12,28},{14,30},{16,0},... | collective-permute-start | bytes 442376 | tf_op jit(solution)/shard_map/cond/branch_1_fun/ppermute | solution.py:1010
  280.6 17.7 %collective-permute-start.14 = (bf16[576,256]{1,0:T(8,128)(2,1)S(1)}, bf16[576,256]{1,0:T(8,128)(2,1)S(1)}, u32[]{:S(2)}, u32[]{:S(2)}) collective-permute-start(bf16[576,256]{1,0:T(8,128)(2,1)S(1)} %get-tuple-element.37.refs_2_.refs_0_), channel_id=1, source_target_pairs={{0,4},{2,6},{4,0},{6,2},{8,12},{10,14},{12,8},{14,10},{16,20},{18,... | collective-permute-start | bytes 884744 | tf_op jit(solution)/shard_map/cond/branch_1_fun/ppermute | solution.py:1010
  283.0 15.3 %collective-permute-start.15 = (bf16[576,256]{1,0:T(8,128)(2,1)S(1)}, bf16[576,256]{1,0:T(8,128)(2,1)S(1)}, u32[]{:S(2)}, u32[]{:S(2)}) collective-permute-start(bf16[576,256]{1,0:T(8,128)(2,1)S(1)} %get-tuple-element.38.refs_1_), channel_id=1, source_target_pairs={{0,2},{2,0},{4,6},{6,4},{8,10},{10,8},{12,14},{14,12},{16,18},{18,... | collective-permute-start | bytes 884744 | tf_op jit(solution)/shard_map/cond/branch_1_fun/ppermute | solution.py:1010
  283.6 14.7 %collective-permute-start.11 = (bf16[2,208,128]{2,1,0:T(8,128)(2,1)S(1)}, bf16[2,208,128]{2,1,0:T(8,128)(2,1)S(1)}, u32[]{:S(2)}, u32[]{:S(2)}) collective-permute-start(bf16[2,208,128]{2,1,0:T(8,128)(2,1)S(1)} %branch_1_fun.21.refs_2_.refs_0_), channel_id=1, source_target_pairs={{0,16},{2,18},{4,20},{6,22},{8,24},{10,26},{12,28},{14,30},{16,0},... | collective-permute-start | bytes 319496 | tf_op jit(solution)/shard_map/cond/branch_1_fun/ppermute | solution.py:1010
  298.4 20.2 %collective-permute-start.18 = (bf16[1152,256]{1,0:T(8,128)(2,1)S(1)}, bf16[1152,256]{1,0:T(8,128)(2,1)S(1)}, u32[]{:S(2)}, u32[]{:S(2)}) collective-permute-start(bf16[1152,256]{1,0:T(8,128)(2,1)S(1)} %get-tuple-element.39.refs_2_.refs_0_), channel_id=1, source_target_pairs={{0,2},{2,0},{4,6},{6,4},{8,10},{10,8},{12,14},{14,12},{16,18},{18,... | collective-permute-start | bytes 1769480 | tf_op jit(solution)/shard_map/cond/branch_1_fun/ppermute | solution.py:1010
  299.8 18.9 %collective-permute-start.19 = (bf16[1152,256]{1,0:T(8,128)(2,1)S(1)}, bf16[1152,256]{1,0:T(8,128)(2,1)S(1)}, u32[]{:S(2)}, u32[]{:S(2)}) collective-permute-start(bf16[1152,256]{1,0:T(8,128)(2,1)S(1)} %get-tuple-element.42.refs_1_), channel_id=1, source_target_pairs={{0,4},{2,6},{4,0},{6,2},{8,12},{10,14},{12,8},{14,10},{16,20},{18,... | collective-permute-start | bytes 1769480 | tf_op jit(solution)/shard_map/cond/branch_1_fun/ppermute | solution.py:1010
  299.8 16.1 %collective-permute-start.13 = (bf16[2,416,128]{2,1,0:T(8,128)(2,1)S(1)}, bf16[2,416,128]{2,1,0:T(8,128)(2,1)S(1)}, u32[]{:S(2)}, u32[]{:S(2)}) collective-permute-start(bf16[2,416,128]{2,1,0:T(8,128)(2,1)S(1)} %branch_1_fun.23.refs_4_.refs_0_), channel_id=1, source_target_pairs={{0,8},{2,10},{4,12},{6,14},{8,0},{10,2},{12,4},{14,6},{16,24},{18,... | collective-permute-start | bytes 638984 | tf_op jit(solution)/shard_map/cond/branch_1_fun/ppermute | solution.py:1010
  (67 other events, 537.8 us)
Sparse Core Ops, SparseCore 0:
  150.1 166.1 all-reduce.1

commit v5 on v4

--- a/solution.py
+++ b/solution.py
@@ -801,10 +801,12 @@
     spread_message(message, rows)
 
 
-def images_kernel(gathered, counts, back, unit, mask, stats, params, weight, block_back, affine, grad, out):
+def entry_grad_kernel(gathered, counts, back, unit, mask, stats, params, affine, grad):
     join_sums(gathered, affine)
     grad_pass(back, unit, mask, affine, stats, params, total_count(counts, 4), grad)
-    send(grad, affine)
+
+
+def images_kernel(grad, weight, block_back, mask, out):
     step = 256
     for start in range(0, out.shape[1], step):
         columns = slice(start, start + step)
@@ -1544,9 +1546,9 @@
     second_kept, second_sent = halve(
         order, second_parts[:2], second_got, steps()[1], second_shape[0] // 4, second_shape[1] // 2
     )
-    affine_entry, entry_grad, image_grads = call(
-        images_kernel,
-        [((2, mid), F32), ((pixels, mid), BF16), ((pixels, wide_in), BF16)],
+    affine_entry, entry_grad = call(
+        entry_grad_kernel,
+        [((2, mid), F32), ((pixels, mid), BF16)],
         gathered,
         counts,
         entry_back,
@@ -1554,12 +1556,9 @@
         mask,
         entry_stats,
         entry_affine,
-        entry_weight,
-        block_back_saved,
-        late=(3, 7, 8),
+        late=(3,),
         keep=(),
         after=(order[0],),
-        flops=ops(pixels, mid, wide_in),
     )
 
     order[0] = affine_entry
@@ -1606,7 +1605,18 @@
         late=None,
         after=(third_own[0],),
     )
-    order[0] = shortcut_total
+    (image_grads,) = call(
+        images_kernel,
+        [((pixels, wide_in), BF16)],
+        entry_grad,
+        entry_weight,
+        block_back_saved,
+        mask,
+        late=None,
+        after=(shortcut_total,),
+        flops=ops(pixels, mid, wide_in),
+    )
+    order[0] = image_grads
     widen_total, closing_total, middle_total, entry_total = run_after(
         order,
         functools.partial(out_kernel, third_out, steps()[0]),

time: 346 us -> 345 us (level)
  waiting for transfers between devices: 127 us -> 123 us
    pallas_call x38 -> x39, Pallas kernels: 86.8 us -> 88.8 us  [call(): pl.pallas_call(body, out_shape=[jax.ShapeDtypeStruct(shape, dtype) if fre...]
  transfers between devices with their start and end apart: 55 -> 55, of which waited for: 37 -> 36; matrix products, arithmetic and copies ran while one was open for 0% -> 0% of each run, Pallas kernels for 15% -> 16%
where the time goes in v5:
time: 345 us; the launch traced here: 344 us
  waiting for transfers between devices  123 us (36%)
  Pallas kernels  88.8 us (26%)
  starting transfers between devices  63 us (18%)
  blocking collectives  49.2 us (14%)
  between operations  15.3 us (4%)
  local copies, waits for them, and re-layouts  4.4 us (1%)
    pallas_call x39, Pallas kernels, call(): pl.pallas_call(body, out_shape=[jax.ShapeDtypeStruct(shape, dtype) if fre...  88.8 us
    ppermute x24, waiting for transfers between devices, to_chip(): return lax.ppermute(value, 'img', [(i, i ^ 1 << bit) for i in range(count)])  77.7 us
    all_to_all x8, waiting for transfers between devices, gather_all(): return lax.all_to_all(message, BOTH, 0, 0, tiled=True)  36.2 us
    all_to_all x8, starting transfers between devices, gather_all(): return lax.all_to_all(message, BOTH, 0, 0, tiled=True)  30.5 us
    ppermute x24, starting transfers between devices, to_chip(): return lax.ppermute(value, 'img', [(i, i ^ 1 << bit) for i in range(count)])  27.4 us
    all_to_all x2, blocking collectives, gather_img(): return lax.all_to_all(message, 'img', 0, 0, tiled=True)  26.8 us
    all_to_all x2, blocking collectives, gather_all(): return lax.all_to_all(message, BOTH, 0, 0, tiled=True)  22.4 us
    ppermute x22, waiting for transfers between devices, swap_rows(): lax.ppermute(value, 'row', [(i, (i + 1) % count) for i in range(count)])  8.82 us
  transfers between devices with their start and end apart: 55, of which 36 were waited for; matrix products, arithmetic and copies ran while one was open for 0% of the time, Pallas kernels for 16%

profile of v5, /device:TPU:0, one launch (start us, length us, event | category | flops | bytes accessed | tf_op | source)
XLA Modules:
  0.0 344.2 jit_solution(9077594633778924807)
XLA Ops:
  11.8 7.3 %all-to-all-start = ((f32[32,8,128]{2,1,0:T(8,128)}), f32[32,8,128]{2,1,0:T(8,128)S(1)}, u32[]{:S(2)}, u32[]{:S(2)}) async-start(f32[32,8,128]{2,1,0:T(8,128)} %get-tuple-element.168), calls=%async_computation | async-start | bytes 262144 | tf_op jit(solution)/shard_map/all_to_all | solution.py:25
  20.4 6.9 %all-to-all-done.refs_0_.refs_1_.refs_2_ = f32[32,8,128]{2,1,0:T(8,128)S(1)} async-done(((f32[32,8,128]{2,1,0:T(8,128)}), f32[32,8,128]{2,1,0:T(8,128)S(1)}, u32[]{:S(2)}, u32[]{:S(2)}) %all-to-all-start) | async-done | bytes 131104 | tf_op jit(solution)/shard_map/all_to_all | solution.py:25
  30.5 10.0 %all_to_all.60.refs_0_ = f32[32,8,128]{2,1,0:T(8,128)S(1)} all-to-all(f32[32,8,128]{2,1,0:T(8,128)S(1)} %get-tuple-element.174), channel_id=1, replica_groups=mesh['img'=16,'row'=2] {'img','row'}, dimensions={0} | all-to-all | bytes 262144 | tf_op jit(solution)/shard_map/all_to_all | solution.py:25
  42.4 12.4 %all_to_all.61.refs_0_ = f32[32,16,128]{2,1,0:T(8,128)S(1)} all-to-all(f32[32,16,128]{2,1,0:T(8,128)S(1)} %get-tuple-element.176), channel_id=1, replica_groups=mesh['img'=16,'row'=2] {'img','row'}, dimensions={0} | all-to-all | bytes 524288 | tf_op jit(solution)/shard_map/all_to_all | solution.py:25
  54.8 4.9 %shard_map.291 = (bf16[384,1024]{1,0:T(8,128)(2,1)}, f32[384,1024]{1,0:T(8,128)}, f32[384,1024]{1,0:T(8,128)}, f32[8,1024]{1,0:T(8,128)}, bf16[96,1024]{1,0:T(8,...) custom-call(f32[32,16,128]{2,1,0:T(8,128)S(1)} %all_to_all.61.refs_0, ...), custom_call_target="tpu_custom_call" | custom-call | flops 402653184 | bytes 9674752 | tf_op jit(solution)/shard_map/pallas_call | solution.py:129
  63.6 6.9 %all-to-all-done.3.refs_0_ = f32[32,8,128]{2,1,0:T(8,128)S(1)} async-done(((f32[32,8,128]{2,1,0:T(8,128)}), f32[32,8,128]{2,1,0:T(8,128)S(1)}, u32[]{:S(2)}, u32[]{:S(2)}) %all-to-all-start.3) | async-done | bytes 131104 | tf_op jit(solution)/shard_map/all_to_all | solution.py:25
  89.7 14.6 %all_to_all.62.refs_0_ = f32[16,40,128]{2,1,0:T(8,128)S(1)} all-to-all(f32[16,40,128]{2,1,0:T(8,128)S(1)} %shard_map.295), channel_id=1, replica_groups=mesh['img'=16,'row'=2] {'img'}, dimensions={0} | all-to-all | bytes 655360 | tf_op jit(solution)/shard_map/all_to_all | solution.py:29
  109.9 12.2 %all_to_all.63 = f32[16,24,128]{2,1,0:T(8,128)S(1)} all-to-all(f32[16,24,128]{2,1,0:T(8,128)S(1)} %broadcast_in_dim.2), channel_id=1, replica_groups=mesh['img'=16,'row'=2] {'img'}, dimensions={0} | all-to-all | bytes 393216 | tf_op jit(solution)/shard_map/all_to_all | solution.py:29
  132.4 5.1 %shard_map.299.refs_12_ = bf16[768,2048]{1,0:T(8,128)(2,1)} custom-call(bf16[96,1024]{1,0:T(8,128)(2,1)} %get-tuple-element.185.refs_0_, bf16[96,512]{1,0:T(8,128)(2,1)} %copy-done.26, bf16[96,512]{1,0:T(8,128)(2,1)} %get-tuple-element.209.refs_2_, bf16[96,256]{1,0:T(8,128)(2,1)} %copy-done.27, bf16[96,2048]{1,0:T(8,128)(2,1)} %get-tuple-element.211.refs_4_.refs_0_, ...), custom_call_target="tpu_custom_call" | custom-call | flops 603979776 | bytes 5177344 | tf_op jit(solution)/shard_map/pallas_call | solution.py:129
  138.2 4.9 %shard_map.300 = (f32[2,512]{1,0:T(2,128)}, bf16[96,512]{1,0:T(8,128)(2,1)}, f32[384,512]{1,0:T(8,128)S(1)}, f32[32,8,128]{2,1,0:T(8,128)}) custom-call(f32[32,8,128]{2,1,0:T(8,128)S(1)} %all-to-all-done.7.refs_0_, f32[32,8,128]{2,1,0:T(8,128)S(1)} %all-to-all-done.refs_0_.refs_1_.refs_2_, f32[96,512]{1,0:T(8,128)S(1)} %get-tuple-element.202.refs_2_, ...), custom_call_target="tpu_custom_call" | custom-call | flops 452984832 | bytes 11292672 | tf_op jit(solution)/shard_map/pallas_call | solution.py:129
  143.9 5.1 %all-to-all-start.8 = ((f32[32,8,128]{2,1,0:T(8,128)}), f32[32,8,128]{2,1,0:T(8,128)S(1)}, u32[]{:S(2)}, u32[]{:S(2)}) async-start(f32[32,8,128]{2,1,0:T(8,128)} %get-tuple-element.214), calls=%async_computation.8 | async-start | bytes 262144 | tf_op jit(solution)/shard_map/all_to_all | solution.py:25
  149.0 5.0 %shard_map.301.refs_8_.refs_11_ = f32[8,384,128]{2,1,0:T(8,128)} custom-call(bf16[96,2048]{1,0:T(8,128)(2,1)} %get-tuple-element.211.refs_4_.refs_0_, bf16[1024,2048]{1,0:T(8,128)(2,1)} %refs_1_.2, f32[2,512]{1,0:T(2,128)} %get-tuple-element.165.refs_2_), custom_call_target="tpu_custom_call" | custom-call | flops 402653184 | bytes 6164480 | tf_op jit(solution)/shard_map/pallas_call | solution.py:129
  157.2 5.6 %shard_map.302 = (f32[2,512]{1,0:T(2,128)}, bf16[384,512]{1,0:T(8,128)(2,1)}, f32[384,1024]{1,0:T(8,128)S(1)}, f32[32,16,128]{2,1,0:T(8,128)}, f32[384,1024]{1,0:T(8,128)}) custom-call(f32[32,8,128]{2,1,0:T(8,128)S(1)} %all-to-all-done.8.refs_0_, f32[32,8,128]{2,1,0:T(8,128)S(1)} %all-to-all-done.refs_0_.refs_1_.refs_2_, ...), custom_call_target="tpu_custom_call" | custom-call | flops 402653184 | bytes 13197312 | tf_op jit(solution)/shard_map/pallas_call | solution.py:129
  174.0 9.1 %all-to-all-done.9.refs_0_ = f32[32,16,128]{2,1,0:T(8,128)S(1)} async-done(((f32[32,16,128]{2,1,0:T(8,128)}), f32[32,16,128]{2,1,0:T(8,128)S(1)}, u32[]{:S(2)}, u32[]{:S(2)}) %all-to-all-start.9) | async-done | bytes 262176 | tf_op jit(solution)/shard_map/all_to_all | solution.py:25
  195.2 5.0 %all-to-all-done.10.refs_0_ = f32[32,8,128]{2,1,0:T(8,128)S(1)} async-done(((f32[32,8,128]{2,1,0:T(8,128)}), f32[32,8,128]{2,1,0:T(8,128)S(1)}, u32[]{:S(2)}, u32[]{:S(2)}) %all-to-all-start.10) | async-done | bytes 131104 | tf_op jit(solution)/shard_map/all_to_all | solution.py:25
  207.8 5.4 %shard_map.306.refs_4_.refs_0_ = bf16[2688,256]{1,0:T(8,128)(2,1)} custom-call(bf16[384,1024]{1,0:T(8,128)(2,1)} %get-tuple-element.243.refs_0_, bf16[384,512]{1,0:T(8,128)(2,1)} %collective-permute-done.36.refs_1_, bf16[384,512]{1,0:T(8,128)(2,1)} %get-tuple-element.245.refs_2_, bf16[384,512]{1,0:T(8,128)(2,1)} %collective-permute-done.37.refs_3_, ...), custom_call_target="tpu_custom_call" | custom-call | flops 1308622848 | bytes 6711296 | tf_op jit(solution)/shard_map/pallas_call | solution.py:129
  223.2 101.9 %conditional.1 = (bf16[1664,128]{1,0:T(8,128)(2,1)S(1)}, bf16[1664,128]{1,0:T(8,128)(2,1)S(1)}, f32[3,3,256,512]{3,2,1,0:T(8,128)}) conditional(s32[]{:T(128)} %bitcast.7, () %tuple.18, (bf16[1664,128]{1,0:T(8,128)(2,1)S(1)}, bf16[1664,128]{1,0:T(8,128)(2,1)S(1)}, bf16[576,256]{1,0:T(8,128)(2,1)S(1)}, bf16[576,256]{1,0:T(8,128)(2,1)S(1)}, ...), branch_computations={%region_2.0_spmd, %region_3.0_spmd} | conditional | bytes 52405048 | solution.py:1599
  227.4 5.8 %collective-permute-done.2.refs_2_ = bf16[576,256]{1,0:T(8,128)(2,1)S(1)} collective-permute-done((bf16[576,256]{1,0:T(8,128)(2,1)S(1)}, bf16[576,256]{1,0:T(8,128)(2,1)S(1)}, u32[]{:S(2)}, u32[]{:S(2)}) %collective-permute-start.2) | collective-permute-done | bytes 294944 | tf_op jit(solution)/shard_map/cond/branch_1_fun/ppermute | solution.py:1012
  236.0 7.3 %collective-permute-done.refs_2_ = bf16[1664,128]{1,0:T(8,128)(2,1)S(1)} collective-permute-done((bf16[1664,128]{1,0:T(8,128)(2,1)S(1)}, bf16[1664,128]{1,0:T(8,128)(2,1)S(1)}, u32[]{:S(2)}, u32[]{:S(2)}) %collective-permute-start) | collective-permute-done | bytes 426016 | tf_op jit(solution)/shard_map/cond/branch_1_fun/ppermute | solution.py:1012
  258.2 8.4 %collective-permute-done.10.refs_1_ = bf16[2,144,256]{2,1,0:T(8,128)(2,1)S(1)} collective-permute-done((bf16[2,144,256]{2,1,0:T(8,128)(2,1)S(1)}, bf16[2,144,256]{2,1,0:T(8,128)(2,1)S(1)}, u32[]{:S(2)}, u32[]{:S(2)}) %collective-permute-start.10) | collective-permute-done | bytes 147488 | tf_op jit(solution)/shard_map/cond/branch_1_fun/ppermute | solution.py:1012
  268.7 9.4 %collective-permute-done.9.refs_1_ = bf16[2,208,128]{2,1,0:T(8,128)(2,1)S(1)} collective-permute-done((bf16[2,208,128]{2,1,0:T(8,128)(2,1)S(1)}, bf16[2,208,128]{2,1,0:T(8,128)(2,1)S(1)}, u32[]{:S(2)}, u32[]{:S(2)}) %collective-permute-start.9) | collective-permute-done | bytes 106528 | tf_op jit(solution)/shard_map/cond/branch_1_fun/ppermute | solution.py:1012
  284.6 12.1 %collective-permute-done.11.refs_1_ = bf16[2,208,128]{2,1,0:T(8,128)(2,1)S(1)} collective-permute-done((bf16[2,208,128]{2,1,0:T(8,128)(2,1)S(1)}, bf16[2,208,128]{2,1,0:T(8,128)(2,1)S(1)}, u32[]{:S(2)}, u32[]{:S(2)}) %collective-permute-start.11) | collective-permute-done | bytes 106528 | tf_op jit(solution)/shard_map/cond/branch_1_fun/ppermute | solution.py:1012
  300.6 17.1 %collective-permute-done.13.refs_1_ = bf16[2,416,128]{2,1,0:T(8,128)(2,1)S(1)} collective-permute-done((bf16[2,416,128]{2,1,0:T(8,128)(2,1)S(1)}, bf16[2,416,128]{2,1,0:T(8,128)(2,1)S(1)}, u32[]{:S(2)}, u32[]{:S(2)}) %collective-permute-start.13) | collective-permute-done | bytes 213024 | tf_op jit(solution)/shard_map/cond/branch_1_fun/ppermute | solution.py:1012
  326.8 4.9 %shard_map.310 = (f32[512,2048]{1,0:T(8,128)}, f32[256,2048]{1,0:T(8,128)}) custom-call(bf16[768,2048]{1,0:T(8,128)(2,1)} %all-reduce.2.cloned.1.call-done.refs_0_, bf16[1664,128]{1,0:T(8,128)(2,1)S(1)} %get-tuple-element.265.refs_1_.refs_0_), custom_call_target="tpu_custom_call" | custom-call | bytes 9863168 | tf_op jit(solution)/shard_map/pallas_call | solution.py:129
  (210 shorter events, 143.5 us)
Async XLA Ops:
  11.8 15.5 %all-to-all-start = ((f32[32,8,128]{2,1,0:T(8,128)}), f32[32,8,128]{2,1,0:T(8,128)S(1)}, u32[]{:S(2)}, u32[]{:S(2)}) async-start(f32[32,8,128]{2,1,0:T(8,128)} %get-tuple-element.168), calls=%async_computation | async-start | bytes 262144 | tf_op jit(solution)/shard_map/all_to_all | solution.py:25
  143.1 183.7 %all-reduce.2.cloned.1.call-start = ((), (), s32[]{:S(2)}) async-start(), calls=%async_computation.12 | async-start | bytes 6291456 | tf_op jit(solution)/shard_map/psum | solution.py:1385
  143.9 13.4 %all-to-all-start.8 = ((f32[32,8,128]{2,1,0:T(8,128)}), f32[32,8,128]{2,1,0:T(8,128)S(1)}, u32[]{:S(2)}, u32[]{:S(2)}) async-start(f32[32,8,128]{2,1,0:T(8,128)} %get-tuple-element.214), calls=%async_computation.8 | async-start | bytes 262144 | tf_op jit(solution)/shard_map/all_to_all | solution.py:25
  162.9 20.2 %all-to-all-start.9 = ((f32[32,16,128]{2,1,0:T(8,128)}), f32[32,16,128]{2,1,0:T(8,128)S(1)}, u32[]{:S(2)}, u32[]{:S(2)}) async-start(f32[32,16,128]{2,1,0:T(8,128)} %get-tuple-element.220), calls=%async_computation.9 | async-start | bytes 524288 | tf_op jit(solution)/shard_map/all_to_all | solution.py:25
  166.8 26.9 %collective-permute-start.40 = (bf16[3,160,384]{2,1,0:T(8,128)(2,1)}, bf16[3,160,384]{2,1,0:T(8,128)(2,1)}, u32[]{:S(2)}, u32[]{:S(2)}) collective-permute-start(bf16[3,160,384]{2,1,0:T(8,128)(2,1)} %get-tuple-element.250), channel_id=1, source_target_pairs={{0,1},{1,0},{2,3},{3,2},{4,5},{5,4},{6,7},{7,6},{8,9},{9,8},{10,11... | collective-permute-start | bytes 1105928 | tf_op jit(solution)/shard_map/ppermute | solution.py:21
  186.5 20.6 %collective-permute-start.39 = (bf16[384,1024]{1,0:T(8,128)(2,1)}, bf16[384,1024]{1,0:T(8,128)(2,1)}, u32[]{:S(2)}, u32[]{:S(2)}) collective-permute-start(bf16[384,1024]{1,0:T(8,128)(2,1)} %get-tuple-element.248.refs_6_), channel_id=1, source_target_pairs={{0,1},{1,0},{2,3},{3,2},{4,5},{5,4},{6,7},{7,6},{8,9},{9,8},{10,11... | collective-permute-start | bytes 2359304 | tf_op jit(solution)/shard_map/ppermute | solution.py:21
  186.6 17.3 %collective-permute-start.36 = (bf16[384,512]{1,0:T(8,128)(2,1)}, bf16[384,512]{1,0:T(8,128)(2,1)}, u32[]{:S(2)}, u32[]{:S(2)}) collective-permute-start(bf16[384,512]{1,0:T(8,128)(2,1)} %get-tuple-element.244), channel_id=1, source_target_pairs={{0,1},{1,0},{2,3},{3,2},{4,5},{5,4},{6,7},{7,6},{8,9},{9,8},{10,11... | collective-permute-start | bytes 1179656 | tf_op jit(solution)/shard_map/ppermute | solution.py:21
  187.6 12.6 %all-to-all-start.10 = ((f32[32,8,128]{2,1,0:T(8,128)}), f32[32,8,128]{2,1,0:T(8,128)S(1)}, u32[]{:S(2)}, u32[]{:S(2)}) async-start(f32[32,8,128]{2,1,0:T(8,128)} %get-tuple-element.230), calls=%async_computation.10 | async-start | bytes 262144 | tf_op jit(solution)/shard_map/all_to_all | solution.py:25
  191.9 22.1 %collective-permute-start.34 = (bf16[1152,256]{1,0:T(8,128)(2,1)}, bf16[1152,256]{1,0:T(8,128)(2,1)S(1)}, u32[]{:S(2)}, u32[]{:S(2)}) collective-permute-start(bf16[1152,256]{1,0:T(8,128)(2,1)} %get-tuple-element.241), channel_id=1, source_target_pairs={{0,2},{2,0},{4,6},{6,4},{8,10},{10,8},{12,14},{14,12},{16,18},{18,... | collective-permute-start | bytes 1769480 | tf_op jit(solution)/shard_map/ppermute | solution.py:1012
  193.7 21.4 %collective-permute-start.35 = (bf16[1152,256]{1,0:T(8,128)(2,1)}, bf16[1152,256]{1,0:T(8,128)(2,1)S(1)}, u32[]{:S(2)}, u32[]{:S(2)}) collective-permute-start(bf16[1152,256]{1,0:T(8,128)(2,1)} %get-tuple-element.242), channel_id=1, source_target_pairs={{0,4},{2,6},{4,0},{6,2},{8,12},{10,14},{12,8},{14,10},{16,20},{18,... | collective-permute-start | bytes 1769480 | tf_op jit(solution)/shard_map/ppermute | solution.py:1012
  195.2 11.7 %collective-permute-start.37 = (bf16[384,512]{1,0:T(8,128)(2,1)S(1)}, bf16[384,512]{1,0:T(8,128)(2,1)}, u32[]{:S(2)}, u32[]{:S(2)}) collective-permute-start(bf16[384,512]{1,0:T(8,128)(2,1)S(1)} %copy-done.19), channel_id=1, source_target_pairs={{0,1},{1,0},{2,3},{3,2},{4,5},{5,4},{6,7},{7,6},{8,9},{9,8},{10,11... | collective-permute-start | bytes 1179656 | tf_op jit(solution)/shard_map/ppermute | solution.py:21
  204.1 12.2 %all-to-all-start.11 = ((f32[32,8,128]{2,1,0:T(8,128)}), f32[32,8,128]{2,1,0:T(8,128)S(1)}, u32[]{:S(2)}, u32[]{:S(2)}) async-start(f32[32,8,128]{2,1,0:T(8,128)} %get-tuple-element.237), calls=%async_computation.11 | async-start | bytes 262144 | tf_op jit(solution)/shard_map/all_to_all | solution.py:25
  206.9 12.8 %collective-permute-start.42 = (bf16[384,512]{1,0:T(8,128)(2,1)}, bf16[384,512]{1,0:T(8,128)(2,1)S(1)}, u32[]{:S(2)}, u32[]{:S(2)}) collective-permute-start(bf16[384,512]{1,0:T(8,128)(2,1)} %get-tuple-element.256), channel_id=1, source_target_pairs={{0,1},{1,0},{2,3},{3,2},{4,5},{5,4},{6,7},{7,6},{8,9},{9,8},{10,11... | collective-permute-start | bytes 1179656 | tf_op jit(solution)/shard_map/ppermute | solution.py:21
  225.4 17.9 %collective-permute-start = (bf16[1664,128]{1,0:T(8,128)(2,1)S(1)}, bf16[1664,128]{1,0:T(8,128)(2,1)S(1)}, u32[]{:S(2)}, u32[]{:S(2)}) collective-permute-start(bf16[1664,128]{1,0:T(8,128)(2,1)S(1)} %get-tuple-element.19), channel_id=1, source_target_pairs={{0,2},{2,0},{4,6},{6,4},{8,10},{10,8},{12,14},{14,12},{16,18},{18,... | collective-permute-start | bytes 1277960 | tf_op jit(solution)/shard_map/cond/branch_1_fun/ppermute | solution.py:1012
  226.7 16.7 %collective-permute-start.1 = (bf16[1664,128]{1,0:T(8,128)(2,1)S(1)}, bf16[1664,128]{1,0:T(8,128)(2,1)S(1)}, u32[]{:S(2)}, u32[]{:S(2)}) collective-permute-start(bf16[1664,128]{1,0:T(8,128)(2,1)S(1)} %get-tuple-element.20), channel_id=1, source_target_pairs={{0,4},{2,6},{4,0},{6,2},{8,12},{10,14},{12,8},{14,10},{16,20},{18,... | collective-permute-start | bytes 1277960 | tf_op jit(solution)/shard_map/cond/branch_1_fun/ppermute | solution.py:1012
  254.8 11.8 %collective-permute-start.10 = (bf16[2,144,256]{2,1,0:T(8,128)(2,1)S(1)}, bf16[2,144,256]{2,1,0:T(8,128)(2,1)S(1)}, u32[]{:S(2)}, u32[]{:S(2)}) collective-permute-start(bf16[2,144,256]{2,1,0:T(8,128)(2,1)S(1)} %branch_1_fun.18.refs_2_.refs_0_), channel_id=1, source_target_pairs={{0,16},{2,18},{4,20},{6,22},{8,24},{10,26},{12,28},{14,30},{16,0},... | collective-permute-start | bytes 442376 | tf_op jit(solution)/shard_map/cond/branch_1_fun/ppermute | solution.py:1012
  266.7 13.3 %collective-permute-start.12 = (bf16[2,288,256]{2,1,0:T(8,128)(2,1)S(1)}, bf16[2,288,256]{2,1,0:T(8,128)(2,1)S(1)}, u32[]{:S(2)}, u32[]{:S(2)}) collective-permute-start(bf16[2,288,256]{2,1,0:T(8,128)(2,1)S(1)} %branch_1_fun.20.refs_2_.refs_0_), channel_id=1, source_target_pairs={{0,8},{2,10},{4,12},{6,14},{8,0},{10,2},{12,4},{14,6},{16,24},{18,... | collective-permute-start | bytes 884744 | tf_op jit(solution)/shard_map/cond/branch_1_fun/ppermute | solution.py:1012
  266.7 11.4 %collective-permute-start.9 = (bf16[2,208,128]{2,1,0:T(8,128)(2,1)S(1)}, bf16[2,208,128]{2,1,0:T(8,128)(2,1)S(1)}, u32[]{:S(2)}, u32[]{:S(2)}) collective-permute-start(bf16[2,208,128]{2,1,0:T(8,128)(2,1)S(1)} %get-tuple-element.36), channel_id=1, source_target_pairs={{0,16},{2,18},{4,20},{6,22},{8,24},{10,26},{12,28},{14,30},{16,0},... | collective-permute-start | bytes 319496 | tf_op jit(solution)/shard_map/cond/branch_1_fun/ppermute | solution.py:1012
  280.0 16.8 %collective-permute-start.14 = (bf16[576,256]{1,0:T(8,128)(2,1)S(1)}, bf16[576,256]{1,0:T(8,128)(2,1)S(1)}, u32[]{:S(2)}, u32[]{:S(2)}) collective-permute-start(bf16[576,256]{1,0:T(8,128)(2,1)S(1)} %get-tuple-element.37.refs_2_.refs_0_), channel_id=1, source_target_pairs={{0,4},{2,6},{4,0},{6,2},{8,12},{10,14},{12,8},{14,10},{16,20},{18,... | collective-permute-start | bytes 884744 | tf_op jit(solution)/shard_map/cond/branch_1_fun/ppermute | solution.py:1012
  281.3 15.5 %collective-permute-start.15 = (bf16[576,256]{1,0:T(8,128)(2,1)S(1)}, bf16[576,256]{1,0:T(8,128)(2,1)S(1)}, u32[]{:S(2)}, u32[]{:S(2)}) collective-permute-start(bf16[576,256]{1,0:T(8,128)(2,1)S(1)} %get-tuple-element.38.refs_1_), channel_id=1, source_target_pairs={{0,2},{2,0},{4,6},{6,4},{8,10},{10,8},{12,14},{14,12},{16,18},{18,... | collective-permute-start | bytes 884744 | tf_op jit(solution)/shard_map/cond/branch_1_fun/ppermute | solution.py:1012
  282.5 14.2 %collective-permute-start.11 = (bf16[2,208,128]{2,1,0:T(8,128)(2,1)S(1)}, bf16[2,208,128]{2,1,0:T(8,128)(2,1)S(1)}, u32[]{:S(2)}, u32[]{:S(2)}) collective-permute-start(bf16[2,208,128]{2,1,0:T(8,128)(2,1)S(1)} %branch_1_fun.21.refs_2_.refs_0_), channel_id=1, source_target_pairs={{0,16},{2,18},{4,20},{6,22},{8,24},{10,26},{12,28},{14,30},{16,0},... | collective-permute-start | bytes 319496 | tf_op jit(solution)/shard_map/cond/branch_1_fun/ppermute | solution.py:1012
  296.9 22.9 %collective-permute-start.18 = (bf16[1152,256]{1,0:T(8,128)(2,1)S(1)}, bf16[1152,256]{1,0:T(8,128)(2,1)S(1)}, u32[]{:S(2)}, u32[]{:S(2)}) collective-permute-start(bf16[1152,256]{1,0:T(8,128)(2,1)S(1)} %get-tuple-element.39.refs_2_.refs_0_), channel_id=1, source_target_pairs={{0,2},{2,0},{4,6},{6,4},{8,10},{10,8},{12,14},{14,12},{16,18},{18,... | collective-permute-start | bytes 1769480 | tf_op jit(solution)/shard_map/cond/branch_1_fun/ppermute | solution.py:1012
  298.2 21.6 %collective-permute-start.19 = (bf16[1152,256]{1,0:T(8,128)(2,1)S(1)}, bf16[1152,256]{1,0:T(8,128)(2,1)S(1)}, u32[]{:S(2)}, u32[]{:S(2)}) collective-permute-start(bf16[1152,256]{1,0:T(8,128)(2,1)S(1)} %get-tuple-element.42.refs_1_), channel_id=1, source_target_pairs={{0,4},{2,6},{4,0},{6,2},{8,12},{10,14},{12,8},{14,10},{16,20},{18,... | collective-permute-start | bytes 1769480 | tf_op jit(solution)/shard_map/cond/branch_1_fun/ppermute | solution.py:1012
  298.6 19.1 %collective-permute-start.13 = (bf16[2,416,128]{2,1,0:T(8,128)(2,1)S(1)}, bf16[2,416,128]{2,1,0:T(8,128)(2,1)S(1)}, u32[]{:S(2)}, u32[]{:S(2)}) collective-permute-start(bf16[2,416,128]{2,1,0:T(8,128)(2,1)S(1)} %branch_1_fun.23.refs_4_.refs_0_), channel_id=1, source_target_pairs={{0,8},{2,10},{4,12},{6,14},{8,0},{10,2},{12,4},{14,6},{16,24},{18,... | collective-permute-start | bytes 638984 | tf_op jit(solution)/shard_map/cond/branch_1_fun/ppermute | solution.py:1012
  (67 other events, 541.3 us)
Sparse Core Ops, SparseCore 0:
  150.1 168.7 all-reduce.1
